TPU v7x, 128 devices: a whole 4x4x4 slice. The times are simulated.
128 devices in a mesh: seq: 16 (over y, x), tp: 8 (over z, core).
Axes of the slice: x: 4, y: 4, z: 4, core: 2. Of those that a mesh axis runs over, the one named last changes fastest.
Arguments:
- context: bfloat16 [128, 192, 1280], P('seq', 'tp'), may hold values from -6 to 6
- residual_in: bfloat16 [128, 192, 1280], P('seq', 'tp'), may hold values from -6 to 6
- out_weight: bfloat16 [1280, 1280], replicated, may hold values from -0.15625 to 0.15625
- final_norm_weight: float32 [1280], replicated, may hold values from 0.1 to 1.9
- final_norm_bias: float32 [1280], replicated, may hold values from -3 to 3
- adapter_in: bfloat16 [5120, 3584], P(None, 'tp'), may hold values from -0.078125 to 0.078125
- adapter_out: bfloat16 [3584, 3584], P('tp'), may hold values from -0.09375 to 0.09375
- emb_grad: bfloat16 [6144, 3584], P('seq', 'tp'), may hold values from -6 to 6
- group_offsets: int32 [128], replicated, may hold values from 0 to 6143, as said below
- group_frames: int32 [128], replicated, may hold values from 4 to 192, as said below
- group_owner: int32 [128], replicated, may hold values from 0 to 127, as said below
Outputs:
- d_context: bfloat16 [128, 192, 1280], P('seq', 'tp')
- d_residual: bfloat16 [128, 192, 1280], P('seq', 'tp')
- d_out_weight: float32 [1280, 1280], P(('seq', 'tp'))
- d_adapter_in: bfloat16 [5120, 3584], P('seq', 'tp')
- d_adapter_out: bfloat16 [3584, 3584], P('tp', 'seq')
Inputs may be any that keep to these rules, and one draw needn't show every extreme that they name: `group_frames`: a multiple of 4; among groups 8 * q to 8 * q + 7 one has all 192 frames. `group_offsets`: the tokens of group k (group_frames[k] / 4 of them) lie within positions (k // 8) * 384 to (k // 8 + 1) * 384 - 1, in increasing order of k and without intersection. `group_owner`: each slot holds exactly one group; the 8 groups k // 8 = q lie in slots whose index // 8 are all different.
All inputs are finite; a program needn't handle non-finite values.
Results may differ from a plain program's by a relative error of at most 0.02.
Values may be sent and summed in bfloat16 or wider, within the bound.
No kernel may reach another device: no remote copies, remote signals or barrier semaphores. Data moves between devices by JAX's collectives and lax.ppermute only.
A program may use at most 128 MiB of HBM per device.

v0:
```python
import jax
import jax.numpy as jnp
from jax import lax
from jax.sharding import PartitionSpec as P


def gelu_exact(values):
    return 0.5 * values * (1.0 + jax.scipy.special.erf(values * 0.7071067811865476))


def gelu_slope(values):
    cumulative = 0.5 * (1.0 + jax.scipy.special.erf(values * 0.7071067811865476))
    density = jnp.exp(-0.5 * values * values) * 0.3989422804014327
    return cumulative + values * density


def per_device(
    context,
    residual_in,
    out_weight,
    final_norm_weight,
    final_norm_bias,
    adapter_in,
    adapter_out,
    emb_grad,
    group_offsets,
    group_frames,
    group_owner,
):
    seq_count = lax.axis_size("seq")
    tp_count = lax.axis_size("tp")
    row_index = lax.axis_index("seq")
    column_index = lax.axis_index("tp")
    slots_here, frames_here, enc_width = context.shape
    tokens_here = frames_here // 4
    stack_width = 4 * enc_width
    group_tokens = tokens_here * tp_count
    total_groups = group_owner.shape[0]
    shard_tokens = emb_grad.shape[0]
    stream = residual_in.astype(jnp.float32) + jnp.einsum(
        "cfe,eo->cfo", context, out_weight, preferred_element_type=jnp.float32
    )
    centered_input = stream - jnp.mean(stream, axis=-1, keepdims=True)
    inverse_deviation = lax.rsqrt(
        jnp.mean(centered_input * centered_input, axis=-1, keepdims=True) + 1e-05
    )
    normalized_input = centered_input * inverse_deviation
    encoder_output = (
        (normalized_input * final_norm_weight + final_norm_bias)
        .astype(jnp.bfloat16)
        .reshape(slots_here, tokens_here, stack_width)
    )
    slot_ids = row_index * slots_here + jnp.arange(slots_here, dtype=jnp.int32)
    group_ids = jnp.arange(total_groups, dtype=jnp.int32)
    holder = group_owner[None, :] == slot_ids[:, None]
    held_group = jnp.sum(jnp.where(holder, group_ids[None, :], 0), axis=1)
    target_row = held_group // slots_here
    rows_range = jnp.arange(seq_count, dtype=jnp.int32)
    outgoing = (target_row[None, :] == rows_range[:, None]).astype(jnp.bfloat16)
    parcels = jnp.einsum(
        "dc,ctf->dtf", outgoing, encoder_output, preferred_element_type=jnp.float32
    ).astype(jnp.bfloat16)
    arrived = lax.all_to_all(parcels, "seq", split_axis=0, concat_axis=0, tiled=True)
    my_groups = row_index * slots_here + jnp.arange(slots_here, dtype=jnp.int32)
    source_row = jnp.take(group_owner, my_groups) // slots_here
    incoming = (source_row[:, None] == rows_range[None, :]).astype(jnp.bfloat16)
    sorted_rows = jnp.einsum(
        "cs,stf->ctf", incoming, arrived, preferred_element_type=jnp.float32
    ).astype(jnp.bfloat16)
    full_rows, full_grad = (
        lax.all_gather(sorted_rows, "tp", axis=1, tiled=True),
        lax.all_gather(emb_grad, "tp", axis=1, tiled=True),
    )
    token_steps = jnp.arange(group_tokens, dtype=jnp.int32)
    starts = jnp.take(group_offsets, my_groups) - row_index * shard_tokens
    counts = jnp.take(group_frames, my_groups) // 4
    places = jnp.clip(starts[:, None] + token_steps[None, :], 0, shard_tokens - 1).reshape(-1)
    live = (token_steps[None, :] < counts[:, None]).reshape(-1)
    picked = jnp.take(full_grad, places, axis=0)
    out_grad = jnp.where(live[:, None], picked, jnp.zeros_like(picked))
    stacked = full_rows.reshape(slots_here * group_tokens, stack_width)
    preact = jnp.dot(stacked, adapter_in, preferred_element_type=jnp.float32)
    hidden = gelu_exact(preact).astype(jnp.bfloat16)
    hid_grad = lax.dot_general(
        out_grad, adapter_out, (((1,), (1,)), ((), ())), preferred_element_type=jnp.float32
    )
    pre_grad = (hid_grad * gelu_slope(preact)).astype(jnp.bfloat16)
    grad_in_part = lax.dot_general(
        stacked, pre_grad, (((0,), (0,)), ((), ())), preferred_element_type=jnp.float32
    )
    grad_out_part = lax.dot_general(
        hidden, out_grad, (((0,), (0,)), ((), ())), preferred_element_type=jnp.float32
    )
    grad_in, grad_out = (
        lax.psum_scatter(
            grad_in_part.astype(jnp.bfloat16), "seq", scatter_dimension=0, tiled=True
        ).astype(jnp.float32),
        lax.psum_scatter(
            grad_out_part.astype(jnp.bfloat16), "seq", scatter_dimension=1, tiled=True
        ).astype(jnp.float32),
    )
    row_part = lax.dot_general(
        pre_grad, adapter_in, (((1,), (1,)), ((), ())), preferred_element_type=jnp.float32
    )
    row_part = row_part.reshape(slots_here, group_tokens, stack_width)
    summed = lax.psum(row_part.astype(jnp.bfloat16), "tp").astype(jnp.float32)
    own_rows = lax.dynamic_slice_in_dim(summed, column_index * tokens_here, tokens_here, 1)
    returning = jnp.einsum(
        "cs,ctf->stf", incoming, own_rows.astype(jnp.bfloat16), preferred_element_type=jnp.float32
    ).astype(jnp.bfloat16)
    came_back = lax.all_to_all(returning, "seq", split_axis=0, concat_axis=0, tiled=True)
    slot_grad = jnp.einsum("dc,dtf->ctf", outgoing, came_back, preferred_element_type=jnp.float32)
    enc_grad = slot_grad.reshape(slots_here, frames_here, enc_width)
    scaled_normed = enc_grad * final_norm_weight
    residual_gradient = inverse_deviation * (
        scaled_normed
        - jnp.mean(scaled_normed, axis=-1, keepdims=True)
        - normalized_input * jnp.mean(scaled_normed * normalized_input, axis=-1, keepdims=True)
    )
    d_residual = residual_gradient.astype(jnp.bfloat16)
    d_context = jnp.einsum(
        "cfo,eo->cfe", d_residual, out_weight, preferred_element_type=jnp.float32
    ).astype(jnp.bfloat16)
    weight_part = jnp.einsum("cfe,cfo->eo", context, d_residual, preferred_element_type=jnp.float32)
    d_out_weight = lax.psum_scatter(weight_part, ("seq", "tp"), scatter_dimension=0, tiled=True)
    return (
        d_context,
        d_residual,
        d_out_weight,
        grad_in.astype(jnp.bfloat16),
        grad_out.astype(jnp.bfloat16),
    )


def solution(mesh):
    placed = (
        P("seq", "tp", None),
        P("seq", "tp", None),
        P(),
        P(),
        P(),
        P(None, "tp"),
        P("tp", None),
        P("seq", "tp"),
        P(),
        P(),
        P(),
    )
    return jax.shard_map(
        per_device,
        mesh=mesh,
        in_specs=placed,
        out_specs=(
            P("seq", "tp", None),
            P("seq", "tp", None),
            P(("seq", "tp"), None),
            P("seq", "tp"),
            P("tp", "seq"),
        ),
        check_vma=False,
    )
```

profile of v0, /device:TPU:0, one launch (start us, length us, event | category | flops | bytes accessed | tf_op | source)
XLA Modules:
  0.0 535.4 jit_solution(11219549329964483907)
XLA Ops:
  7.2 0.7 all-gather.3.cloned.1.call-update
  7.9 1.2 copy-done
  9.1 2.1 fusion.34
  11.3 0.2 multiply_reduce_fusion.1
  11.5 0.7 copy-done.4
  12.2 1.0 add_convert_fusion
  13.2 2.2 reshape.135
  15.4 0.2 select_reduce_fusion
  15.6 1.8 convolution_convert_fusion.3
  17.4 1.6 copy.35
  19.0 7.3 %all-to-all-start = ((bf16[16,6,5120]{2,1,0:T(8,128)(2,1)}), bf16[16,6,5120]{2,1,0:T(8,128)(2,1)}, u32[]{:S(2)}, u32[]{:S(2)}) async-start(bf16[16,6,5120]{2,1,0:T(8,128)(2,1)} %copy.35), calls=%async_computation | async-start | bytes 2621440 | tf_op jit(solution)/shard_map/all_to_all | solution.py:63
  26.4 0.6 gather_fusion.1
  27.1 20.2 %all-to-all-done = bf16[16,6,5120]{2,1,0:T(8,128)(2,1)} async-done(((bf16[16,6,5120]{2,1,0:T(8,128)(2,1)}), bf16[16,6,5120]{2,1,0:T(8,128)(2,1)}, u32[]{:S(2)}, u32[]{:S(2)}) %all-to-all-start) | async-done | bytes 983072 | tf_op jit(solution)/shard_map/all_to_all | solution.py:63
  47.2 3.2 convolution_convert_fusion.5
  50.6 0.6 gather_fusion.3
  51.3 0.1 min.18
  51.4 0.1 min.16
  51.5 0.6 gather_fusion.2
  52.2 0.1 lt.48
  52.4 4.7 copy.33
  57.0 9.9 %gather_fusion = bf16[384,3584]{1,0:T(8,128)(2,1)} fusion(bf16[384,3584]{1,0:T(8,128)(2,1)} %copy.33, s32[1024]{0:T(1024)S(1)} %pad_clamp_fusion), kind=kCustom, calls=%fused_computation.3 | custom fusion | bytes 5506560 | tf_op jit(solution)/shard_map/jit(_take)/gather | solution.py:79
  67.0 13.5 %all-gather.5.cloned.1.call-done = bf16[8,48,5120]{2,0,1:T(8,128)(2,1)} async-done(((bf16[8,6,5120]{2,0,1:T(8,128)(2,1)}), bf16[8,48,5120]{2,0,1:T(8,128)(2,1)}) %all-gather.5.cloned.1.call-update) | async-done | bytes 3932176 | tf_op jit(solution)/shard_map/all_gather | solution.py:71
  80.5 4.4 copy.37
  85.0 6.3 %fusion.35 = f32[384,448]{0,1:T(8,128)S(1)} fusion(bf16[384,5120]{1,0:T(8,128)(2,1)S(1)} %bitcast.44, bf16[5120,448]{0,1:T(8,128)(2,1)} %param.18), kind=kOutput, calls=%fused_computation.81 | convolution fusion | flops 1761607680 | bytes 9207808 | tf_op jit(solution)/shard_map/dot_general | solution.py:82
  91.3 2.1 fusion.10
  93.4 2.3 convolution_convert_fusion.1
  95.8 4.0 copy.38
  99.9 71.8 %all-reduce.4.cloned.1.call-done = bf16[8,48,5120]{2,0,1:T(8,128)(2,1)} async-done(((bf16[8,48,5120]{2,0,1:T(8,128)(2,1)}), bf16[8,48,5120]{2,0,1:T(8,128)(2,1)}) %all-reduce.4.cloned.1.call-update) | async-done | bytes 3932176 | tf_op jit(solution)/shard_map/psum | solution.py:106
  171.7 1.6 convolution_convert_fusion.2
  173.3 0.6 copy.39
  173.8 24.9 %all_to_all.10 = bf16[16,6,5120]{2,1,0:T(8,128)(2,1)S(1)} all-to-all(bf16[16,6,5120]{2,1,0:T(8,128)(2,1)S(1)} %copy.39), channel_id=1, replica_groups=mesh['seq'=16,'tp'=8] {'seq'}, dimensions={0} | all-to-all | bytes 1966080 | tf_op jit(solution)/shard_map/all_to_all | solution.py:111
  198.7 1.1 fusion.11
  199.9 1.7 copy.41
  201.6 2.6 reshape.137
  204.2 1.8 multiply_reduce_fusion.2
  206.0 1.8 multiply_convert_fusion
  207.9 0.8 copy-done.7
  208.6 3.8 convolution_bitcast_fusion
  212.5 5.6 %convolution_convert_fusion.4 = bf16[448,3584]{1,0:T(8,128)(2,1)} fusion(f32[384,448]{0,1:T(8,128)} %copy-done.13, bf16[384,3584]{1,0:T(8,128)(2,1)} %gather_fusion, pred[384]{0:T(512)(128)(4,1)S(1)} %compare_and_fusion.1, pred[384]{0:T(512)(128)(4,1)S(1)} %lt.48), kind=kOutput, calls=%fused_computation.9 | convolution fusion | flops 1238343680 | bytes 6652672 | tf_op jit(solution)/shard_map/dot_general | solution.py:91
  218.1 5.8 %copy.45 = bf16[448,3584]{0,1:T(8,128)(2,1)} copy(bf16[448,3584]{1,0:T(8,128)(2,1)} %convolution_convert_fusion.4) | data formatting | bytes 6422528
  224.0 7.4 %convolution_convert_fusion = bf16[5120,448]{1,0:T(8,128)(2,1)} fusion(bf16[384,5120]{1,0:T(8,128)(2,1)} %bitcast.45, bf16[384,448]{0,1:T(8,128)(2,1)} %copy-done.9), kind=kOutput, calls=%fused_computation.5 | convolution fusion | flops 1763901440 | bytes 8863744 | tf_op jit(solution)/shard_map/dot_general | solution.py:88
  231.5 3.1 fusion.7
  234.6 133.8 %all-reduce.6.cloned.1.call-done = f32[1280,1280]{0,1:T(8,128)} async-done(((f32[1280,1280]{0,1:T(8,128)}), f32[1280,1280]{0,1:T(8,128)}) %all-reduce.6.cloned.1.call-update) | async-done | bytes 6553616
  368.4 2.4 constant_dynamic-slice_fusion
  370.8 1.9 copy.42
  372.7 73.6 %reduce-scatter.8.cloned.1.call-done = bf16[224,448]{1,0:T(8,128)(2,1)} async-done(((bf16[3584,448]{1,0:T(8,128)(2,1)}), bf16[224,448]{1,0:T(8,128)(2,1)}) %reduce-scatter.8.cloned.1.call-update) | async-done | bytes 200720
  446.3 1.8 copy.46
  448.1 80.5 %reduce-scatter.6.cloned.1.call-done = bf16[320,448]{1,0:T(8,128)(2,1)} async-done(((bf16[5120,448]{1,0:T(8,128)(2,1)}), bf16[320,448]{1,0:T(8,128)(2,1)}) %reduce-scatter.6.cloned.1.call-update) | async-done | bytes 286736 | tf_op jit(solution)/shard_map/reduce_scatter | solution.py:95
  (57 shorter events, 0.7 us)
Async XLA Ops:
  7.2 1.9 copy-start
  7.2 45.2 %all-gather.3.cloned.1.call-start = ((), (), s32[]{:S(2)}) async-start(), calls=%async_computation.4 | async-start | bytes 3096576 | tf_op jit(solution)/shard_map/all_gather | solution.py:72
  9.1 3.1 copy-start.10
  9.1 3.1 copy-start.11
  11.2 0.9 copy-start.4
  11.2 4.1 copy-start.1
  17.4 33.1 %copy-start.2 = (s32[128]{0:T(128)S(1)}, s32[128]{0:T(128)}, u32[]{:S(2)}) copy-start(s32[128]{0:T(128)} %param.21) | copy-start | bytes 1540
  19.0 32.4 %copy-start.3 = (s32[128]{0:T(128)S(1)}, s32[128]{0:T(128)}, u32[]{:S(2)}) copy-start(s32[128]{0:T(128)} %param.22) | copy-start | bytes 1540
  19.0 28.2 %all-to-all-start = ((bf16[16,6,5120]{2,1,0:T(8,128)(2,1)}), bf16[16,6,5120]{2,1,0:T(8,128)(2,1)}, u32[]{:S(2)}, u32[]{:S(2)}) async-start(bf16[16,6,5120]{2,1,0:T(8,128)(2,1)} %copy.35), calls=%async_computation | async-start | bytes 2621440 | tf_op jit(solution)/shard_map/all_to_all | solution.py:63
  26.4 54.2 %all-gather.5.cloned.1.call-start = ((), (), s32[]{:S(2)}) async-start(), calls=%async_computation.5 | async-start | bytes 4423680 | tf_op jit(solution)/shard_map/all_gather | solution.py:71
  50.5 121.2 %all-reduce.4.cloned.1.call-start = ((), (), s32[]{:S(2)}) async-start(), calls=%async_computation.6 | async-start | bytes 7864320 | tf_op jit(solution)/shard_map/psum | solution.py:106
  80.5 12.9 %slice-start = ((s8[4587520]{0:T(1024)(128)(4,1)}), s8[4194304]{0:T(1024)(128)(4,1)S(1)}, s32[]{:S(2)}) async-start(s8[4587520]{0:T(1024)(128)(4,1)} %bitcast.42), calls=%async_computation.10 | async-start | bytes 8388608
  84.9 6.3 %copy-start.5 = (bf16[8,48,5120]{2,1,0:T(8,128)(2,1)}, bf16[8,48,5120]{2,1,0:T(8,128)(2,1)S(1)}, u32[]{:S(2)}) copy-start(bf16[8,48,5120]{2,1,0:T(8,128)(2,1)S(1)} %copy.37) | copy-start | bytes 11796484
  84.9 6.3 %copy-start.6 = (bf16[384,3584]{1,0:T(8,128)(2,1)S(1)}, bf16[384,3584]{1,0:T(8,128)(2,1)}, u32[]{:S(2)}) copy-start(bf16[384,3584]{1,0:T(8,128)(2,1)} %gather_fusion) | copy-start | bytes 8257540
  84.9 6.3 %copy-start.12 = (bf16[448,3584]{1,0:T(8,128)(2,1)S(1)}, bf16[448,3584]{1,0:T(8,128)(2,1)}, u32[]{:S(2)}) copy-start(bf16[448,3584]{1,0:T(8,128)(2,1)} %param.19) | copy-start | bytes 9633796
  85.0 8.4 %slice-start.1 = ((s8[4587520]{0:T(1024)(128)(4,1)}), s8[393216]{0:T(1024)(128)(4,1)S(1)}, s32[]{:S(2)}) async-start(s8[4587520]{0:T(1024)(128)(4,1)} %bitcast.42), calls=%async_computation.11 | async-start | bytes 786432
  91.3 2.1 copy-start.13
  93.4 2.3 copy-start.9
  99.8 268.5 %all-reduce.6.cloned.1.call-start = ((), (), s32[]{:S(2)}) async-start(), calls=%async_computation.9 | async-start | bytes 13107200
  204.2 4.5 copy-start.8
  207.8 0.8 copy-start.7
  212.5 233.8 %reduce-scatter.8.cloned.1.call-start = ((), (), s32[]{:S(2)}) async-start(), calls=%async_computation.8 | async-start | bytes 3899392
  224.0 304.6 %reduce-scatter.6.cloned.1.call-start = ((), (), s32[]{:S(2)}) async-start(), calls=%async_computation.7 | async-start | bytes 5570560 | tf_op jit(solution)/shard_map/reduce_scatter | solution.py:95
Sparse Core Ops, SparseCore 0:
  9.7 29.0 all-gather.2
  50.6 29.8 all-gather.4
  100.0 71.7 all-reduce.3
  212.6 155.7 all-reduce.5
  371.6 74.6 reduce-scatter.7
  450.1 78.4 reduce-scatter.5
where the time goes:
time: 536 us; the launch traced here: 535 us
  waiting for transfers between devices  394 us (74%)
  local copies, waits for them, and re-layouts  48.5 us (9%)
  matrix products  40.5 us (8%)
  blocking collectives  24.9 us (5%)
  between operations  14.4 us (3%)
  starting transfers between devices  7.54 us (1%)
  other arithmetic  5.38 us (1%)
    unnamed x8, waiting for transfers between devices  208 us
    reduce_scatter x1, waiting for transfers between devices, per_device(): lax.psum_scatter(grad_in_part.astype(jnp.bfloat16), 'seq', scatter_dimens...  80.5 us
    psum x1, waiting for transfers between devices, per_device(): summed = lax.psum(row_part.astype(jnp.bfloat16), 'tp').astype(jnp.float32)  71.8 us
    all_to_all x1, blocking collectives, per_device(): lax.all_to_all(returning, 'seq', split_axis=0, concat_axis=0, tiled=True)  24.9 us
    all_to_all x1, waiting for transfers between devices, per_device(): lax.all_to_all(parcels, 'seq', split_axis=0, concat_axis=0, tiled=True)  20.2 us
    unnamed x36, local copies, waits for them, and re-layouts  14.6 us
    all_gather x1, waiting for transfers between devices, per_device(): lax.all_gather(sorted_rows, 'tp', axis=1, tiled=True)  13.5 us
  transfers between devices with their start and end apart: 7, of which 6 were waited for; matrix products, arithmetic and copies ran while one was open for 11% of the time, Pallas kernels for 0%

commit v1 on v0

v1 whole, which is shorter than its diff:
```python
import jax
import jax.numpy as jnp
from jax import lax
from jax.experimental import pallas as pl
from jax.experimental.pallas import tpu as pltpu
from jax.sharding import PartitionSpec as P

F32 = jnp.float32
BF16 = jnp.bfloat16
ZN, CN = 4, 2
YN, XN = 4, 4
TP = ZN * CN
PARAMS = pltpu.CompilerParams(vmem_limit_bytes=48 * 1024 * 1024)

CORE_SWAP = [(i, i ^ 1) for i in range(TP)]
Z_GROUPS = [[z * CN + c for z in range(ZN)] for c in range(CN)]


def z_shift(step):
    return [(z * CN + c, ((z + step) % ZN) * CN + c) for z in range(ZN) for c in range(CN)]


def x_shift(step):
    return [(y * XN + x, y * XN + (x + step) % XN) for y in range(YN) for x in range(XN)]


def y_shift(step):
    return [(y * XN + x, ((y + step) % YN) * XN + x) for y in range(YN) for x in range(XN)]


def gelu_parts(values):
    cumulative = 0.5 * (1.0 + lax.erf(values * 0.7071067811865476))
    density = jnp.exp(-0.5 * values * values) * 0.3989422804014327
    return values * cumulative, cumulative + values * density


def mm(a, b, ca=1, cb=0):
    return lax.dot_general(a, b, (((ca,), (cb,)), ((), ())), preferred_element_type=F32)


def iota(shape, dim):
    return lax.broadcasted_iota(jnp.int32, shape, dim)


def struct(shape, dtype):
    return jax.ShapeDtypeStruct(shape, dtype)


def whole(shape):
    return pl.BlockSpec(shape, lambda *_: (0,) * len(shape))


SMEM = pl.BlockSpec(memory_space=pltpu.SMEM)
VMEM = pl.BlockSpec(memory_space=pltpu.VMEM)


def cost(flops, nbytes, transcendentals=0):
    return pl.CostEstimate(flops=flops, bytes_accessed=nbytes, transcendentals=transcendentals)


def parcel_kernel(ids, offsets, frames, owner, grad, out):
    out[...] = jnp.zeros_like(out)
    s = ids[4]
    row, col = iota((48, 384), 0), iota((48, 384), 1)
    for k in range(8):
        group = s * 8 + k
        start = offsets[group] - s * 384
        count = lax.shift_right_logical(frames[group], 2)
        dest = lax.shift_right_logical(owner[group], 3)
        pick = jnp.where((row < count) & (col == row + start), 1.0, 0.0).astype(BF16)
        out[dest] = mm(pick, grad[...]).astype(BF16)


def parcels_of(ids, offsets, frames, owner, grad):
    return pl.pallas_call(
        parcel_kernel,
        out_shape=struct((16, 48, 448), BF16),
        in_specs=[SMEM, SMEM, SMEM, SMEM, VMEM],
        out_specs=VMEM,
        compiler_params=PARAMS,
        cost_estimate=cost(2 * 384 * 384 * 448, 2_000_000),
    )(ids, offsets, frames, owner, grad)


def select_kernel(ids, owner, arrived, keep, give):
    s, c = ids[4], ids[3]
    row = iota((192, 128), 0)
    z = lax.shift_right_logical(row * 1366, 16)
    rest = row - z * 48
    slot = lax.shift_right_logical(rest * 10923, 16)
    six = rest - slot * 6
    group = iota((192, 128), 1)
    source = jnp.sum(
        jnp.where(owner[...] == s * 8 + slot, lax.shift_right_logical(group, 3), 0), axis=1, keepdims=True
    )
    column = iota((192, 768), 1)
    tokens = arrived[...].reshape(768, 448)
    base = source * 48 + z[:, :1] * 12 + six[:, :1]
    for out, core in ((keep, c), (give, 1 - c)):
        route = jnp.where(column == base + core * 6, 1.0, 0.0).astype(BF16)
        out[...] = mm(route, tokens).astype(BF16)


def select_of(ids, owner, arrived):
    return pl.pallas_call(
        select_kernel,
        out_shape=(struct((192, 448), BF16), struct((192, 448), BF16)),
        in_specs=[SMEM, VMEM, VMEM],
        out_specs=(VMEM, VMEM),
        compiler_params=PARAMS,
        cost_estimate=cost(4 * 192 * 768 * 448, 1_500_000),
    )(ids, owner.reshape(1, 128), arrived)


def encode_kernel(context, residual, weight, gain, bias, stacked, normed, inverse, scratch):
    stream = residual[...].astype(F32) + mm(context[...], weight[...])
    centered = stream - jnp.mean(stream, axis=-1, keepdims=True)
    inv = lax.rsqrt(jnp.mean(centered * centered, axis=-1, keepdims=True) + 1e-05)
    norm = centered * inv
    normed[...] = norm
    inverse[...] = jnp.broadcast_to(inv, inverse.shape)
    encoded = norm * gain[...] + bias[...]
    for piece in range(10):
        scratch[piece] = encoded[:, piece * 128 : (piece + 1) * 128]
    for r in range(4):
        for piece in range(10):
            at = r * 1280 + piece * 128
            stacked[:, at : at + 128] = scratch[piece, pl.ds(r, 48, stride=4), :].astype(BF16)


def encode_of(context, residual, weight, gain, bias):
    return pl.pallas_call(
        encode_kernel,
        out_shape=(struct((48, 5120), BF16), struct((192, 1280), F32), struct((192, 128), F32)),
        in_specs=[VMEM] * 5,
        out_specs=(VMEM,) * 3,
        scratch_shapes=[pltpu.VMEM((10, 192, 128), F32)],
        compiler_params=PARAMS,
        cost_estimate=cost(2 * 192 * 1280 * 1280, 6_000_000),
    )(context, residual, weight, gain.reshape(1, 1280), bias.reshape(1, 1280))


def norm_back_kernel(rows, normed, inverse, gain, out, scratch):
    for r in range(4):
        for piece in range(10):
            at = r * 1280 + piece * 128
            total = rows[0, :, at : at + 128].astype(F32)
            for k in range(1, 4):
                total = total + rows[k, :, at : at + 128].astype(F32)
            scratch[piece, pl.ds(r, 48, stride=4), :] = total.astype(BF16).astype(F32)
    scaled = jnp.concatenate([scratch[piece] for piece in range(10)], axis=1) * gain[...]
    norm = normed[...]
    mean = jnp.mean(scaled, axis=-1, keepdims=True)
    along = jnp.mean(scaled * norm, axis=-1, keepdims=True)
    out[...] = (inverse[:, :1] * (scaled - mean - norm * along)).astype(BF16)


def norm_back_of(rows, normed, inverse, gain):
    return pl.pallas_call(
        norm_back_kernel,
        out_shape=struct((192, 1280), BF16),
        in_specs=[VMEM] * 4,
        out_specs=VMEM,
        scratch_shapes=[pltpu.VMEM((10, 192, 128), F32)],
        compiler_params=PARAMS,
        cost_estimate=cost(192 * 1280 * 20, 4_000_000),
    )(rows, normed, inverse, gain.reshape(1, 1280))


def preact_kernel(ids, b0, b1, b2, b3, own_w, other_w, stk, hid_own, hid_other, slope_own, slope_other, acc, acc_other):
    i = pl.program_id(0)
    for step, block in enumerate((b0, b1, b2, b3)):
        at = pl.multiple_of(lax.rem(ids[2] + step, 4) * 48, 16)
        stk[pl.ds(at, 48), :] = block[...]

    @pl.when(i == 0)
    def _():
        acc[...] = jnp.zeros_like(acc)
        acc_other[...] = jnp.zeros_like(acc_other)

    rows = stk[...]
    acc[...] += mm(rows, own_w[...])
    acc_other[...] += mm(rows, other_w[...])

    @pl.when(i == pl.num_programs(0) - 1)
    def _():
        hidden, slope = gelu_parts(acc[...])
        hid_own[...] = hidden.astype(BF16)
        slope_own[...] = slope
        hidden, slope = gelu_parts(acc_other[...])
        hid_other[...] = hidden.astype(BF16)
        slope_other[...] = slope


def preact_of(ids, blocks, own_w, other_w):
    return pl.pallas_call(
        preact_kernel,
        out_shape=(
            struct((192, 5120), BF16),
            struct((192, 448), BF16),
            struct((192, 448), BF16),
            struct((192, 448), F32),
            struct((192, 448), F32),
        ),
        grid=(5,),
        in_specs=[SMEM]
        + [pl.BlockSpec((48, 1024), lambda i: (0, i))] * 4
        + [pl.BlockSpec((1024, 448), lambda i: (i, 0))] * 2,
        out_specs=(pl.BlockSpec((192, 1024), lambda i: (0, i)),) + (whole((192, 448)),) * 4,
        scratch_shapes=[pltpu.VMEM((192, 448), F32)] * 2,
        compiler_params=PARAMS,
        cost_estimate=cost(4 * 192 * 5120 * 448, 13_000_000, 4 * 192 * 448),
    )(ids, *blocks, own_w, other_w)


def pre_grad_kernel(
    ids, g0, g1, g2, g3, out_own, out_other, in_own, in_other, hid_other, slope_own, slope_other,
    row_part, grads, pre_own, send, acc, acc_other,
):
    i = pl.program_id(0)

    @pl.when(i == 0)
    def _():
        acc[...] = jnp.zeros_like(acc)
        acc_other[...] = jnp.zeros_like(acc_other)

    for step, block in enumerate((g0, g1, g2, g3)):

        @pl.when(i == step)
        def _(block=block):
            piece = block[...]
            grads[...] = piece
            acc[...] += mm(piece, out_own[...], 1, 1)
            acc_other[...] += mm(piece, out_other[...], 1, 1)

    @pl.when(i == 3)
    def _():
        pre_own[...] = (acc[...] * slope_own[...]).astype(BF16)
        send[0:192, :] = (acc_other[...] * slope_other[...]).astype(BF16)
        send[192:384, :] = hid_other[...]

    @pl.when(i > 3)
    def _():
        row_part[...] = (mm(pre_own[...], in_own[...], 1, 1) + mm(send[0:192, :], in_other[...], 1, 1)).astype(BF16)


def pre_grad_of(ids, blocks, out_own, out_other, in_own, in_other, hid_other, slope_own, slope_other):
    def turn(i, ids):
        return (0, lax.rem(ids[2] + jnp.minimum(i, 3), 4))

    def later(i, ids):
        return (jnp.maximum(i - 4, 0), 0)

    return pl.pallas_call(
        pre_grad_kernel,
        out_shape=(
            struct((192, 5120), BF16),
            struct((192, 3584), BF16),
            struct((192, 448), BF16),
            struct((384, 448), BF16),
        ),
        grid_spec=pltpu.PrefetchScalarGridSpec(
            num_scalar_prefetch=1,
            grid=(9,),
            in_specs=[whole((192, 896))] * 4
            + [pl.BlockSpec((448, 896), turn)] * 2
            + [pl.BlockSpec((1024, 448), later)] * 2
            + [whole((192, 448))] * 3,
            out_specs=(
                pl.BlockSpec((192, 1024), lambda i, ids: (0, jnp.maximum(i - 4, 0))),
                pl.BlockSpec((192, 896), turn),
                whole((192, 448)),
                whole((384, 448)),
            ),
            scratch_shapes=[pltpu.VMEM((192, 448), F32)] * 2,
        ),
        compiler_params=PARAMS,
        cost_estimate=cost(4 * 192 * 448 * (3584 + 5120), 22_000_000),
    )(ids, *blocks, out_own, out_other, in_own, in_other, hid_other, slope_own, slope_other)


def weight_grad_kernel(ids, stk, stk_other, og, og_other, pre, hid, recv, *outs):
    i = pl.program_id(0)
    y_here, x_here = ids[0], ids[1]
    x_first, y_first = outs[:4], outs[4:]

    @pl.when(i < 8)
    def _():
        y = lax.shift_right_logical(i, 1)
        value = (mm(stk[...], pre[...], 0, 0) + mm(stk_other[...], recv[0:192, :], 0, 0)).astype(BF16)
        y_turn = lax.rem(y - y_here + 4, 4)
        for n in range(2):
            x = lax.rem(i, 2) * 2 + n
            x_turn = lax.rem(x - x_here + 4, 4)
            for k in range(4):

                @pl.when(x_turn == k)
                def _(k=k, n=n):
                    x_first[k][y] = value[n * 320 : n * 320 + 272]

                @pl.when(y_turn == k)
                def _(k=k, n=n, x=x):
                    y_first[k][x, 0:48, :] = value[n * 320 + 272 : n * 320 + 320]

    @pl.when(i >= 8)
    def _():
        y = i - 8
        value = (mm(og[...], hid[...], 0, 0) + mm(og_other[...], recv[192:384, :], 0, 0)).astype(BF16)
        y_turn = lax.rem(y - y_here + 4, 4)
        for k in range(4):

            @pl.when(y_turn == k)
            def _(k=k):
                for x in range(4):
                    y_first[k][x, 48:272, :] = value[x * 224 : x * 224 + 224]


def weight_grads_of(ids, stk, stk_other, og, og_other, pre, hid, recv):
    first = pl.BlockSpec((192, 640), lambda i, ids: (0, jnp.minimum(i, 7)))
    second = pl.BlockSpec((192, 896), lambda i, ids: (0, jnp.maximum(i - 8, 0)))
    return pl.pallas_call(
        weight_grad_kernel,
        out_shape=(struct((4, 272, 448), BF16),) * 8,
        grid_spec=pltpu.PrefetchScalarGridSpec(
            num_scalar_prefetch=1,
            grid=(12,),
            in_specs=[first, first, second, second, whole((192, 448)), whole((192, 448)), whole((384, 448))],
            out_specs=(whole((4, 272, 448)),) * 8,
        ),
        compiler_params=PARAMS,
        cost_estimate=cost(4 * 192 * 448 * (3584 + 5120), 16_000_000),
    )(ids, stk, stk_other, og, og_other, pre, hid, recv)


def spread_kernel(where, a, b, c, d, *outs):
    i = pl.program_id(0)
    value = (a[0].astype(F32) + b[0].astype(F32) + c[0].astype(F32) + d[0].astype(F32)).astype(BF16)
    for k in range(4):

        @pl.when(i == k)
        def _(k=k):
            outs[k][...] = value


def spread_of(where, parts):
    block = pl.BlockSpec((1, 272, 448), lambda i, where: (lax.rem(where[0] + i, 4), 0, 0))
    return pl.pallas_call(
        spread_kernel,
        out_shape=(struct((272, 448), BF16),) * 4,
        grid_spec=pltpu.PrefetchScalarGridSpec(
            num_scalar_prefetch=1,
            grid=(4,),
            in_specs=[block] * 4,
            out_specs=(whole((272, 448)),) * 4,
        ),
        compiler_params=PARAMS,
        cost_estimate=cost(16 * 272 * 448, 6_000_000),
    )(where, *parts)


def finish_kernel(a0, a1, a2, a3, b0, b1, b2, b3, grad_in, grad_out):
    first = a0[...].astype(F32) + a1[...].astype(F32) + a2[...].astype(F32) + a3[...].astype(F32)
    second = b0[...].astype(F32) + b1[...].astype(F32) + b2[...].astype(F32) + b3[...].astype(F32)
    grad_in[0:272, :] = first.astype(BF16)
    grad_in[272:320, :] = second[0:48].astype(BF16)
    grad_out[...] = second[48:272].T.astype(BF16)


def finish_of(first, second):
    return pl.pallas_call(
        finish_kernel,
        out_shape=(struct((320, 448), BF16), struct((448, 224), BF16)),
        in_specs=[VMEM] * 8,
        out_specs=(VMEM, VMEM),
        compiler_params=PARAMS,
        cost_estimate=cost(8 * 272 * 448, 3_000_000),
    )(*first, *second)


def ring_of(parts, shift):
    far = lax.ppermute(parts[2], "seq", shift(2))
    up = lax.ppermute(parts[1], "seq", shift(1))
    down = lax.ppermute(parts[3], "seq", shift(-1))
    return (parts[0], up, down, far)


def out_weight_kernel(ctx, ctx_other, grad, grad_other, out):
    out[...] = (mm(ctx[...], grad[...], 0, 0) + mm(ctx_other[...], grad_other[...], 0, 0)).astype(BF16)


def out_weight_of(ctx, ctx_other, grad, grad_other):
    block = pl.BlockSpec((192, 128), lambda i: (0, i))
    return pl.pallas_call(
        out_weight_kernel,
        out_shape=struct((640, 1280), BF16),
        grid=(5,),
        in_specs=[block, block, whole((192, 1280)), whole((192, 1280))],
        out_specs=pl.BlockSpec((128, 1280), lambda i: (i, 0)),
        compiler_params=PARAMS,
        cost_estimate=cost(4 * 192 * 640 * 1280, 4_000_000),
    )(ctx, ctx_other, grad, grad_other)


def swap(value):
    return lax.ppermute(value, "tp", CORE_SWAP)


def z_blocks(block):
    far = lax.ppermute(block, "tp", z_shift(2))
    behind = lax.ppermute(block, "tp", z_shift(1))
    ahead = lax.ppermute(block, "tp", z_shift(-1))
    return (block, ahead, far, behind)


def z_exchange(parts):
    return lax.all_to_all(parts, "tp", split_axis=0, concat_axis=0, axis_index_groups=Z_GROUPS, tiled=True)


def per_device(
    context,
    residual_in,
    out_weight,
    final_norm_weight,
    final_norm_bias,
    adapter_in,
    adapter_out,
    emb_grad,
    group_offsets,
    group_frames,
    group_owner,
):
    s = lax.axis_index("seq")
    t = lax.axis_index("tp")
    c = t % 2
    ids = jnp.stack([s // 4, s % 4, t // 2, c, s]).astype(jnp.int32)
    context = context.reshape(192, 1280)
    residual_in = residual_in.reshape(192, 1280)

    stacked_here, normed, inverse = encode_of(context, residual_in, out_weight, final_norm_weight, final_norm_bias)
    in_other = swap(adapter_in)
    out_other = swap(adapter_out)
    rows = z_blocks(stacked_here)

    parcels = parcels_of(ids, group_offsets, group_frames, group_owner, emb_grad)
    arrived = lax.all_to_all(parcels, "seq", split_axis=0, concat_axis=0, tiled=True)
    keep, give = select_of(ids, group_owner, arrived)
    got = swap(give)
    grad_pair = jnp.where(c == 0, jnp.concatenate([keep, got], axis=1), jnp.concatenate([got, keep], axis=1))
    grads = z_blocks(grad_pair)

    place = jnp.arange(1280, dtype=jnp.int32)
    core = (place // 640 + c) % 2
    target = (2 * ((place % 640) // 160) + core) * 10 + ((place % 160) // 10) * 80 + place % 10
    order = (jnp.arange(1280, dtype=jnp.int32)[:, None] == target[None, :]).astype(BF16)
    ordered = mm(context, order).astype(BF16)
    context_keep, context_got = ordered[:, :640], swap(ordered[:, 640:])

    stk, hid_own, hid_other, slope_own, slope_other = preact_of(ids, rows, adapter_in, in_other)
    stk_other = swap(stk)
    row_part, og, pre_own, send = pre_grad_of(
        ids, grads, adapter_out, out_other, adapter_in, in_other, hid_other, slope_own, slope_other
    )
    row_parts = z_exchange(row_part.reshape(4, 48, 5120))
    recv = swap(send)
    og_other = swap(og)

    parts = weight_grads_of(ids, stk, stk_other, og, og_other, pre_own, hid_own, recv)
    x_first = ring_of(parts[:4], x_shift)
    y_first = ring_of(parts[4:], y_shift)
    x_first = ring_of(spread_of(ids[0:1], x_first), y_shift)
    y_first = ring_of(spread_of(ids[1:2], y_first), x_shift)
    grad_in, grad_out = finish_of(x_first, y_first)

    d_residual = norm_back_of(row_parts, normed, inverse, final_norm_weight)
    residual_other = swap(d_residual)
    d_context = mm(d_residual, out_weight, 1, 1).astype(BF16)
    weight_part = out_weight_of(context_keep, context_got, d_residual, residual_other)
    weight_z = z_exchange(weight_part.reshape(4, 160, 1280))
    weight_z = jnp.sum(weight_z.astype(F32), axis=0).astype(BF16)
    pieces = lax.all_to_all(weight_z.reshape(16, 10, 1280), "seq", split_axis=0, concat_axis=0, tiled=True)
    d_out_weight = jnp.sum(pieces.astype(F32), axis=0)

    return (
        d_context.reshape(8, 24, 1280),
        d_residual.reshape(8, 24, 1280),
        d_out_weight,
        grad_in,
        grad_out,
    )


def solution(mesh):
    placed = (
        P("seq", "tp", None),
        P("seq", "tp", None),
        P(),
        P(),
        P(),
        P(None, "tp"),
        P("tp", None),
        P("seq", "tp"),
        P(),
        P(),
        P(),
    )
    return jax.shard_map(
        per_device,
        mesh=mesh,
        in_specs=placed,
        out_specs=(
            P("seq", "tp", None),
            P("seq", "tp", None),
            P(("seq", "tp"), None),
            P("seq", "tp"),
            P("tp", "seq"),
        ),
        check_vma=False,
    )
```

time: 536 us -> 256 us (0.48)
  waiting for transfers between devices: 394 us -> 84.7 us
  Pallas kernels: 0 us -> 55.7 us
  starting transfers between devices: 7.54 us -> 46.1 us
  matrix products: 40.5 us -> 3.43 us
  between operations: 14.4 us -> 0.94 us
  local copies, waits for them, and re-layouts: 48.5 us -> 36 us
    unnamed x8 -> x0, waiting for transfers between devices: 208 us -> none
    reduce_scatter x1 -> x0, waiting for transfers between devices: 80.5 us -> none  [per_device(): lax.psum_scatter(grad_in_part.astype(jnp.bfloat16), 'seq', scatter_dimens...]
    psum x1 -> x0, waiting for transfers between devices: 71.8 us -> none  [per_device(): summed = lax.psum(row_part.astype(jnp.bfloat16), 'tp').astype(jnp.float32)]
    ppermute x0 -> x26, waiting for transfers between devices: none -> 59.9 us  [the longest x4 35.9 us: ring_of(): up = lax.ppermute(parts[1], 'seq', shift(1))]
    pallas_call x0 -> x11, Pallas kernels: none -> 55.7 us  [the longest x1 14.9 us: weight_grads_of(): pl.pallas_call(weight_grad_kernel, out_shape=(struct((4, 272, 448), BF16)...]
    dot_general x12 -> x2, matrix products: 40.5 us -> 3.43 us  [mm(): lax.dot_general(a, b, (((ca,), (cb,)), ((), ())), preferred_element_type=...]
    ppermute x0 -> x26, starting transfers between devices: none -> 30 us  [the longest x4 10.1 us: ring_of(): down = lax.ppermute(parts[3], 'seq', shift(-1))]
    all_gather x2 -> x0, waiting for transfers between devices: 13.6 us -> none  [the longest x1 13.5 us: per_device(): lax.all_gather(sorted_rows, 'tp', axis=1, tiled=True)]
  transfers between devices with their start and end apart: 7 -> 29, of which waited for: 6 -> 12; matrix products, arithmetic and copies ran while one was open for 11% -> 11% of each run, Pallas kernels for 0% -> 22%
where the time goes in v1:
time: 256 us; the launch traced here: 255 us
  waiting for transfers between devices  84.7 us (33%)
  Pallas kernels  55.7 us (22%)
  starting transfers between devices  46.1 us (18%)
  local copies, waits for them, and re-layouts  36 us (14%)
  blocking collectives  21.5 us (8%)
  other arithmetic  6.41 us (3%)
  matrix products  3.43 us (1%)
    ppermute x4, waiting for transfers between devices, ring_of(): up = lax.ppermute(parts[1], 'seq', shift(1))  35.9 us
    unnamed x68, local copies, waits for them, and re-layouts  26.2 us
    all_to_all x2, waiting for transfers between devices, z_exchange(): lax.all_to_all(parts, 'tp', split_axis=0, concat_axis=0, axis_index_group...  24.8 us
    all_to_all x1, blocking collectives, per_device(): lax.all_to_all(parcels, 'seq', split_axis=0, concat_axis=0, tiled=True)  21.5 us
    pallas_call x1, Pallas kernels, weight_grads_of(): pl.pallas_call(weight_grad_kernel, out_shape=(struct((4, 272, 448), BF16)...  14.9 us
    pallas_call x1, Pallas kernels, pre_grad_of(): pl.pallas_call(pre_grad_kernel, out_shape=(struct((192, 5120), BF16), str...  13.8 us
    ppermute x4, waiting for transfers between devices, ring_of(): down = lax.ppermute(parts[3], 'seq', shift(-1))  12.8 us
    ppermute x4, starting transfers between devices, ring_of(): down = lax.ppermute(parts[3], 'seq', shift(-1))  10.1 us
  transfers between devices with their start and end apart: 29, of which 12 were waited for; matrix products, arithmetic and copies ran while one was open for 11% of the time, Pallas kernels for 22%

profile of v1, /device:TPU:0, one launch (start us, length us, event | category | flops | bytes accessed | tf_op | source)
XLA Modules:
  0.0 254.7 jit_solution(11745868123778814958)
XLA Ops:
  1.2 1.9 copy.24.grad
  6.2 1.2 shard_map.146
  7.4 21.5 %all_to_all.20.arrived = bf16[16,48,448]{2,1,0:T(8,128)(2,1)S(1)} all-to-all(bf16[16,48,448]{2,1,0:T(8,128)(2,1)S(1)} %shard_map.146), channel_id=1, replica_groups=mesh['seq'=16,'tp'=8] {'seq'}, dimensions={0} | all-to-all | bytes 1376256 | tf_op jit(solution)/shard_map/all_to_all | solution.py:445
  28.9 1.1 shard_map.147
  32.3 2.1 shard_map.148
  36.0 4.0 %collective-permute-start.6 = (bf16[48,5120]{1,0:T(8,128)(2,1)}, bf16[48,5120]{1,0:T(8,128)(2,1)}, u32[]{:S(2)}, u32[]{:S(2)}) collective-permute-start(bf16[48,5120]{1,0:T(8,128)(2,1)} %get-tuple-element.39.b0), channel_id=1, source_target_pairs={{0,6},{1,7},{2,0},{3,1},{4,2},{5,3},{6,4},{7,5},{8,14},{9,15},{10,... | collective-permute-start | bytes 1474568 | tf_op jit(solution)/shard_map/ppermute | solution.py:411
  40.7 1.3 collective-permute-start.8
  42.0 7.5 %copy.27.own_w.in_own = bf16[5120,448]{1,0:T(8,128)(2,1)} copy(bf16[5120,448]{0,1:T(8,128)(2,1)} %param.16) | data formatting | bytes 9175040 | tf_op args[5]
  49.5 2.0 maximum_select_fusion.g0
  51.5 2.0 collective-permute-start.1
  53.5 7.6 %copy.28.other_w.in_other = bf16[5120,448]{1,0:T(8,128)(2,1)} copy(bf16[5120,448]{0,1:T(8,128)(2,1)} %collective-permute-done.5) | data formatting | bytes 9175040 | tf_op jit(solution)/shard_map/ppermute | solution.py:405
  61.1 1.3 collective-permute-done.6.b1
  63.5 3.5 %collective-permute-start.3 = (bf16[192,896]{1,0:T(8,128)(2,1)}, bf16[192,896]{1,0:T(8,128)(2,1)S(1)}, u32[]{:S(2)}, u32[]{:S(2)}) collective-permute-start(bf16[192,896]{1,0:T(8,128)(2,1)} %maximum_select_fusion.g0), channel_id=1, source_target_pairs={{0,2},{1,3},{2,4},{3,5},{4,6},{5,7},{6,0},{7,1},{8,10},{9,11},{10,... | collective-permute-start | bytes 1032200 | tf_op jit(solution)/shard_map/ppermute | solution.py:410
  67.0 8.8 %shard_map.149 = (bf16[192,5120]{1,0:T(8,128)(2,1)}, bf16[192,448]{1,0:T(8,128)(2,1)S(1)}, bf16[192,448]{1,0:T(8,128)(2,1)S(1)}, f32[192,448]{1,0:T(8,128)S(1)}, f32[192,448]{1,0:T(8,128)S(1)}) custom-call(s32[5]{0:T(128)S(1)} %stack.23.ids, bf16[48,5120]{1,0:T(8,128)(2,1)} %get-tuple-element.39.b0, bf16[48,5120]{1,0:T(8,128)(2,1)} %collective-permute-done.6.b1, ...), custom_call_target="tpu_custom_call" | custom-call | flops 1761607680 | bytes 13000000 | tf_op jit(solution)/shard_map/pallas_call | solution.py:196
  76.7 4.0 %collective-permute-done.3.g3 = bf16[192,896]{1,0:T(8,128)(2,1)S(1)} collective-permute-done((bf16[192,896]{1,0:T(8,128)(2,1)}, bf16[192,896]{1,0:T(8,128)(2,1)S(1)}, u32[]{:S(2)}, u32[]{:S(2)}) %collective-permute-start.3) | collective-permute-done | bytes 344096 | tf_op jit(solution)/shard_map/ppermute | solution.py:410
  80.7 13.8 %shard_map.150 = (bf16[192,5120]{1,0:T(8,128)(2,1)}, bf16[192,3584]{1,0:T(8,128)(2,1)S(1)}, bf16[192,448]{1,0:T(8,128)(2,1)S(1)}, bf16[384,448]{1,0:T(8,128)(2,1)S(1)}) custom-call(s32[5]{0:T(128)S(1)} %stack.23.ids, bf16[192,896]{1,0:T(8,128)(2,1)} %maximum_select_fusion.g0, bf16[192,896]{1,0:T(8,128)(2,1)} %collective-permute-done.1.g1, ...), custom_call_target="tpu_custom_call" | custom-call | flops 2994733056 | bytes 22000000 | tf_op jit(solution)/shard_map/pallas_call | solution.py:254
  97.1 4.6 %all-to-all-start.1 = ((bf16[4,48,5120]{2,1,0:T(8,128)(2,1)}), bf16[4,48,5120]{2,1,0:T(8,128)(2,1)}, u32[]{:S(2)}, u32[]{:S(2)}) async-start(bf16[4,48,5120]{2,1,0:T(8,128)(2,1)} %bitcast.23), calls=%async_computation.1 | async-start | bytes 3932160 | tf_op jit(solution)/shard_map/all_to_all | solution.py:416
  102.3 24.8 %all-to-all-done.1.rows = bf16[4,48,5120]{2,1,0:T(8,128)(2,1)} async-done(((bf16[4,48,5120]{2,1,0:T(8,128)(2,1)}), bf16[4,48,5120]{2,1,0:T(8,128)(2,1)}, u32[]{:S(2)}, u32[]{:S(2)}) %all-to-all-start.1) | async-done | bytes 1966112 | tf_op jit(solution)/shard_map/all_to_all | solution.py:416
  127.1 1.2 copy-done.9
  128.3 3.1 %shard_map.151.grad = bf16[192,1280]{1,0:T(8,128)(2,1)} custom-call(bf16[4,48,5120]{2,1,0:T(8,128)(2,1)} %all-to-all-done.1.rows, f32[192,1280]{1,0:T(8,128)S(1)} %copy-done.9, f32[192,128]{1,0:T(8,128)S(1)} %copy-done.14, f32[1,1280]{1,0:T(1,128)S(1)} %reshape.109.gain), custom_call_target="tpu_custom_call" | custom-call | flops 4915200 | bytes 4000000 | tf_op jit(solution)/shard_map/pallas_call | solution.py:159
  131.5 14.9 %shard_map.153 = (bf16[4,272,448]{2,1,0:T(8,128)(2,1)S(1)}, bf16[4,272,448]{2,1,0:T(8,128)(2,1)S(1)}, bf16[4,272,448]{2,1,0:T(8,128)(2,1)S(1)}, bf16[4,272,448]{...) custom-call(s32[5]{0:T(128)S(1)} %stack.23.ids, ...), custom_call_target="tpu_custom_call" | custom-call | flops 2994733056 | bytes 16000000 | tf_op jit(solution)/shard_map/pallas_call | solution.py:321
  146.5 1.4 fusion.3
  149.2 1.1 collective-permute-done.9.ctx_other
  150.3 2.0 shard_map.152
  152.3 1.2 copy-done.1
  153.4 4.4 %all-to-all-start.2 = ((bf16[4,160,1280]{2,1,0:T(8,128)(2,1)}), bf16[4,160,1280]{2,1,0:T(8,128)(2,1)}, u32[]{:S(2)}, u32[]{:S(2)}) async-start(bf16[4,160,1280]{2,1,0:T(8,128)(2,1)} %bitcast.17), calls=%async_computation.2 | async-start | bytes 3276800 | tf_op jit(solution)/shard_map/all_to_all | solution.py:416
  157.8 2.6 %collective-permute-start.21 = (bf16[4,272,448]{2,1,0:T(8,128)(2,1)}, bf16[4,272,448]{2,1,0:T(8,128)(2,1)S(1)}, u32[]{:S(2)}, u32[]{:S(2)}) collective-permute-start(bf16[4,272,448]{2,1,0:T(8,128)(2,1)} %get-tuple-element.61), channel_id=1, source_target_pairs={{0,96},{8,104},{16,112},{24,120},{32,0},{40,8},{48,16},{56,24},{64... | collective-permute-start | bytes 2924552 | tf_op jit(solution)/shard_map/ppermute | solution.py:383
  161.0 2.7 %collective-permute-start.15 = (bf16[4,272,448]{2,1,0:T(8,128)(2,1)}, bf16[4,272,448]{2,1,0:T(8,128)(2,1)}, u32[]{:S(2)}, u32[]{:S(2)}) collective-permute-start(bf16[4,272,448]{2,1,0:T(8,128)(2,1)} %copy-done.21), channel_id=1, source_target_pairs={{0,24},{8,0},{16,8},{24,16},{32,56},{40,32},{48,40},{56,48},{64,88... | collective-permute-start | bytes 2924552 | tf_op jit(solution)/shard_map/ppermute | solution.py:383
  163.6 35.2 %collective-permute-done.20.b = bf16[4,272,448]{2,1,0:T(8,128)(2,1)} collective-permute-done((bf16[4,272,448]{2,1,0:T(8,128)(2,1)}, bf16[4,272,448]{2,1,0:T(8,128)(2,1)}, u32[]{:S(2)}, u32[]{:S(2)}) %collective-permute-start.20) | collective-permute-done | bytes 974880 | tf_op jit(solution)/shard_map/ppermute | solution.py:382
  199.8 9.1 %collective-permute-done.21.c = bf16[4,272,448]{2,1,0:T(8,128)(2,1)S(1)} collective-permute-done((bf16[4,272,448]{2,1,0:T(8,128)(2,1)}, bf16[4,272,448]{2,1,0:T(8,128)(2,1)S(1)}, u32[]{:S(2)}, u32[]{:S(2)}) %collective-permute-start.21) | collective-permute-done | bytes 974880 | tf_op jit(solution)/shard_map/ppermute | solution.py:383
  208.8 1.2 copy-done.7
  210.1 3.4 %shard_map.155 = (bf16[272,448]{1,0:T(8,128)(2,1)S(1)}, bf16[272,448]{1,0:T(8,128)(2,1)}, bf16[272,448]{1,0:T(8,128)(2,1)S(1)}, bf16[272,448]{1,0:T(8,128)(2,1)S(1)}) custom-call(s32[1]{0:T(128)} %bitcast.1.where, bf16[4,272,448]{2,1,0:T(8,128)(2,1)S(1)} %copy-done.7, bf16[4,272,448]{2,1,0:T(8,128)(2,1)} %collective-permute-done.20.b, ...), custom_call_target="tpu_custom_call" | custom-call | flops 1949696 | bytes 6000000 | tf_op jit(solution)/shard_map/pallas_call | solution.py:347
  215.5 2.5 reduce_sum.21
  218.0 2.0 reshape.115
  220.0 7.1 %all-to-all-start.3 = ((bf16[16,10,1280]{2,1,0:T(8,128)(2,1)}), bf16[16,10,1280]{2,1,0:T(8,128)(2,1)}, u32[]{:S(2)}, u32[]{:S(2)}) async-start(bf16[16,10,1280]{2,1,0:T(8,128)(2,1)} %reshape.115), calls=%async_computation.3 | async-start | bytes 1310720 | tf_op jit(solution)/shard_map/all_to_all | solution.py:480
  227.1 3.1 %collective-permute-start.24 = (bf16[272,448]{1,0:T(8,128)(2,1)}, bf16[272,448]{1,0:T(8,128)(2,1)S(1)}, u32[]{:S(2)}, u32[]{:S(2)}) collective-permute-start(bf16[272,448]{1,0:T(8,128)(2,1)} %copy-done.25), channel_id=1, source_target_pairs={{0,24},{8,0},{16,8},{24,16},{32,56},{40,32},{48,40},{56,48},{64,88... | collective-permute-start | bytes 731144 | tf_op jit(solution)/shard_map/ppermute | solution.py:383
  231.1 1.2 copy-done.6
  232.3 3.2 %shard_map.154 = (bf16[272,448]{1,0:T(8,128)(2,1)S(1)}, bf16[272,448]{1,0:T(8,128)(2,1)S(1)}, bf16[272,448]{1,0:T(8,128)(2,1)S(1)}, bf16[272,448]{1,0:T(8,128)(2,1)S(1)}) custom-call(s32[1]{0:T(128)} %bitcast.where, bf16[4,272,448]{2,1,0:T(8,128)(2,1)S(1)} %copy-done.6, bf16[4,272,448]{2,1,0:T(8,128)(2,1)} %collective-permute-done.14.b, ...), custom_call_target="tpu_custom_call" | custom-call | flops 1949696 | bytes 6000000 | tf_op jit(solution)/shard_map/pallas_call | solution.py:347
  235.6 1.5 collective-permute-start.17
  237.1 1.8 collective-permute-start.18
  238.9 1.8 collective-permute-start.19
  240.6 2.0 convolution_convert_fusion
  242.6 1.2 collective-permute-done.24.b2
  243.8 2.0 collective-permute-done.25.b3
  246.4 2.6 %collective-permute-done.18.a2 = bf16[272,448]{1,0:T(8,128)(2,1)S(1)} collective-permute-done((bf16[272,448]{1,0:T(8,128)(2,1)S(1)}, bf16[272,448]{1,0:T(8,128)(2,1)S(1)}, u32[]{:S(2)}, u32[]{:S(2)}) %collective-permute-start.18) | collective-permute-done | bytes 243744 | tf_op jit(solution)/shard_map/ppermute | solution.py:383
  249.0 1.8 collective-permute-done.19.a3
  250.8 2.1 shard_map.156
  252.9 1.8 convert_reduce_fusion
  (102 shorter events, 19.6 us)
Async XLA Ops:
  0.6 50.9 %collective-permute-start.5 = (bf16[5120,448]{0,1:T(8,128)(2,1)}, bf16[5120,448]{0,1:T(8,128)(2,1)}, u32[]{:S(2)}, u32[]{:S(2)}) collective-permute-start(bf16[5120,448]{0,1:T(8,128)(2,1)} %param.16), channel_id=1, source_target_pairs={{0,1},{1,0},{2,3},{3,2},{4,5},{5,4},{6,7},{7,6},{8,9},{9,8},{10,11... | collective-permute-start | bytes 13762568 | tf_op jit(solution)/shard_map/ppermute | solution.py:405
  0.7 80.0 %collective-permute-start.4 = (bf16[448,3584]{1,0:T(8,128)(2,1)}, bf16[448,3584]{1,0:T(8,128)(2,1)}, u32[]{:S(2)}, u32[]{:S(2)}) collective-permute-start(bf16[448,3584]{1,0:T(8,128)(2,1)} %out_own.1), channel_id=1, source_target_pairs={{0,1},{1,0},{2,3},{3,2},{4,5},{5,4},{6,7},{7,6},{8,9},{9,8},{10,11... | collective-permute-start | bytes 9633800 | tf_op jit(solution)/shard_map/ppermute | solution.py:405
  1.2 27.7 %copy-start.18 = (s32[128]{0:T(128)S(1)}, s32[128]{0:T(128)}, u32[]{:S(2)}) copy-start(s32[128]{0:T(128)} %owner.1) | copy-start | bytes 1540
  6.2 24.0 %copy-start.31 = (f32[1280]{0:T(1024)S(1)}, f32[1280]{0:T(1024)}, u32[]{:S(2)}) copy-start(f32[1280]{0:T(1024)} %param.14) | copy-start | bytes 15364
  6.2 24.0 %copy-start.32 = (f32[1280]{0:T(1024)S(1)}, f32[1280]{0:T(1024)}, u32[]{:S(2)}) copy-start(f32[1280]{0:T(1024)} %param.15) | copy-start | bytes 15364
  6.2 24.0 %copy-start = (bf16[1280,1280]{1,0:T(8,128)(2,1)S(1)}, bf16[1280,1280]{1,0:T(8,128)(2,1)}, u32[]{:S(2)}) copy-start(bf16[1280,1280]{1,0:T(8,128)(2,1)} %weight.1) | copy-start | bytes 9830404
  30.1 9.9 %collective-permute-start = (bf16[192,448]{1,0:T(8,128)(2,1)S(1)}, bf16[192,448]{1,0:T(8,128)(2,1)S(1)}, u32[]{:S(2)}, u32[]{:S(2)}) collective-permute-start(bf16[192,448]{1,0:T(8,128)(2,1)S(1)} %get-tuple-element.38), channel_id=1, source_target_pairs={{0,1},{1,0},{2,3},{3,2},{4,5},{5,4},{6,7},{7,6},{8,9},{9,8},{10,11... | collective-permute-start | bytes 516104 | tf_op jit(solution)/shard_map/ppermute | solution.py:405
  36.0 26.4 %collective-permute-start.6 = (bf16[48,5120]{1,0:T(8,128)(2,1)}, bf16[48,5120]{1,0:T(8,128)(2,1)}, u32[]{:S(2)}, u32[]{:S(2)}) collective-permute-start(bf16[48,5120]{1,0:T(8,128)(2,1)} %get-tuple-element.39.b0), channel_id=1, source_target_pairs={{0,6},{1,7},{2,0},{3,1},{4,2},{5,3},{6,4},{7,5},{8,14},{9,15},{10,... | collective-permute-start | bytes 1474568 | tf_op jit(solution)/shard_map/ppermute | solution.py:411
  40.0 23.4 %collective-permute-start.7 = (bf16[48,5120]{1,0:T(8,128)(2,1)}, bf16[48,5120]{1,0:T(8,128)(2,1)}, u32[]{:S(2)}, u32[]{:S(2)}) collective-permute-start(bf16[48,5120]{1,0:T(8,128)(2,1)} %get-tuple-element.39.b0), channel_id=1, source_target_pairs={{0,4},{1,5},{2,6},{3,7},{4,0},{5,1},{6,2},{7,3},{8,12},{9,13},{10,... | collective-permute-start | bytes 1474568 | tf_op jit(solution)/shard_map/ppermute | solution.py:409
  40.7 26.3 %collective-permute-start.8 = (bf16[48,5120]{1,0:T(8,128)(2,1)}, bf16[48,5120]{1,0:T(8,128)(2,1)}, u32[]{:S(2)}, u32[]{:S(2)}) collective-permute-start(bf16[48,5120]{1,0:T(8,128)(2,1)} %get-tuple-element.39.b0), channel_id=1, source_target_pairs={{0,2},{1,3},{2,4},{3,5},{4,6},{5,7},{6,0},{7,1},{8,10},{9,11},{10,... | collective-permute-start | bytes 1474568 | tf_op jit(solution)/shard_map/ppermute | solution.py:410
  51.5 25.2 %collective-permute-start.1 = (bf16[192,896]{1,0:T(8,128)(2,1)}, bf16[192,896]{1,0:T(8,128)(2,1)}, u32[]{:S(2)}, u32[]{:S(2)}) collective-permute-start(bf16[192,896]{1,0:T(8,128)(2,1)} %maximum_select_fusion.g0), channel_id=1, source_target_pairs={{0,6},{1,7},{2,0},{3,1},{4,2},{5,3},{6,4},{7,5},{8,14},{9,15},{10,... | collective-permute-start | bytes 1032200 | tf_op jit(solution)/shard_map/ppermute | solution.py:411
  62.4 14.3 %collective-permute-start.2 = (bf16[192,896]{1,0:T(8,128)(2,1)}, bf16[192,896]{1,0:T(8,128)(2,1)S(1)}, u32[]{:S(2)}, u32[]{:S(2)}) collective-permute-start(bf16[192,896]{1,0:T(8,128)(2,1)} %maximum_select_fusion.g0), channel_id=1, source_target_pairs={{0,4},{1,5},{2,6},{3,7},{4,0},{5,1},{6,2},{7,3},{8,12},{9,13},{10,... | collective-permute-start | bytes 1032200 | tf_op jit(solution)/shard_map/ppermute | solution.py:409
  63.5 17.3 %collective-permute-start.3 = (bf16[192,896]{1,0:T(8,128)(2,1)}, bf16[192,896]{1,0:T(8,128)(2,1)S(1)}, u32[]{:S(2)}, u32[]{:S(2)}) collective-permute-start(bf16[192,896]{1,0:T(8,128)(2,1)} %maximum_select_fusion.g0), channel_id=1, source_target_pairs={{0,2},{1,3},{2,4},{3,5},{4,6},{5,7},{6,0},{7,1},{8,10},{9,11},{10,... | collective-permute-start | bytes 1032200 | tf_op jit(solution)/shard_map/ppermute | solution.py:410
  75.7 18.8 %copy-start.26 = (bf16[192,448]{1,0:T(8,128)(2,1)}, bf16[192,448]{1,0:T(8,128)(2,1)S(1)}, u32[]{:S(2)}) copy-start(bf16[192,448]{1,0:T(8,128)(2,1)S(1)} %get-tuple-element.49.hid) | copy-start | bytes 516100
  75.7 55.7 %collective-permute-start.11 = (bf16[192,5120]{1,0:T(8,128)(2,1)}, bf16[192,5120]{1,0:T(8,128)(2,1)}, u32[]{:S(2)}, u32[]{:S(2)}) collective-permute-start(bf16[192,5120]{1,0:T(8,128)(2,1)} %get-tuple-element.46.stk), channel_id=1, source_target_pairs={{0,1},{1,0},{2,3},{3,2},{4,5},{5,4},{6,7},{7,6},{8,9},{9,8},{10,11... | collective-permute-start | bytes 5898248 | tf_op jit(solution)/shard_map/ppermute | solution.py:405
  97.1 30.0 %copy-start.14 = (f32[192,128]{1,0:T(8,128)S(1)}, f32[192,128]{1,0:T(8,128)}, u32[]{:S(2)}) copy-start(f32[192,128]{1,0:T(8,128)} %copy-done.13) | copy-start | bytes 294916
  97.1 30.0 %all-to-all-start.1 = ((bf16[4,48,5120]{2,1,0:T(8,128)(2,1)}), bf16[4,48,5120]{2,1,0:T(8,128)(2,1)}, u32[]{:S(2)}, u32[]{:S(2)}) async-start(bf16[4,48,5120]{2,1,0:T(8,128)(2,1)} %bitcast.23), calls=%async_computation.1 | async-start | bytes 3932160 | tf_op jit(solution)/shard_map/all_to_all | solution.py:416
  101.7 29.8 %collective-permute-start.12 = (bf16[192,3584]{1,0:T(8,128)(2,1)}, bf16[192,3584]{1,0:T(8,128)(2,1)}, u32[]{:S(2)}, u32[]{:S(2)}) collective-permute-start(bf16[192,3584]{1,0:T(8,128)(2,1)} %copy-done.19), channel_id=1, source_target_pairs={{0,1},{1,0},{2,3},{3,2},{4,5},{5,4},{6,7},{7,6},{8,9},{9,8},{10,11... | collective-permute-start | bytes 4128776 | tf_op jit(solution)/shard_map/ppermute | solution.py:405
  101.7 29.7 %collective-permute-start.13 = (bf16[384,448]{1,0:T(8,128)(2,1)}, bf16[384,448]{1,0:T(8,128)(2,1)}, u32[]{:S(2)}, u32[]{:S(2)}) collective-permute-start(bf16[384,448]{1,0:T(8,128)(2,1)} %copy-done.23), channel_id=1, source_target_pairs={{0,1},{1,0},{2,3},{3,2},{4,5},{5,4},{6,7},{7,6},{8,9},{9,8},{10,11... | collective-permute-start | bytes 1032200 | tf_op jit(solution)/shard_map/ppermute | solution.py:405
  127.1 1.2 copy-start.9
  128.3 3.1 %copy-start.27 = (bf16[192,448]{1,0:T(8,128)(2,1)S(1)}, bf16[192,448]{1,0:T(8,128)(2,1)}, u32[]{:S(2)}) copy-start(bf16[192,448]{1,0:T(8,128)(2,1)} %copy-done.26) | copy-start | bytes 516100
  128.3 3.2 %copy-start.29 = (bf16[192,448]{1,0:T(8,128)(2,1)S(1)}, bf16[192,448]{1,0:T(8,128)(2,1)}, u32[]{:S(2)}) copy-start(bf16[192,448]{1,0:T(8,128)(2,1)} %copy-done.28) | copy-start | bytes 516100
  131.4 18.9 %collective-permute-start.10 = (bf16[192,1280]{1,0:T(8,128)(2,1)}, bf16[192,1280]{1,0:T(8,128)(2,1)S(1)}, u32[]{:S(2)}, u32[]{:S(2)}) collective-permute-start(bf16[192,1280]{1,0:T(8,128)(2,1)} %shard_map.151.grad), channel_id=1, source_target_pairs={{0,1},{1,0},{2,3},{3,2},{4,5},{5,4},{6,7},{7,6},{8,9},{9,8},{10,11... | collective-permute-start | bytes 1474568 | tf_op jit(solution)/shard_map/ppermute | solution.py:405
  131.5 15.0 %copy-start.12 = (bf16[8,24,1280]{2,1,0:T(8,128)(2,1)S(1)}, bf16[8,24,1280]{2,1,0:T(8,128)(2,1)}, u32[]{:S(2)}) copy-start(bf16[8,24,1280]{2,1,0:T(8,128)(2,1)} %param.11) | copy-start | bytes 1474564
  146.4 1.6 copy-start.5
  146.4 1.6 copy-start.20
  146.4 1.7 copy-start.21
  146.4 2.1 copy-start.22
  146.4 3.9 %copy-start.2 = (bf16[192,1280]{1,0:T(8,128)(2,1)S(1)}, bf16[192,1280]{1,0:T(8,128)(2,1)}, u32[]{:S(2)}) copy-start(bf16[192,1280]{1,0:T(8,128)(2,1)} %shard_map.151.grad) | copy-start | bytes 1474564
  146.4 52.4 %collective-permute-start.20 = (bf16[4,272,448]{2,1,0:T(8,128)(2,1)}, bf16[4,272,448]{2,1,0:T(8,128)(2,1)}, u32[]{:S(2)}, u32[]{:S(2)}) collective-permute-start(bf16[4,272,448]{2,1,0:T(8,128)(2,1)} %get-tuple-element.60), channel_id=1, source_target_pairs={{0,32},{8,40},{16,48},{24,56},{32,64},{40,72},{48,80},{56,88},{64,... | collective-permute-start | bytes 2924552 | tf_op jit(solution)/shard_map/ppermute | solution.py:382
  148.6 1.7 collective-permute-start.9
  152.3 1.2 copy-start.1
  153.4 62.0 %all-to-all-start.2 = ((bf16[4,160,1280]{2,1,0:T(8,128)(2,1)}), bf16[4,160,1280]{2,1,0:T(8,128)(2,1)}, u32[]{:S(2)}, u32[]{:S(2)}) async-start(bf16[4,160,1280]{2,1,0:T(8,128)(2,1)} %bitcast.17), calls=%async_computation.2 | async-start | bytes 3276800 | tf_op jit(solution)/shard_map/all_to_all | solution.py:416
  157.8 51.0 %collective-permute-start.21 = (bf16[4,272,448]{2,1,0:T(8,128)(2,1)}, bf16[4,272,448]{2,1,0:T(8,128)(2,1)S(1)}, u32[]{:S(2)}, u32[]{:S(2)}) collective-permute-start(bf16[4,272,448]{2,1,0:T(8,128)(2,1)} %get-tuple-element.61), channel_id=1, source_target_pairs={{0,96},{8,104},{16,112},{24,120},{32,0},{40,8},{48,16},{56,24},{64... | collective-permute-start | bytes 2924552 | tf_op jit(solution)/shard_map/ppermute | solution.py:383
  160.4 48.4 %collective-permute-start.22 = (bf16[4,272,448]{2,1,0:T(8,128)(2,1)}, bf16[4,272,448]{2,1,0:T(8,128)(2,1)S(1)}, u32[]{:S(2)}, u32[]{:S(2)}) collective-permute-start(bf16[4,272,448]{2,1,0:T(8,128)(2,1)} %get-tuple-element.62), channel_id=1, source_target_pairs={{0,64},{8,72},{16,80},{24,88},{32,96},{40,104},{48,112},{56,120},{... | collective-permute-start | bytes 2924552 | tf_op jit(solution)/shard_map/ppermute | solution.py:381
  160.4 69.8 %collective-permute-start.14 = (bf16[4,272,448]{2,1,0:T(8,128)(2,1)}, bf16[4,272,448]{2,1,0:T(8,128)(2,1)}, u32[]{:S(2)}, u32[]{:S(2)}) collective-permute-start(bf16[4,272,448]{2,1,0:T(8,128)(2,1)} %copy-done.22), channel_id=1, source_target_pairs={{0,8},{8,16},{16,24},{24,0},{32,40},{40,48},{48,56},{56,32},{64,72... | collective-permute-start | bytes 2924552 | tf_op jit(solution)/shard_map/ppermute | solution.py:382
  161.0 70.1 %collective-permute-start.15 = (bf16[4,272,448]{2,1,0:T(8,128)(2,1)}, bf16[4,272,448]{2,1,0:T(8,128)(2,1)}, u32[]{:S(2)}, u32[]{:S(2)}) collective-permute-start(bf16[4,272,448]{2,1,0:T(8,128)(2,1)} %copy-done.21), channel_id=1, source_target_pairs={{0,24},{8,0},{16,8},{24,16},{32,56},{40,32},{48,40},{56,48},{64,88... | collective-permute-start | bytes 2924552 | tf_op jit(solution)/shard_map/ppermute | solution.py:383
  198.8 32.2 %collective-permute-start.16 = (bf16[4,272,448]{2,1,0:T(8,128)(2,1)}, bf16[4,272,448]{2,1,0:T(8,128)(2,1)}, u32[]{:S(2)}, u32[]{:S(2)}) collective-permute-start(bf16[4,272,448]{2,1,0:T(8,128)(2,1)} %copy-done.20), channel_id=1, source_target_pairs={{0,16},{8,24},{16,0},{24,8},{32,48},{40,56},{48,32},{56,40},{64,80... | collective-permute-start | bytes 2924552 | tf_op jit(solution)/shard_map/ppermute | solution.py:381
  208.8 1.2 copy-start.7
  214.9 23.9 %collective-permute-start.23 = (bf16[272,448]{1,0:T(8,128)(2,1)}, bf16[272,448]{1,0:T(8,128)(2,1)}, u32[]{:S(2)}, u32[]{:S(2)}) collective-permute-start(bf16[272,448]{1,0:T(8,128)(2,1)} %get-tuple-element.64), channel_id=1, source_target_pairs={{0,8},{8,16},{16,24},{24,0},{32,40},{40,48},{48,56},{56,32},{64,72... | collective-permute-start | bytes 731144 | tf_op jit(solution)/shard_map/ppermute | solution.py:382
  220.0 32.9 %all-to-all-start.3 = ((bf16[16,10,1280]{2,1,0:T(8,128)(2,1)}), bf16[16,10,1280]{2,1,0:T(8,128)(2,1)}, u32[]{:S(2)}, u32[]{:S(2)}) async-start(bf16[16,10,1280]{2,1,0:T(8,128)(2,1)} %reshape.115), calls=%async_computation.3 | async-start | bytes 1310720 | tf_op jit(solution)/shard_map/all_to_all | solution.py:480
  227.1 16.7 %collective-permute-start.24 = (bf16[272,448]{1,0:T(8,128)(2,1)}, bf16[272,448]{1,0:T(8,128)(2,1)S(1)}, u32[]{:S(2)}, u32[]{:S(2)}) collective-permute-start(bf16[272,448]{1,0:T(8,128)(2,1)} %copy-done.25), channel_id=1, source_target_pairs={{0,24},{8,0},{16,8},{24,16},{32,56},{40,32},{48,40},{56,48},{64,88... | collective-permute-start | bytes 731144 | tf_op jit(solution)/shard_map/ppermute | solution.py:383
  230.2 15.5 %collective-permute-start.25 = (bf16[272,448]{1,0:T(8,128)(2,1)}, bf16[272,448]{1,0:T(8,128)(2,1)S(1)}, u32[]{:S(2)}, u32[]{:S(2)}) collective-permute-start(bf16[272,448]{1,0:T(8,128)(2,1)} %copy-done.24), channel_id=1, source_target_pairs={{0,16},{8,24},{16,0},{24,8},{32,48},{40,56},{48,32},{56,40},{64,80... | collective-permute-start | bytes 731144 | tf_op jit(solution)/shard_map/ppermute | solution.py:381
  231.1 1.2 copy-start.6
  232.3 8.3 %copy-start.3 = (bf16[192,1280]{1,0:T(8,128)(2,1)S(1)}, bf16[192,1280]{1,0:T(8,128)(2,1)}, u32[]{:S(2)}) copy-start(bf16[192,1280]{1,0:T(8,128)(2,1)} %shard_map.151.grad) | copy-start | bytes 1474564
  235.6 10.9 %collective-permute-start.17 = (bf16[272,448]{1,0:T(8,128)(2,1)S(1)}, bf16[272,448]{1,0:T(8,128)(2,1)S(1)}, u32[]{:S(2)}, u32[]{:S(2)}) collective-permute-start(bf16[272,448]{1,0:T(8,128)(2,1)S(1)} %get-tuple-element.56), channel_id=1, source_target_pairs={{0,32},{8,40},{16,48},{24,56},{32,64},{40,72},{48,80},{56,88},{64,... | collective-permute-start | bytes 731144 | tf_op jit(solution)/shard_map/ppermute | solution.py:382
  237.1 11.9 %collective-permute-start.18 = (bf16[272,448]{1,0:T(8,128)(2,1)S(1)}, bf16[272,448]{1,0:T(8,128)(2,1)S(1)}, u32[]{:S(2)}, u32[]{:S(2)}) collective-permute-start(bf16[272,448]{1,0:T(8,128)(2,1)S(1)} %get-tuple-element.57), channel_id=1, source_target_pairs={{0,96},{8,104},{16,112},{24,120},{32,0},{40,8},{48,16},{56,24},{64... | collective-permute-start | bytes 731144 | tf_op jit(solution)/shard_map/ppermute | solution.py:383
  238.9 11.9 %collective-permute-start.19 = (bf16[272,448]{1,0:T(8,128)(2,1)S(1)}, bf16[272,448]{1,0:T(8,128)(2,1)S(1)}, u32[]{:S(2)}, u32[]{:S(2)}) collective-permute-start(bf16[272,448]{1,0:T(8,128)(2,1)S(1)} %get-tuple-element.58), channel_id=1, source_target_pairs={{0,64},{8,72},{16,80},{24,88},{32,96},{40,104},{48,112},{56,120},{... | collective-permute-start | bytes 731144 | tf_op jit(solution)/shard_map/ppermute | solution.py:381
  (14 other events, 11.3 us)

commit v2 on v1

v2 whole, which is shorter than its diff:
```python
import jax
import jax.numpy as jnp
from jax import lax
from jax.experimental import pallas as pl
from jax.experimental.pallas import tpu as pltpu
from jax.sharding import PartitionSpec as P

F32 = jnp.float32
BF16 = jnp.bfloat16
ZN, CN = 4, 2
YN, XN = 4, 4
TP = ZN * CN
PARAMS = pltpu.CompilerParams(vmem_limit_bytes=56 * 1024 * 1024)

CORE_SWAP = [(i, i ^ 1) for i in range(TP)]
Z_GROUPS = [[z * CN + c for z in range(ZN)] for c in range(CN)]


def z_shift(step):
    return [(z * CN + c, ((z + step) % ZN) * CN + c) for z in range(ZN) for c in range(CN)]


def x_shift(step):
    return [(y * XN + x, y * XN + (x + step) % XN) for y in range(YN) for x in range(XN)]


def y_shift(step):
    return [(y * XN + x, ((y + step) % YN) * XN + x) for y in range(YN) for x in range(XN)]


def gelu_parts(values):
    cumulative = 0.5 * (1.0 + lax.erf(values * 0.7071067811865476))
    density = jnp.exp(-0.5 * values * values) * 0.3989422804014327
    return values * cumulative, cumulative + values * density


def mm(a, b, ca=1, cb=0):
    return lax.dot_general(a, b, (((ca,), (cb,)), ((), ())), preferred_element_type=F32)


def iota(shape, dim):
    return lax.broadcasted_iota(jnp.int32, shape, dim)


def struct(shape, dtype):
    return jax.ShapeDtypeStruct(shape, dtype)


def whole(shape):
    return pl.BlockSpec(shape, lambda *_: (0,) * len(shape))


SMEM = pl.BlockSpec(memory_space=pltpu.SMEM)
VMEM = pl.BlockSpec(memory_space=pltpu.VMEM)


HINT = pl.CostEstimate(flops=1, bytes_accessed=1, transcendentals=0)
LONG = pl.CostEstimate(flops=40_000_000_000, bytes_accessed=100_000_000, transcendentals=1_000_000)


def parcel_kernel(ids, offsets, frames, owner, grad_t, out):
    out[...] = jnp.zeros_like(out)
    s = ids[4]
    row, col = iota((48, 384), 0), iota((48, 384), 1)
    picks, dests = [], []
    for k in range(8):
        group = s * 8 + k
        start = offsets[group] - s * 384
        count = lax.shift_right_logical(frames[group], 2)
        dests.append(lax.shift_right_logical(owner[group], 3))
        picks.append(jnp.where((row < count) & (col == row + start), 1.0, 0.0))
    tokens = mm(jnp.concatenate(picks).astype(BF16), grad_t[...], 1, 1).astype(BF16)
    for k in range(8):
        out[dests[k]] = tokens[k * 48 : k * 48 + 48]


def parcels_of(ids, offsets, frames, owner, grad_t):
    return pl.pallas_call(
        parcel_kernel,
        out_shape=struct((16, 48, 448), BF16),
        in_specs=[SMEM, SMEM, SMEM, SMEM, VMEM],
        out_specs=VMEM,
        compiler_params=PARAMS,
        cost_estimate=HINT,
    )(ids, offsets, frames, owner, grad_t)


def select_kernel(ids, owner, arrived, keep, give):
    s, c = ids[4], ids[3]
    row = iota((192, 128), 0)
    z = lax.shift_right_logical(row * 1366, 16)
    rest = row - z * 48
    slot = lax.shift_right_logical(rest * 10923, 16)
    six = rest - slot * 6
    group = iota((192, 128), 1)
    source = jnp.sum(
        jnp.where(owner[...] == s * 8 + slot, lax.shift_right_logical(group, 3), 0), axis=1, keepdims=True
    )
    column = iota((192, 768), 1)
    tokens = arrived[...].reshape(768, 448)
    base = source * 48 + z[:, :1] * 12 + six[:, :1]
    for out, core in ((keep, c), (give, 1 - c)):
        route = jnp.where(column == base + core * 6, 1.0, 0.0).astype(BF16)
        out[...] = mm(route, tokens).astype(BF16)


def select_of(ids, owner, arrived):
    return pl.pallas_call(
        select_kernel,
        out_shape=(struct((192, 448), BF16), struct((192, 448), BF16)),
        in_specs=[SMEM, VMEM, VMEM],
        out_specs=(VMEM, VMEM),
        compiler_params=PARAMS,
        cost_estimate=HINT,
    )(ids, owner.reshape(1, 128), arrived)


def pair_kernel(ids, keep, got, out):
    first = ids[3] == 0
    both = jnp.concatenate(
        [jnp.where(first, keep[...], got[...]), jnp.where(first, got[...], keep[...])], axis=1
    )
    for k in range(4):
        out[k] = both


def pair_of(ids, keep, got):
    return pl.pallas_call(
        pair_kernel,
        out_shape=struct((4, 192, 896), BF16),
        in_specs=[SMEM, VMEM, VMEM],
        out_specs=VMEM,
        compiler_params=PARAMS,
        cost_estimate=HINT,
    )(ids, keep, got)


def encode_kernel(context, residual, weight, gain, bias, stacked, normed, inverse, scratch):
    stream = residual[...].astype(F32) + mm(context[...], weight[...])
    centered = stream - jnp.mean(stream, axis=-1, keepdims=True)
    inv = lax.rsqrt(jnp.mean(centered * centered, axis=-1, keepdims=True) + 1e-05)
    norm = centered * inv
    normed[...] = norm
    inverse[...] = jnp.broadcast_to(inv, inverse.shape)
    encoded = norm * gain[...] + bias[...]
    for piece in range(10):
        scratch[piece] = encoded[:, piece * 128 : (piece + 1) * 128]
    for r in range(4):
        for piece in range(10):
            at = r * 1280 + piece * 128
            stacked[:, at : at + 128] = scratch[piece, pl.ds(r, 48, stride=4), :].astype(BF16)


def encode_of(context, residual, weight, gain, bias):
    return pl.pallas_call(
        encode_kernel,
        out_shape=(struct((48, 5120), BF16), struct((192, 1280), F32), struct((192, 128), F32)),
        in_specs=[VMEM] * 5,
        out_specs=(VMEM,) * 3,
        scratch_shapes=[pltpu.VMEM((10, 192, 128), F32)],
        compiler_params=PARAMS,
        cost_estimate=HINT,
    )(context, residual, weight, gain.reshape(1, 1280), bias.reshape(1, 1280))


def norm_back_kernel(rows, normed, inverse, gain, out, scratch):
    for r in range(4):
        for piece in range(10):
            at = r * 1280 + piece * 128
            total = rows[0, :, at : at + 128].astype(F32)
            for k in range(1, 4):
                total = total + rows[k, :, at : at + 128].astype(F32)
            scratch[piece, pl.ds(r, 48, stride=4), :] = total.astype(BF16).astype(F32)
    scaled = jnp.concatenate([scratch[piece] for piece in range(10)], axis=1) * gain[...]
    norm = normed[...]
    mean = jnp.mean(scaled, axis=-1, keepdims=True)
    along = jnp.mean(scaled * norm, axis=-1, keepdims=True)
    out[...] = (inverse[:, :1] * (scaled - mean - norm * along)).astype(BF16)


def norm_back_of(rows, normed, inverse, gain):
    return pl.pallas_call(
        norm_back_kernel,
        out_shape=struct((192, 1280), BF16),
        in_specs=[VMEM] * 4,
        out_specs=VMEM,
        scratch_shapes=[pltpu.VMEM((10, 192, 128), F32)],
        compiler_params=PARAMS,
        cost_estimate=LONG,
    )(rows, normed, inverse, gain.reshape(1, 1280))


def preact_kernel(ids, b0, b1, b2, b3, own_w, other_w, stk, hid_own, hid_other, slope_own, slope_other, acc, acc_other):
    i = pl.program_id(0)
    for step, block in enumerate((b0, b1, b2, b3)):
        at = pl.multiple_of(lax.rem(ids[2] + step, 4) * 48, 16)
        stk[pl.ds(at, 48), :] = block[...]

    @pl.when(i == 0)
    def _():
        acc[...] = jnp.zeros_like(acc)
        acc_other[...] = jnp.zeros_like(acc_other)

    rows = stk[...]
    acc[...] += mm(own_w[...], rows, 1, 1)
    acc_other[...] += mm(other_w[...], rows, 1, 1)

    @pl.when(i == pl.num_programs(0) - 1)
    def _():
        hidden, slope = gelu_parts(acc[...])
        hid_own[...] = hidden.astype(BF16)
        slope_own[...] = slope
        hidden, slope = gelu_parts(acc_other[...])
        hid_other[...] = hidden.astype(BF16)
        slope_other[...] = slope


def preact_of(ids, blocks, own_w, other_w):
    return pl.pallas_call(
        preact_kernel,
        out_shape=(
            struct((192, 5120), BF16),
            struct((448, 192), BF16),
            struct((448, 192), BF16),
            struct((448, 192), F32),
            struct((448, 192), F32),
        ),
        grid=(5,),
        in_specs=[SMEM]
        + [pl.BlockSpec((48, 1024), lambda i: (0, i))] * 4
        + [pl.BlockSpec((448, 1024), lambda i: (0, i))] * 2,
        out_specs=(pl.BlockSpec((192, 1024), lambda i: (0, i)),) + (whole((448, 192)),) * 4,
        scratch_shapes=[pltpu.VMEM((448, 192), F32)] * 2,
        compiler_params=PARAMS,
        cost_estimate=HINT,
    )(ids, *blocks, own_w, other_w)


def pre_grad_kernel(
    og, out_own, out_other, hid_other, slope_own, slope_other,
    pre_own, send, turned, turned_other, acc, acc_other,
):
    i = pl.program_id(0)

    @pl.when(i == 0)
    def _():
        acc[...] = jnp.zeros_like(acc)
        acc_other[...] = jnp.zeros_like(acc_other)

    piece = og[0]
    acc[...] += mm(out_own[...], piece, 1, 1)
    acc_other[...] += mm(out_other[...], piece, 1, 1)

    @pl.when(i == 3)
    def _():
        own = acc[...] * slope_own[...]
        other = acc_other[...] * slope_other[...]
        pre_own[...] = own.astype(BF16)
        send[0:448, :] = other.astype(BF16)
        send[448:896, :] = hid_other[...]
        turned[...] = own.T.astype(BF16)
        turned_other[...] = other.T.astype(BF16)


def pre_grad_of(og, out_own, out_other, hid_other, slope_own, slope_other):
    wide = pl.BlockSpec((448, 896), lambda i: (0, i))
    return pl.pallas_call(
        pre_grad_kernel,
        out_shape=(
            struct((448, 192), BF16),
            struct((896, 192), BF16),
            struct((192, 448), BF16),
            struct((192, 448), BF16),
        ),
        grid=(4,),
        in_specs=[pl.BlockSpec((1, 192, 896), lambda i: (i, 0, 0)), wide, wide] + [whole((448, 192))] * 3,
        out_specs=(whole((448, 192)), whole((896, 192)), whole((192, 448)), whole((192, 448))),
        scratch_shapes=[pltpu.VMEM((448, 192), F32)] * 2,
        compiler_params=PARAMS,
        cost_estimate=HINT,
    )(og, out_own, out_other, hid_other, slope_own, slope_other)


def row_kernel(pre, pre_other, in_own, in_other, out):
    out[...] = (mm(pre[...], in_own[...]) + mm(pre_other[...], in_other[...])).astype(BF16)


def rows_of(pre, pre_other, in_own, in_other):
    wide = pl.BlockSpec((448, 1280), lambda i: (0, i))
    return pl.pallas_call(
        row_kernel,
        out_shape=struct((192, 5120), BF16),
        grid=(4,),
        in_specs=[whole((192, 448))] * 2 + [wide] * 2,
        out_specs=pl.BlockSpec((192, 1280), lambda i: (0, i)),
        compiler_params=PARAMS,
        cost_estimate=HINT,
    )(pre, pre_other, in_own, in_other)


def x_columns(stk, og, x, out):
    for y in range(4):
        out[:, y * 320 : y * 320 + 320] = stk[:, (4 * y + x) * 320 : (4 * y + x + 1) * 320]
        out[:, 1280 + y * 224 : 1504 + y * 224] = og[y, :, x * 224 : x * 224 + 224]


def weight_grad_kernel(ids, stk, stk_other, og, og_other, pre, hid, recv, *outs):
    i = pl.program_id(0)
    x_first, y_first = outs[:5], outs[5:10]
    picked, picked_other = outs[10:]
    for x in range(4):

        @pl.when(i == x)
        def _(x=x):
            x_columns(stk, og, x, picked)
            x_columns(stk_other, og_other, x, picked_other)

    across = jnp.concatenate(
        [
            mm(pre[0:224], picked[:, 0:1280]) + mm(recv[0:224], picked_other[:, 0:1280]),
            mm(hid[0:224], picked[:, 1280:2176]) + mm(recv[448:672], picked_other[:, 1280:2176]),
        ],
        axis=1,
    ).astype(BF16)
    at = pl.ds(pl.multiple_of(i * 1280, 128), 1280)
    down = jnp.concatenate(
        [
            mm(pre[224:448], stk[:, at]) + mm(recv[224:448], stk_other[:, at]),
            mm(hid[224:448], og[i]) + mm(recv[672:896], og_other[i]),
        ],
        axis=1,
    ).astype(BF16)
    x_turn = lax.rem(i - ids[1] + 4, 4)
    y_turn = lax.rem(i - ids[0] + 4, 4)
    for turn, dests, value in ((x_turn, x_first, across), (y_turn, y_first, down)):
        for dest, k in ((0, 0), (1, 1), (2, 3)):

            @pl.when(turn == k)
            def _(dest=dests[dest], value=value):
                dest[...] = value

        @pl.when(turn == 2)
        def _(dests=dests, value=value):
            dests[3][...] = value[0:112]
            dests[4][...] = value[112:224]


def weight_grads_of(ids, stk, stk_other, og, og_other, pre, hid, recv):
    once = pl.Buffered(buffer_count=1)

    def single(shape):
        return pl.BlockSpec(shape, lambda *_: (0,) * len(shape), pipeline_mode=once)

    shapes = [(224, 2176)] * 3 + [(112, 2176)] * 2
    return pl.pallas_call(
        weight_grad_kernel,
        out_shape=tuple(struct(shape, BF16) for shape in shapes * 2),
        grid=(4,),
        in_specs=[SMEM]
        + [single((192, 5120))] * 2
        + [single((4, 192, 896))] * 2
        + [single((448, 192)), single((448, 192)), single((896, 192))],
        out_specs=tuple(single(shape) for shape in shapes * 2),
        scratch_shapes=[pltpu.VMEM((192, 2176), BF16)] * 2,
        compiler_params=PARAMS,
        cost_estimate=LONG,
    )(ids, stk, stk_other, og, og_other, pre, hid, recv)


def bump_kernel(x_up, x_down, y_up, y_down, a, b, c, d, *outs):
    for part, got, out in zip((x_up, x_down, y_up, y_down), (a, b, c, d), outs, strict=True):
        out[...] = (part[...].astype(F32) + got[...].astype(F32)).astype(BF16)


def bump_of(x_up, x_down, y_up, y_down, got):
    first = pl.BlockSpec((112, 2176), lambda i: (0, 0))
    second = pl.BlockSpec((112, 2176), lambda i: (1, 0))
    sides = [first, second, first, second]
    return pl.pallas_call(
        bump_kernel,
        out_shape=(struct((224, 2176), BF16),) * 4,
        grid=(1,),
        in_specs=sides + [first] * 4,
        out_specs=tuple(sides),
        input_output_aliases={0: 0, 1: 1, 2: 2, 3: 3},
        compiler_params=PARAMS,
        cost_estimate=HINT,
    )(x_up, x_down, y_up, y_down, *got)


def spread_kernel(where, a, b, c, *outs):
    value = (a[...].astype(F32) + b[...].astype(F32) + c[...].astype(F32)).astype(BF16)
    for n in range(4):
        piece = jnp.concatenate(
            [value[:, n * 320 : n * 320 + 320], value[:, 1280 + n * 224 : 1280 + n * 224 + 224]], axis=1
        )
        turn = lax.rem(n - where[0] + 4, 4)
        for k in range(4):

            @pl.when(turn == k)
            def _(k=k, piece=piece):
                outs[k][...] = piece


def spread_of(where, parts):
    return pl.pallas_call(
        spread_kernel,
        out_shape=(struct((224, 544), BF16),) * 4,
        in_specs=[SMEM] + [VMEM] * 3,
        out_specs=(VMEM,) * 4,
        compiler_params=PARAMS,
        cost_estimate=HINT,
    )(where, *parts)


def finish_kernel(a0, a1, a2, a3, b0, b1, b2, b3, grad_in, grad_out):
    first = a0[...].astype(F32) + a1[...].astype(F32) + a2[...].astype(F32) + a3[...].astype(F32)
    second = b0[...].astype(F32) + b1[...].astype(F32) + b2[...].astype(F32) + b3[...].astype(F32)
    both = jnp.concatenate([first, second], axis=0)
    grad_in[...] = both[:, 0:320].T.astype(BF16)
    grad_out[...] = both[:, 320:544].astype(BF16)


def finish_of(first, second):
    return pl.pallas_call(
        finish_kernel,
        out_shape=(struct((320, 448), BF16), struct((448, 224), BF16)),
        in_specs=[VMEM] * 8,
        out_specs=(VMEM, VMEM),
        compiler_params=PARAMS,
        cost_estimate=HINT,
    )(*first, *second)


def weight_sum_kernel(parts, out):
    total = parts[0].astype(F32)
    for k in range(1, 4):
        total = total + parts[k].astype(F32)
    out[...] = jnp.zeros_like(out)
    for n in range(16):
        out[n, 0:10, :] = total[n * 10 : n * 10 + 10].astype(BF16)


def weight_sum_of(parts):
    return pl.pallas_call(
        weight_sum_kernel,
        out_shape=struct((16, 16, 1280), BF16),
        in_specs=[VMEM],
        out_specs=VMEM,
        compiler_params=PARAMS,
        cost_estimate=HINT,
    )(parts)


def ring_of(parts, shift):
    far = lax.ppermute(parts[2], "seq", shift(2))
    up = lax.ppermute(parts[1], "seq", shift(1))
    down = lax.ppermute(parts[3], "seq", shift(-1))
    return (parts[0], up, down, far)


def order_kernel(target, context, out):
    pick = jnp.where(iota((1280, 256), 0) == target[...], 1.0, 0.0).astype(BF16)
    out[...] = mm(context[...], pick).astype(BF16)


def order_of(target, context):
    return pl.pallas_call(
        order_kernel,
        out_shape=struct((192, 1280), BF16),
        grid=(5,),
        in_specs=[pl.BlockSpec((1, 256), lambda i: (0, i)), whole((192, 1280))],
        out_specs=pl.BlockSpec((192, 256), lambda i: (0, i)),
        compiler_params=PARAMS,
        cost_estimate=LONG,
    )(target.reshape(1, 1280), context)


def out_weight_kernel(ctx, ctx_other, grad, grad_other, out):
    out[...] = (mm(ctx[...], grad[...], 0, 0) + mm(ctx_other[...], grad_other[...], 0, 0)).astype(BF16)


def out_weight_of(ctx, ctx_other, grad, grad_other):
    block = pl.BlockSpec((192, 128), lambda i: (0, i))
    return pl.pallas_call(
        out_weight_kernel,
        out_shape=struct((640, 1280), BF16),
        grid=(5,),
        in_specs=[block, block, whole((192, 1280)), whole((192, 1280))],
        out_specs=pl.BlockSpec((128, 1280), lambda i: (i, 0)),
        compiler_params=PARAMS,
        cost_estimate=HINT,
    )(ctx, ctx_other, grad, grad_other)


def swap(value):
    return lax.ppermute(value, "tp", CORE_SWAP)


def z_blocks(block):
    far = lax.ppermute(block, "tp", z_shift(2))
    behind = lax.ppermute(block, "tp", z_shift(1))
    ahead = lax.ppermute(block, "tp", z_shift(-1))
    return (block, ahead, far, behind)


def z_exchange(parts):
    return lax.all_to_all(parts, "tp", split_axis=0, concat_axis=0, axis_index_groups=Z_GROUPS, tiled=True)


def per_device(
    context,
    residual_in,
    out_weight,
    final_norm_weight,
    final_norm_bias,
    adapter_in,
    adapter_out,
    emb_grad,
    group_offsets,
    group_frames,
    group_owner,
):
    s = lax.axis_index("seq")
    t = lax.axis_index("tp")
    c = t % 2
    ids = jnp.stack([s // 4, s % 4, t // 2, c, s]).astype(jnp.int32)
    context = context.reshape(192, 1280)
    residual_in = residual_in.reshape(192, 1280)

    in_own = adapter_in.T
    in_other = swap(in_own)
    out_other = swap(adapter_out)

    parcels = parcels_of(ids, group_offsets, group_frames, group_owner, emb_grad.T)
    arrived = lax.all_to_all(parcels, "seq", split_axis=0, concat_axis=0, tiled=True)
    context, _ = lax.optimization_barrier((context, parcels))
    stacked_here, normed, inverse = encode_of(context, residual_in, out_weight, final_norm_weight, final_norm_bias)
    rows = z_blocks(stacked_here)
    arrived, in_other, out_other, _ = lax.optimization_barrier((arrived, in_other, out_other, stacked_here))

    keep, give = select_of(ids, group_owner, arrived)
    got = swap(give)
    grad_pair = pair_of(ids, keep, got)
    og = z_exchange(grad_pair)

    place = jnp.arange(1280, dtype=jnp.int32)
    core = (place // 640 + c) % 2
    target = (2 * ((place % 640) // 160) + core) * 10 + ((place % 160) // 10) * 80 + place % 10
    ordered = order_of(target, context)
    context_keep, context_got = ordered[:, :640], swap(ordered[:, 640:])

    rows, _ = lax.optimization_barrier((rows, grad_pair))
    stk, hid_own, hid_other, slope_own, slope_other = preact_of(ids, rows, in_own, in_other)
    stk_other = swap(stk)
    og, _ = lax.optimization_barrier((og, ordered))
    og_other = swap(og)
    pre_own, send, pre_rows, pre_rows_other = pre_grad_of(
        og, adapter_out, out_other, hid_other, slope_own, slope_other
    )
    recv = swap(send)
    row_part = rows_of(pre_rows, pre_rows_other, in_own, in_other)
    row_parts = z_exchange(row_part.reshape(4, 48, 5120))

    pre_own, _ = lax.optimization_barrier((pre_own, row_part))
    parts = weight_grads_of(ids, stk, stk_other, og, og_other, pre_own, hid_own, recv)
    x_here, x_up, x_down, x_far, x_far2 = parts[:5]
    y_here, y_up, y_down, y_far, y_far2 = parts[5:]
    got = (
        lax.ppermute(x_far, "seq", x_shift(1)),
        lax.ppermute(x_far2, "seq", x_shift(-1)),
        lax.ppermute(y_far, "seq", y_shift(1)),
        lax.ppermute(y_far2, "seq", y_shift(-1)),
    )
    row_parts, got = lax.optimization_barrier((row_parts, got))

    d_residual = norm_back_of(row_parts, normed, inverse, final_norm_weight)
    residual_other = swap(d_residual)
    weight_part = out_weight_of(context_keep, context_got, d_residual, residual_other)
    d_context = mm(d_residual, out_weight, 1, 1).astype(BF16)
    weight_parts, _ = lax.optimization_barrier((z_exchange(weight_part.reshape(4, 160, 1280)), d_context))
    weight_z = weight_sum_of(weight_parts)
    pieces = lax.all_to_all(weight_z, "seq", split_axis=0, concat_axis=0, tiled=True)
    d_out_weight = jnp.sum(pieces.astype(F32), axis=0)[:10]

    x_up, x_down, y_up, y_down = bump_of(x_up, x_down, y_up, y_down, got)
    x_sums = (x_here, lax.ppermute(x_up, "seq", x_shift(1)), lax.ppermute(x_down, "seq", x_shift(-1)))
    y_sums = (y_here, lax.ppermute(y_up, "seq", y_shift(1)), lax.ppermute(y_down, "seq", y_shift(-1)))
    first = ring_of(spread_of(ids[0:1], x_sums), y_shift)
    second = ring_of(spread_of(ids[1:2], y_sums), x_shift)
    grad_in, grad_out = finish_of(first, second)

    return (
        d_context.reshape(8, 24, 1280),
        d_residual.reshape(8, 24, 1280),
        d_out_weight,
        grad_in,
        grad_out,
    )


def solution(mesh):
    placed = (
        P("seq", "tp", None),
        P("seq", "tp", None),
        P(),
        P(),
        P(),
        P(None, "tp"),
        P("tp", None),
        P("seq", "tp"),
        P(),
        P(),
        P(),
    )
    return jax.shard_map(
        per_device,
        mesh=mesh,
        in_specs=placed,
        out_specs=(
            P("seq", "tp", None),
            P("seq", "tp", None),
            P(("seq", "tp"), None),
            P("seq", "tp"),
            P("tp", "seq"),
        ),
        check_vma=False,
    )
```

time: 256 us -> 192 us (0.75)
  waiting for transfers between devices: 84.7 us -> 41.7 us
  local copies, waits for them, and re-layouts: 36 us -> 7.94 us
  Pallas kernels: 55.7 us -> 78.4 us
  blocking collectives: 21.5 us -> 0 us
  starting transfers between devices: 46.1 us -> 58.4 us
  other arithmetic: 6.41 us -> 1.44 us
    ppermute x4 -> x2, waiting for transfers between devices: 35.9 us -> 0.36 us  [ring_of(): up = lax.ppermute(parts[1], 'seq', shift(1))]
    all_to_all x1 -> x0, blocking collectives: 21.5 us -> none  [per_device(): lax.all_to_all(parcels, 'seq', split_axis=0, concat_axis=0, tiled=True)]
    unnamed x68 -> x42, local copies, waits for them, and re-layouts: 26.2 us -> 5.35 us
    ppermute x0 -> x8, starting transfers between devices: none -> 13 us  [the longest x1 3 us: per_device(): lax.ppermute(x_down, 'seq', x_shift(-1))]
    pallas_call x4 -> x9, Pallas kernels: 35.3 us -> 48 us  [the longest x1 14.3 us: weight_grads_of(): pl.pallas_call(weight_grad_kernel, out_shape=tuple((struct(shape, BF16) f...]
    all_to_all x2 -> x3, waiting for transfers between devices: 24.8 us -> 14.7 us  [z_exchange(): lax.all_to_all(parts, 'tp', split_axis=0, concat_axis=0, axis_index_group...]
    ppermute x4 -> x2, waiting for transfers between devices: 12.8 us -> 4.34 us  [ring_of(): down = lax.ppermute(parts[3], 'seq', shift(-1))]
    ppermute x1 -> x0, local copies, waits for them, and re-layouts: 7.65 us -> none  [swap(): return lax.ppermute(value, 'tp', CORE_SWAP)]
  transfers between devices with their start and end apart: 29 -> 30, of which waited for: 12 -> 15; matrix products, arithmetic and copies ran while one was open for 11% -> 3% of each run, Pallas kernels for 22% -> 37%
where the time goes in v2:
time: 192 us; the launch traced here: 191 us
  Pallas kernels  78.4 us (41%)
  starting transfers between devices  58.4 us (30%)
  waiting for transfers between devices  41.7 us (22%)
  local copies, waits for them, and re-layouts  7.94 us (4%)
  matrix products  2.01 us (1%)
    all_to_all x3, waiting for transfers between devices, z_exchange(): lax.all_to_all(parts, 'tp', split_axis=0, concat_axis=0, axis_index_group...  14.7 us
    pallas_call x1, Pallas kernels, weight_grads_of(): pl.pallas_call(weight_grad_kernel, out_shape=tuple((struct(shape, BF16) f...  14.3 us
    all_to_all x3, starting transfers between devices, z_exchange(): lax.all_to_all(parts, 'tp', split_axis=0, concat_axis=0, axis_index_group...  13.7 us
    pallas_call x1, Pallas kernels, preact_of(): pl.pallas_call(preact_kernel, out_shape=(struct((192, 5120), BF16), struc...  9.22 us
    pallas_call x2, Pallas kernels, spread_of(): pl.pallas_call(spread_kernel, out_shape=(struct((224, 544), BF16),) * 4,...  7.64 us
    all_to_all x1, starting transfers between devices, per_device(): lax.all_to_all(parcels, 'seq', split_axis=0, concat_axis=0, tiled=True)  7.17 us
    pallas_call x1, Pallas kernels, pre_grad_of(): pl.pallas_call(pre_grad_kernel, out_shape=(struct((448, 192), BF16), stru...  7.02 us
    pallas_call x1, Pallas kernels, rows_of(): pl.pallas_call(row_kernel, out_shape=struct((192, 5120), BF16), grid=(4,)...  6.64 us
  transfers between devices with their start and end apart: 30, of which 15 were waited for; matrix products, arithmetic and copies ran while one was open for 3% of the time, Pallas kernels for 37%

profile of v2, /device:TPU:0, one launch (start us, length us, event | category | flops | bytes accessed | tf_op | source)
XLA Modules:
  0.0 190.6 jit_solution(4247496022960781520)
XLA Ops:
  1.9 2.4 %shard_map.146 = bf16[16,48,448]{2,1,0:T(8,128)(2,1)} custom-call(s32[5]{0:T(128)} %stack.23.ids, s32[128]{0:T(128)} %offsets.1, s32[128]{0:T(128)} %frames.1, s32[128]{0:T(128)} %owner.1, bf16[448,384]{1,0:T(8,128)(2,1)} %bitcast.27), custom_call_target="tpu_custom_call" | custom-call | flops 1 | bytes 1 | tf_op jit(solution)/shard_map/pallas_call | solution.py:78
  4.3 7.2 %all-to-all-start = ((bf16[16,48,448]{2,1,0:T(8,128)(2,1)}), bf16[16,48,448]{2,1,0:T(8,128)(2,1)}, u32[]{:S(2)}, u32[]{:S(2)}) async-start(bf16[16,48,448]{2,1,0:T(8,128)(2,1)} %shard_map.146), calls=%async_computation | async-start | bytes 1572864 | tf_op jit(solution)/shard_map/all_to_all | solution.py:536
  12.6 4.7 %shard_map.147 = (bf16[48,5120]{1,0:T(8,128)(2,1)}, f32[192,1280]{1,0:T(8,128)}, f32[192,128]{1,0:T(8,128)}) custom-call(bf16[192,1280]{1,0:T(8,128)(2,1)} %bitcast.24, bf16[192,1280]{1,0:T(8,128)(2,1)} %bitcast.23, bf16[1280,1280]{1,0:T(8,128)(2,1)} %weight.1, f32[1,1280]{1,0:T(1,128)} %reshape.232.gain, f32[1,1280]{1,0:T(1,128)} %reshape.233.bias), custom_call_target="tpu_custom_call" | custom-call | flops 1 | bytes 1 | tf_op jit(solution)/shard_map/pallas_call | solution.py:155
  17.3 1.9 %collective-permute-start.5 = (bf16[48,5120]{1,0:T(8,128)(2,1)}, bf16[48,5120]{1,0:T(8,128)(2,1)}, u32[]{:S(2)}, u32[]{:S(2)}) collective-permute-start(bf16[48,5120]{1,0:T(8,128)(2,1)} %get-tuple-element.66.b0), channel_id=1, source_target_pairs={{0,2},{1,3},{2,4},{3,5},{4,6},{5,7},{6,0},{7,1},{8,10},{9,11},{10,... | collective-permute-start | bytes 1474568 | tf_op jit(solution)/shard_map/ppermute | solution.py:502
  19.2 3.6 %collective-permute-start.4 = (bf16[48,5120]{1,0:T(8,128)(2,1)}, bf16[48,5120]{1,0:T(8,128)(2,1)}, u32[]{:S(2)}, u32[]{:S(2)}) collective-permute-start(bf16[48,5120]{1,0:T(8,128)(2,1)} %get-tuple-element.66.b0), channel_id=1, source_target_pairs={{0,4},{1,5},{2,6},{3,7},{4,0},{5,1},{6,2},{7,3},{8,12},{9,13},{10,... | collective-permute-start | bytes 1474568 | tf_op jit(solution)/shard_map/ppermute | solution.py:501
  23.8 2.3 %all-to-all-done.arrived = bf16[16,48,448]{2,1,0:T(8,128)(2,1)} async-done(((bf16[16,48,448]{2,1,0:T(8,128)(2,1)}), bf16[16,48,448]{2,1,0:T(8,128)(2,1)}, u32[]{:S(2)}, u32[]{:S(2)}) %all-to-all-start) | async-done | bytes 688160 | tf_op jit(solution)/shard_map/all_to_all | solution.py:536
  26.1 3.1 %shard_map.148 = (bf16[192,448]{1,0:T(8,128)(2,1)}, bf16[192,448]{1,0:T(8,128)(2,1)}) custom-call(s32[5]{0:T(128)} %stack.23.ids, s32[1,128]{1,0:T(1,128)} %bitcast.29, bf16[16,48,448]{2,1,0:T(8,128)(2,1)} %all-to-all-done.arrived), custom_call_target="tpu_custom_call" | custom-call | flops 1 | bytes 1 | tf_op jit(solution)/shard_map/pallas_call | solution.py:108
  31.5 2.3 %shard_map.149 = bf16[4,192,896]{2,1,0:T(8,128)(2,1)} custom-call(s32[5]{0:T(128)} %stack.23.ids, bf16[192,448]{1,0:T(8,128)(2,1)} %get-tuple-element.62.keep, bf16[192,448]{1,0:T(8,128)(2,1)} %copy-done.18), custom_call_target="tpu_custom_call" | custom-call | flops 1 | bytes 1 | tf_op jit(solution)/shard_map/pallas_call | solution.py:128
  33.9 5.3 %all-to-all-start.1 = ((bf16[4,192,896]{2,1,0:T(8,128)(2,1)}), bf16[4,192,896]{2,1,0:T(8,128)(2,1)S(1)}, u32[]{:S(2)}, u32[]{:S(2)}) async-start(bf16[4,192,896]{2,1,0:T(8,128)(2,1)} %shard_map.149), calls=%async_computation.1 | async-start | bytes 2752512 | tf_op jit(solution)/shard_map/all_to_all | solution.py:508
  39.2 6.4 %collective-permute-done.4.b2 = bf16[48,5120]{1,0:T(8,128)(2,1)} collective-permute-done((bf16[48,5120]{1,0:T(8,128)(2,1)}, bf16[48,5120]{1,0:T(8,128)(2,1)}, u32[]{:S(2)}, u32[]{:S(2)}) %collective-permute-start.4) | collective-permute-done | bytes 491552 | tf_op jit(solution)/shard_map/ppermute | solution.py:501
  45.6 9.2 %shard_map.151 = (bf16[192,5120]{1,0:T(8,128)(2,1)}, bf16[448,192]{1,0:T(8,128)(2,1)}, bf16[448,192]{1,0:T(8,128)(2,1)}, f32[448,192]{1,0:T(8,128)}, f32[448,192]{1,0:T(8,128)}) custom-call(s32[5]{0:T(128)} %stack.23.ids, bf16[48,5120]{1,0:T(8,128)(2,1)} %get-tuple-element.66.b0, bf16[48,5120]{1,0:T(8,128)(2,1)} %collective-permute-done.3.b1, ...), custom_call_target="tpu_custom_call" | custom-call | flops 1 | bytes 1 | tf_op jit(solution)/shard_map/pallas_call | solution.py:219
  54.9 4.0 %shard_map.150 = bf16[192,1280]{1,0:T(8,128)(2,1)} custom-call(s32[1,1280]{1,0:T(1,128)} %fusion.1.target, bf16[192,1280]{1,0:T(8,128)(2,1)} %bitcast.25), custom_call_target="tpu_custom_call" | custom-call | flops 40000000000 | bytes 100000000 | tf_op jit(solution)/shard_map/pallas_call | solution.py:468
  60.4 7.0 %shard_map.152 = (bf16[448,192]{1,0:T(8,128)(2,1)}, bf16[896,192]{1,0:T(8,128)(2,1)}, bf16[192,448]{1,0:T(8,128)(2,1)}, bf16[192,448]{1,0:T(8,128)(2,1)}) custom-call(bf16[4,192,896]{2,1,0:T(8,128)(2,1)} %copy-done.2, bf16[448,3584]{1,0:T(8,128)(2,1)} %out_own.1, bf16[448,3584]{1,0:T(8,128)(2,1)} %copy-done.3, bf16[448,192]{1,0:T(8,128)(2,1)} %get-tuple-element.71.hid_other, ...), custom_call_target="tpu_custom_call" | custom-call | flops 1 | bytes 1 | tf_op jit(solution)/shard_map/pallas_call | solution.py:267
  67.6 6.6 %shard_map.153 = bf16[192,5120]{1,0:T(8,128)(2,1)} custom-call(bf16[192,448]{1,0:T(8,128)(2,1)} %get-tuple-element.74.pre, bf16[192,448]{1,0:T(8,128)(2,1)} %get-tuple-element.75.pre_other, bf16[448,5120]{1,0:T(8,128)(2,1)} %bitcast.19, bf16[448,5120]{1,0:T(8,128)(2,1)} %collective-permute-done.other_w.in_other), custom_call_target="tpu_custom_call" | custom-call | flops 1 | bytes 1 | tf_op jit(solution)/shard_map/pallas_call | solution.py:290
  74.2 3.9 %all-to-all-start.2 = ((bf16[4,48,5120]{2,1,0:T(8,128)(2,1)}), bf16[4,48,5120]{2,1,0:T(8,128)(2,1)S(1)}, u32[]{:S(2)}, u32[]{:S(2)}) async-start(bf16[4,48,5120]{2,1,0:T(8,128)(2,1)} %bitcast.20), calls=%async_computation.2 | async-start | bytes 3932160 | tf_op jit(solution)/shard_map/all_to_all | solution.py:508
  78.1 14.3 %shard_map.154 = (bf16[224,2176]{1,0:T(8,128)(2,1)}, bf16[224,2176]{1,0:T(8,128)(2,1)}, bf16[224,2176]{1,0:T(8,128)(2,1)}, bf16[112,2176]{1,0:T(8,128)(2,1)}, bf...) custom-call(s32[5]{0:T(128)} %stack.23.ids, ...), custom_call_target="tpu_custom_call" | custom-call | flops 40000000000 | bytes 100000000 | tf_op jit(solution)/shard_map/pallas_call | solution.py:355
  92.4 1.9 %collective-permute-start.9 = (bf16[112,2176]{1,0:T(8,128)(2,1)}, bf16[112,2176]{1,0:T(8,128)(2,1)S(1)}, u32[]{:S(2)}, u32[]{:S(2)}) collective-permute-start(bf16[112,2176]{1,0:T(8,128)(2,1)} %get-tuple-element.81), channel_id=1, source_target_pairs={{0,8},{8,16},{16,24},{24,0},{32,40},{40,48},{48,56},{56,32},{64,72... | collective-permute-start | bytes 1462280 | tf_op jit(solution)/shard_map/ppermute | solution.py:570
  94.3 1.3 collective-permute-start.10
  95.7 1.9 collective-permute-start.11
  97.6 1.3 collective-permute-start.12
  98.9 4.6 %all-to-all-done.2.rows = bf16[4,48,5120]{2,1,0:T(8,128)(2,1)S(1)} async-done(((bf16[4,48,5120]{2,1,0:T(8,128)(2,1)}), bf16[4,48,5120]{2,1,0:T(8,128)(2,1)S(1)}, u32[]{:S(2)}, u32[]{:S(2)}) %all-to-all-start.2) | async-done | bytes 1966112 | tf_op jit(solution)/shard_map/all_to_all | solution.py:508
  103.5 3.5 %collective-permute-done.9.a = bf16[112,2176]{1,0:T(8,128)(2,1)S(1)} collective-permute-done((bf16[112,2176]{1,0:T(8,128)(2,1)}, bf16[112,2176]{1,0:T(8,128)(2,1)S(1)}, u32[]{:S(2)}, u32[]{:S(2)}) %collective-permute-start.9) | collective-permute-done | bytes 487456 | tf_op jit(solution)/shard_map/ppermute | solution.py:570
  107.2 2.6 %collective-permute-done.11.c = bf16[112,2176]{1,0:T(8,128)(2,1)} collective-permute-done((bf16[112,2176]{1,0:T(8,128)(2,1)}, bf16[112,2176]{1,0:T(8,128)(2,1)}, u32[]{:S(2)}, u32[]{:S(2)}) %collective-permute-start.11) | collective-permute-done | bytes 487456 | tf_op jit(solution)/shard_map/ppermute | solution.py:572
  110.0 3.4 %shard_map.155.grad = bf16[192,1280]{1,0:T(8,128)(2,1)} custom-call(bf16[4,48,5120]{2,1,0:T(8,128)(2,1)} %copy-done.4, f32[192,1280]{1,0:T(8,128)} %get-tuple-element.86.normed, f32[192,128]{1,0:T(8,128)} %get-tuple-element.87.inverse, f32[1,1280]{1,0:T(1,128)} %reshape.232.gain), custom_call_target="tpu_custom_call" | custom-call | flops 40000000000 | bytes 100000000 | tf_op jit(solution)/shard_map/pallas_call | solution.py:182
  114.7 1.1 collective-permute-done.13.ctx_other
  116.7 5.0 %shard_map.156 = bf16[640,1280]{1,0:T(8,128)(2,1)} custom-call(bf16[192,640]{1,0:T(8,128)(2,1)} %get-tuple-element.114.ctx, bf16[192,640]{1,0:T(8,128)(2,1)} %copy-done.17, bf16[192,1280]{1,0:T(8,128)(2,1)} %shard_map.155.grad, bf16[192,1280]{1,0:T(8,128)(2,1)} %copy-done.8), custom_call_target="tpu_custom_call" | custom-call | flops 1 | bytes 1 | tf_op jit(solution)/shard_map/pallas_call | solution.py:485
  121.7 4.5 %all-to-all-start.3 = ((bf16[4,160,1280]{2,1,0:T(8,128)(2,1)}), bf16[4,160,1280]{2,1,0:T(8,128)(2,1)S(1)}, u32[]{:S(2)}, u32[]{:S(2)}) async-start(bf16[4,160,1280]{2,1,0:T(8,128)(2,1)} %bitcast.21), calls=%async_computation.3 | async-start | bytes 3276800 | tf_op jit(solution)/shard_map/all_to_all | solution.py:508
  126.2 3.6 %shard_map.158 = (bf16[224,2176]{1,0:T(8,128)(2,1)}, bf16[224,2176]{1,0:T(8,128)(2,1)}, bf16[224,2176]{1,0:T(8,128)(2,1)}, bf16[224,2176]{1,0:T(8,128)(2,1)}) custom-call(bf16[224,2176]{1,0:T(8,128)(2,1)} %get-tuple-element.90.x_up, ...), custom_call_target="tpu_custom_call", output_to_operand_aliasing={{0}: (0, {}), {1}: (1, {}), {2}: (2, {}), {3}: (3, {})} | custom-call | flops 1 | bytes 1 | tf_op jit(solution)/shard_map/pallas_call | solution.py:379
  130.0 3.0 %collective-permute-start.16 = (bf16[224,2176]{1,0:T(8,128)(2,1)}, bf16[224,2176]{1,0:T(8,128)(2,1)}, u32[]{:S(2)}, u32[]{:S(2)}) collective-permute-start(bf16[224,2176]{1,0:T(8,128)(2,1)} %get-tuple-element.99), channel_id=1, source_target_pairs={{0,24},{8,0},{16,8},{24,16},{32,56},{40,32},{48,40},{56,48},{64,88... | collective-permute-start | bytes 2924552 | tf_op jit(solution)/shard_map/ppermute | solution.py:587
  133.0 1.5 collective-permute-start.20
  134.5 1.8 collective-permute-start.21
  136.3 2.0 %convolution_convert_fusion = bf16[192,1280]{1,0:T(8,128)(2,1)} fusion(bf16[192,1280]{1,0:T(8,128)(2,1)S(1)} %copy-done.5, bf16[1280,1280]{1,0:T(8,128)(2,1)S(1)} %copy-done), kind=kOutput, calls=%fused_computation | convolution fusion | flops 629391360 | bytes 4259840 | tf_op jit(solution)/shard_map/dot_general | solution.py:38
  138.3 9.8 %all-to-all-done.3.parts = bf16[4,160,1280]{2,1,0:T(8,128)(2,1)S(1)} async-done(((bf16[4,160,1280]{2,1,0:T(8,128)(2,1)}), bf16[4,160,1280]{2,1,0:T(8,128)(2,1)S(1)}, u32[]{:S(2)}, u32[]{:S(2)}) %all-to-all-start.3) | async-done | bytes 1638432 | tf_op jit(solution)/shard_map/all_to_all | solution.py:508
  148.1 1.2 copy-done.1
  149.3 2.5 %shard_map.157 = bf16[16,16,1280]{2,1,0:T(8,128)(2,1)} custom-call(bf16[4,160,1280]{2,1,0:T(8,128)(2,1)} %copy-done.1), custom_call_target="tpu_custom_call" | custom-call | flops 1 | bytes 1 | tf_op jit(solution)/shard_map/pallas_call | solution.py:445
  151.8 5.5 %all-to-all-start.4 = ((bf16[16,16,1280]{2,1,0:T(8,128)(2,1)}), bf16[16,16,1280]{2,1,0:T(8,128)(2,1)S(1)}, u32[]{:S(2)}, u32[]{:S(2)}) async-start(bf16[16,16,1280]{2,1,0:T(8,128)(2,1)} %shard_map.157), calls=%async_computation.4 | async-start | bytes 1310720 | tf_op jit(solution)/shard_map/all_to_all | solution.py:583
  157.4 3.8 %shard_map.159 = (bf16[224,544]{1,0:T(8,128)(2,1)}, bf16[224,544]{1,0:T(8,128)(2,1)}, bf16[224,544]{1,0:T(8,128)(2,1)}, bf16[224,544]{1,0:T(8,128)(2,1)}) custom-call(s32[1]{0:T(128)} %bitcast.where, bf16[224,2176]{1,0:T(8,128)(2,1)} %get-tuple-element.89.a, bf16[224,2176]{1,0:T(8,128)(2,1)} %collective-permute-done.15.b, ...), custom_call_target="tpu_custom_call" | custom-call | flops 1 | bytes 1 | tf_op jit(solution)/shard_map/pallas_call | solution.py:406
  161.2 1.9 %collective-permute-start.17 = (bf16[224,544]{1,0:T(8,128)(2,1)}, bf16[224,544]{1,0:T(8,128)(2,1)S(1)}, u32[]{:S(2)}, u32[]{:S(2)}) collective-permute-start(bf16[224,544]{1,0:T(8,128)(2,1)} %get-tuple-element.101), channel_id=1, source_target_pairs={{0,32},{8,40},{16,48},{24,56},{32,64},{40,72},{48,80},{56,88},{64,... | collective-permute-start | bytes 731144 | tf_op jit(solution)/shard_map/ppermute | solution.py:457
  163.1 1.3 collective-permute-start.18
  164.4 2.2 %collective-permute-start.19 = (bf16[224,544]{1,0:T(8,128)(2,1)}, bf16[224,544]{1,0:T(8,128)(2,1)S(1)}, u32[]{:S(2)}, u32[]{:S(2)}) collective-permute-start(bf16[224,544]{1,0:T(8,128)(2,1)} %get-tuple-element.103), channel_id=1, source_target_pairs={{0,64},{8,72},{16,80},{24,88},{32,96},{40,104},{48,112},{56,120},{... | collective-permute-start | bytes 731144 | tf_op jit(solution)/shard_map/ppermute | solution.py:456
  167.6 3.8 %shard_map.160 = (bf16[224,544]{1,0:T(8,128)(2,1)}, bf16[224,544]{1,0:T(8,128)(2,1)}, bf16[224,544]{1,0:T(8,128)(2,1)}, bf16[224,544]{1,0:T(8,128)(2,1)}) custom-call(s32[1]{0:T(128)} %bitcast.1.where, bf16[224,2176]{1,0:T(8,128)(2,1)} %get-tuple-element.104.a, bf16[224,2176]{1,0:T(8,128)(2,1)} %copy-done.6, bf16[224,2176]{1,0:T(8,128)(2,1)} %collective-permute-done.21.c), custom_call_target="tpu_custom_call" | custom-call | flops 1 | bytes 1 | tf_op jit(solution)/shard_map/pallas_call | solution.py:406
  171.4 1.5 collective-permute-start.22
  172.9 1.8 collective-permute-start.23
  175.0 2.3 %collective-permute-start.24 = (bf16[224,544]{1,0:T(8,128)(2,1)}, bf16[224,544]{1,0:T(8,128)(2,1)S(1)}, u32[]{:S(2)}, u32[]{:S(2)}) collective-permute-start(bf16[224,544]{1,0:T(8,128)(2,1)} %get-tuple-element.110), channel_id=1, source_target_pairs={{0,16},{8,24},{16,0},{24,8},{32,48},{40,56},{48,32},{56,40},{64,80... | collective-permute-start | bytes 731144 | tf_op jit(solution)/shard_map/ppermute | solution.py:456
  177.3 3.7 %collective-permute-done.19.a3 = bf16[224,544]{1,0:T(8,128)(2,1)S(1)} collective-permute-done((bf16[224,544]{1,0:T(8,128)(2,1)}, bf16[224,544]{1,0:T(8,128)(2,1)S(1)}, u32[]{:S(2)}, u32[]{:S(2)}) %collective-permute-start.19) | collective-permute-done | bytes 243744 | tf_op jit(solution)/shard_map/ppermute | solution.py:456
  181.0 4.3 %collective-permute-done.23.b2 = bf16[224,544]{1,0:T(8,128)(2,1)S(1)} collective-permute-done((bf16[224,544]{1,0:T(8,128)(2,1)}, bf16[224,544]{1,0:T(8,128)(2,1)S(1)}, u32[]{:S(2)}, u32[]{:S(2)}) %collective-permute-start.23) | collective-permute-done | bytes 243744 | tf_op jit(solution)/shard_map/ppermute | solution.py:458
  185.3 1.2 collective-permute-done.24.b3
  187.2 2.7 %shard_map.161 = (bf16[320,448]{1,0:T(8,128)(2,1)}, bf16[448,224]{1,0:T(8,128)(2,1)}) custom-call(bf16[224,544]{1,0:T(8,128)(2,1)} %get-tuple-element.100.a0, bf16[224,544]{1,0:T(8,128)(2,1)} %copy-done.11, bf16[224,544]{1,0:T(8,128)(2,1)} %copy-done.12, bf16[224,544]{1,0:T(8,128)(2,1)} %copy-done.13, bf16[224,544]{1,0:T(8,128)(2,1)} %get-tuple-element.107.b0, ...), custom_call_target="tpu_custom_call" | custom-call | flops 1 | bytes 1 | tf_op jit(solution)/shard_map/pallas_call | solution.py:425
  (77 shorter events, 13.0 us)
Async XLA Ops:
  0.6 10.8 %copy-start.19 = (f32[1280]{0:T(1024)S(1)}, f32[1280]{0:T(1024)}, u32[]{:S(2)}) copy-start(f32[1280]{0:T(1024)} %param.14) | copy-start | bytes 15364
  0.6 11.4 %copy-start.20 = (f32[1280]{0:T(1024)S(1)}, f32[1280]{0:T(1024)}, u32[]{:S(2)}) copy-start(f32[1280]{0:T(1024)} %param.15) | copy-start | bytes 15364
  0.7 25.5 %collective-permute-start = (bf16[448,5120]{1,0:T(8,128)(2,1)}, bf16[448,5120]{1,0:T(8,128)(2,1)}, u32[]{:S(2)}, u32[]{:S(2)}) collective-permute-start(bf16[448,5120]{1,0:T(8,128)(2,1)} %bitcast.17), channel_id=1, source_target_pairs={{0,1},{1,0},{2,3},{3,2},{4,5},{5,4},{6,7},{7,6},{8,9},{9,8},{10,11... | collective-permute-start | bytes 13762568 | tf_op jit(solution)/shard_map/ppermute | solution.py:497
  0.7 25.4 %collective-permute-start.1 = (bf16[448,3584]{1,0:T(8,128)(2,1)}, bf16[448,3584]{1,0:T(8,128)(2,1)S(1)}, u32[]{:S(2)}, u32[]{:S(2)}) collective-permute-start(bf16[448,3584]{1,0:T(8,128)(2,1)} %out_own.1), channel_id=1, source_target_pairs={{0,1},{1,0},{2,3},{3,2},{4,5},{5,4},{6,7},{7,6},{8,9},{9,8},{10,11... | collective-permute-start | bytes 9633800 | tf_op jit(solution)/shard_map/ppermute | solution.py:497
  4.3 21.9 %all-to-all-start = ((bf16[16,48,448]{2,1,0:T(8,128)(2,1)}), bf16[16,48,448]{2,1,0:T(8,128)(2,1)}, u32[]{:S(2)}, u32[]{:S(2)}) async-start(bf16[16,48,448]{2,1,0:T(8,128)(2,1)} %shard_map.146), calls=%async_computation | async-start | bytes 1572864 | tf_op jit(solution)/shard_map/all_to_all | solution.py:536
  17.3 21.9 %collective-permute-start.5 = (bf16[48,5120]{1,0:T(8,128)(2,1)}, bf16[48,5120]{1,0:T(8,128)(2,1)}, u32[]{:S(2)}, u32[]{:S(2)}) collective-permute-start(bf16[48,5120]{1,0:T(8,128)(2,1)} %get-tuple-element.66.b0), channel_id=1, source_target_pairs={{0,2},{1,3},{2,4},{3,5},{4,6},{5,7},{6,0},{7,1},{8,10},{9,11},{10,... | collective-permute-start | bytes 1474568 | tf_op jit(solution)/shard_map/ppermute | solution.py:502
  19.2 26.4 %collective-permute-start.4 = (bf16[48,5120]{1,0:T(8,128)(2,1)}, bf16[48,5120]{1,0:T(8,128)(2,1)}, u32[]{:S(2)}, u32[]{:S(2)}) collective-permute-start(bf16[48,5120]{1,0:T(8,128)(2,1)} %get-tuple-element.66.b0), channel_id=1, source_target_pairs={{0,4},{1,5},{2,6},{3,7},{4,0},{5,1},{6,2},{7,3},{8,12},{9,13},{10,... | collective-permute-start | bytes 1474568 | tf_op jit(solution)/shard_map/ppermute | solution.py:501
  22.8 22.8 %collective-permute-start.3 = (bf16[48,5120]{1,0:T(8,128)(2,1)}, bf16[48,5120]{1,0:T(8,128)(2,1)}, u32[]{:S(2)}, u32[]{:S(2)}) collective-permute-start(bf16[48,5120]{1,0:T(8,128)(2,1)} %get-tuple-element.66.b0), channel_id=1, source_target_pairs={{0,6},{1,7},{2,0},{3,1},{4,2},{5,3},{6,4},{7,5},{8,14},{9,15},{10,... | collective-permute-start | bytes 1474568 | tf_op jit(solution)/shard_map/ppermute | solution.py:503
  26.1 7.8 %copy-start.3 = (bf16[448,3584]{1,0:T(8,128)(2,1)}, bf16[448,3584]{1,0:T(8,128)(2,1)S(1)}, u32[]{:S(2)}) copy-start(bf16[448,3584]{1,0:T(8,128)(2,1)S(1)} %collective-permute-done.1.out_other) | copy-start | bytes 9633796
  29.2 1.7 collective-permute-start.2
  33.9 25.3 %all-to-all-start.1 = ((bf16[4,192,896]{2,1,0:T(8,128)(2,1)}), bf16[4,192,896]{2,1,0:T(8,128)(2,1)S(1)}, u32[]{:S(2)}, u32[]{:S(2)}) async-start(bf16[4,192,896]{2,1,0:T(8,128)(2,1)} %shard_map.149), calls=%async_computation.1 | async-start | bytes 2752512 | tf_op jit(solution)/shard_map/all_to_all | solution.py:508
  54.8 23.3 %collective-permute-start.6 = (bf16[192,5120]{1,0:T(8,128)(2,1)}, bf16[192,5120]{1,0:T(8,128)(2,1)}, u32[]{:S(2)}, u32[]{:S(2)}) collective-permute-start(bf16[192,5120]{1,0:T(8,128)(2,1)} %get-tuple-element.76.stk), channel_id=1, source_target_pairs={{0,1},{1,0},{2,3},{3,2},{4,5},{5,4},{6,7},{7,6},{8,9},{9,8},{10,11... | collective-permute-start | bytes 5898248 | tf_op jit(solution)/shard_map/ppermute | solution.py:497
  59.2 1.2 copy-start.2
  59.2 18.9 %collective-permute-start.7 = (bf16[4,192,896]{2,1,0:T(8,128)(2,1)S(1)}, bf16[4,192,896]{2,1,0:T(8,128)(2,1)}, u32[]{:S(2)}, u32[]{:S(2)}) collective-permute-start(bf16[4,192,896]{2,1,0:T(8,128)(2,1)S(1)} %all-to-all-done.1.og), channel_id=1, source_target_pairs={{0,1},{1,0},{2,3},{3,2},{4,5},{5,4},{6,7},{7,6},{8,9},{9,8},{10,11... | collective-permute-start | bytes 4128776 | tf_op jit(solution)/shard_map/ppermute | solution.py:497
  67.4 10.7 %collective-permute-start.8 = (bf16[896,192]{1,0:T(8,128)(2,1)}, bf16[896,192]{1,0:T(8,128)(2,1)}, u32[]{:S(2)}, u32[]{:S(2)}) collective-permute-start(bf16[896,192]{1,0:T(8,128)(2,1)} %get-tuple-element.80), channel_id=1, source_target_pairs={{0,1},{1,0},{2,3},{3,2},{4,5},{5,4},{6,7},{7,6},{8,9},{9,8},{10,11... | collective-permute-start | bytes 1032200 | tf_op jit(solution)/shard_map/ppermute | solution.py:497
  74.2 29.3 %all-to-all-start.2 = ((bf16[4,48,5120]{2,1,0:T(8,128)(2,1)}), bf16[4,48,5120]{2,1,0:T(8,128)(2,1)S(1)}, u32[]{:S(2)}, u32[]{:S(2)}) async-start(bf16[4,48,5120]{2,1,0:T(8,128)(2,1)} %bitcast.20), calls=%async_computation.2 | async-start | bytes 3932160 | tf_op jit(solution)/shard_map/all_to_all | solution.py:508
  92.4 14.6 %collective-permute-start.9 = (bf16[112,2176]{1,0:T(8,128)(2,1)}, bf16[112,2176]{1,0:T(8,128)(2,1)S(1)}, u32[]{:S(2)}, u32[]{:S(2)}) collective-permute-start(bf16[112,2176]{1,0:T(8,128)(2,1)} %get-tuple-element.81), channel_id=1, source_target_pairs={{0,8},{8,16},{16,24},{24,0},{32,40},{40,48},{48,56},{56,32},{64,72... | collective-permute-start | bytes 1462280 | tf_op jit(solution)/shard_map/ppermute | solution.py:570
  94.3 12.9 %collective-permute-start.10 = (bf16[112,2176]{1,0:T(8,128)(2,1)}, bf16[112,2176]{1,0:T(8,128)(2,1)S(1)}, u32[]{:S(2)}, u32[]{:S(2)}) collective-permute-start(bf16[112,2176]{1,0:T(8,128)(2,1)} %get-tuple-element.82), channel_id=1, source_target_pairs={{0,24},{8,0},{16,8},{24,16},{32,56},{40,32},{48,40},{56,48},{64,88... | collective-permute-start | bytes 1462280 | tf_op jit(solution)/shard_map/ppermute | solution.py:571
  95.7 14.2 %collective-permute-start.11 = (bf16[112,2176]{1,0:T(8,128)(2,1)}, bf16[112,2176]{1,0:T(8,128)(2,1)}, u32[]{:S(2)}, u32[]{:S(2)}) collective-permute-start(bf16[112,2176]{1,0:T(8,128)(2,1)} %get-tuple-element.83), channel_id=1, source_target_pairs={{0,32},{8,40},{16,48},{24,56},{32,64},{40,72},{48,80},{56,88},{64,... | collective-permute-start | bytes 1462280 | tf_op jit(solution)/shard_map/ppermute | solution.py:572
  97.6 12.5 %collective-permute-start.12 = (bf16[112,2176]{1,0:T(8,128)(2,1)}, bf16[112,2176]{1,0:T(8,128)(2,1)}, u32[]{:S(2)}, u32[]{:S(2)}) collective-permute-start(bf16[112,2176]{1,0:T(8,128)(2,1)} %get-tuple-element.84), channel_id=1, source_target_pairs={{0,96},{8,104},{16,112},{24,120},{32,0},{40,8},{48,16},{56,24},{64... | collective-permute-start | bytes 1462280 | tf_op jit(solution)/shard_map/ppermute | solution.py:573
  103.5 6.5 %copy-start.4 = (bf16[4,48,5120]{2,1,0:T(8,128)(2,1)}, bf16[4,48,5120]{2,1,0:T(8,128)(2,1)S(1)}, u32[]{:S(2)}) copy-start(bf16[4,48,5120]{2,1,0:T(8,128)(2,1)S(1)} %all-to-all-done.2.rows) | copy-start | bytes 5898244
  107.0 6.5 %copy-start.9 = (bf16[112,2176]{1,0:T(8,128)(2,1)}, bf16[112,2176]{1,0:T(8,128)(2,1)S(1)}, u32[]{:S(2)}) copy-start(bf16[112,2176]{1,0:T(8,128)(2,1)S(1)} %collective-permute-done.9.a) | copy-start | bytes 1462276
  107.2 6.2 %copy-start.10 = (bf16[112,2176]{1,0:T(8,128)(2,1)}, bf16[112,2176]{1,0:T(8,128)(2,1)S(1)}, u32[]{:S(2)}) copy-start(bf16[112,2176]{1,0:T(8,128)(2,1)S(1)} %collective-permute-done.10.b) | copy-start | bytes 1462276
  110.0 3.4 %copy-start.7 = (bf16[192,1280]{1,0:T(8,128)(2,1)S(1)}, bf16[192,1280]{1,0:T(8,128)(2,1)}, u32[]{:S(2)}) copy-start(bf16[192,1280]{1,0:T(8,128)(2,1)} %shard_map.150) | copy-start | bytes 1474564
  113.5 2.4 %collective-permute-start.14 = (bf16[192,1280]{1,0:T(8,128)(2,1)}, bf16[192,1280]{1,0:T(8,128)(2,1)S(1)}, u32[]{:S(2)}, u32[]{:S(2)}) collective-permute-start(bf16[192,1280]{1,0:T(8,128)(2,1)} %shard_map.155.grad), channel_id=1, source_target_pairs={{0,1},{1,0},{2,3},{3,2},{4,5},{5,4},{6,7},{7,6},{8,9},{9,8},{10,11... | collective-permute-start | bytes 1474568 | tf_op jit(solution)/shard_map/ppermute | solution.py:497
  114.2 1.6 collective-permute-start.13
  115.8 0.9 copy-start.8
  121.7 26.4 %all-to-all-start.3 = ((bf16[4,160,1280]{2,1,0:T(8,128)(2,1)}), bf16[4,160,1280]{2,1,0:T(8,128)(2,1)S(1)}, u32[]{:S(2)}, u32[]{:S(2)}) async-start(bf16[4,160,1280]{2,1,0:T(8,128)(2,1)} %bitcast.21), calls=%async_computation.3 | async-start | bytes 3276800 | tf_op jit(solution)/shard_map/all_to_all | solution.py:508
  126.2 10.1 %copy-start = (bf16[1280,1280]{1,0:T(8,128)(2,1)S(1)}, bf16[1280,1280]{1,0:T(8,128)(2,1)}, u32[]{:S(2)}) copy-start(bf16[1280,1280]{1,0:T(8,128)(2,1)} %weight.1) | copy-start | bytes 9830404
  126.2 10.1 %copy-start.5 = (bf16[192,1280]{1,0:T(8,128)(2,1)S(1)}, bf16[192,1280]{1,0:T(8,128)(2,1)}, u32[]{:S(2)}) copy-start(bf16[192,1280]{1,0:T(8,128)(2,1)} %shard_map.155.grad) | copy-start | bytes 1474564
  129.8 27.6 %collective-permute-start.15 = (bf16[224,2176]{1,0:T(8,128)(2,1)}, bf16[224,2176]{1,0:T(8,128)(2,1)}, u32[]{:S(2)}, u32[]{:S(2)}) collective-permute-start(bf16[224,2176]{1,0:T(8,128)(2,1)} %get-tuple-element.98), channel_id=1, source_target_pairs={{0,8},{8,16},{16,24},{24,0},{32,40},{40,48},{48,56},{56,32},{64,72... | collective-permute-start | bytes 2924552 | tf_op jit(solution)/shard_map/ppermute | solution.py:587
  130.0 27.4 %collective-permute-start.16 = (bf16[224,2176]{1,0:T(8,128)(2,1)}, bf16[224,2176]{1,0:T(8,128)(2,1)}, u32[]{:S(2)}, u32[]{:S(2)}) collective-permute-start(bf16[224,2176]{1,0:T(8,128)(2,1)} %get-tuple-element.99), channel_id=1, source_target_pairs={{0,24},{8,0},{16,8},{24,16},{32,56},{40,32},{48,40},{56,48},{64,88... | collective-permute-start | bytes 2924552 | tf_op jit(solution)/shard_map/ppermute | solution.py:587
  133.0 33.6 %collective-permute-start.20 = (bf16[224,2176]{1,0:T(8,128)(2,1)}, bf16[224,2176]{1,0:T(8,128)(2,1)S(1)}, u32[]{:S(2)}, u32[]{:S(2)}) collective-permute-start(bf16[224,2176]{1,0:T(8,128)(2,1)} %get-tuple-element.105), channel_id=1, source_target_pairs={{0,32},{8,40},{16,48},{24,56},{32,64},{40,72},{48,80},{56,88},{64,... | collective-permute-start | bytes 2924552 | tf_op jit(solution)/shard_map/ppermute | solution.py:588
  134.5 32.2 %collective-permute-start.21 = (bf16[224,2176]{1,0:T(8,128)(2,1)}, bf16[224,2176]{1,0:T(8,128)(2,1)}, u32[]{:S(2)}, u32[]{:S(2)}) collective-permute-start(bf16[224,2176]{1,0:T(8,128)(2,1)} %get-tuple-element.106), channel_id=1, source_target_pairs={{0,96},{8,104},{16,112},{24,120},{32,0},{40,8},{48,16},{56,24},{64... | collective-permute-start | bytes 2924552 | tf_op jit(solution)/shard_map/ppermute | solution.py:588
  148.1 1.2 copy-start.1
  151.8 38.1 %all-to-all-start.4 = ((bf16[16,16,1280]{2,1,0:T(8,128)(2,1)}), bf16[16,16,1280]{2,1,0:T(8,128)(2,1)S(1)}, u32[]{:S(2)}, u32[]{:S(2)}) async-start(bf16[16,16,1280]{2,1,0:T(8,128)(2,1)} %shard_map.157), calls=%async_computation.4 | async-start | bytes 1310720 | tf_op jit(solution)/shard_map/all_to_all | solution.py:583
  161.2 13.8 %collective-permute-start.17 = (bf16[224,544]{1,0:T(8,128)(2,1)}, bf16[224,544]{1,0:T(8,128)(2,1)S(1)}, u32[]{:S(2)}, u32[]{:S(2)}) collective-permute-start(bf16[224,544]{1,0:T(8,128)(2,1)} %get-tuple-element.101), channel_id=1, source_target_pairs={{0,32},{8,40},{16,48},{24,56},{32,64},{40,72},{48,80},{56,88},{64,... | collective-permute-start | bytes 731144 | tf_op jit(solution)/shard_map/ppermute | solution.py:457
  163.1 14.2 %collective-permute-start.18 = (bf16[224,544]{1,0:T(8,128)(2,1)}, bf16[224,544]{1,0:T(8,128)(2,1)S(1)}, u32[]{:S(2)}, u32[]{:S(2)}) collective-permute-start(bf16[224,544]{1,0:T(8,128)(2,1)} %get-tuple-element.102), channel_id=1, source_target_pairs={{0,96},{8,104},{16,112},{24,120},{32,0},{40,8},{48,16},{56,24},{64... | collective-permute-start | bytes 731144 | tf_op jit(solution)/shard_map/ppermute | solution.py:458
  164.4 16.5 %collective-permute-start.19 = (bf16[224,544]{1,0:T(8,128)(2,1)}, bf16[224,544]{1,0:T(8,128)(2,1)S(1)}, u32[]{:S(2)}, u32[]{:S(2)}) collective-permute-start(bf16[224,544]{1,0:T(8,128)(2,1)} %get-tuple-element.103), channel_id=1, source_target_pairs={{0,64},{8,72},{16,80},{24,88},{32,96},{40,104},{48,112},{56,120},{... | collective-permute-start | bytes 731144 | tf_op jit(solution)/shard_map/ppermute | solution.py:456
  166.6 0.9 copy-start.6
  171.4 9.5 %collective-permute-start.22 = (bf16[224,544]{1,0:T(8,128)(2,1)}, bf16[224,544]{1,0:T(8,128)(2,1)S(1)}, u32[]{:S(2)}, u32[]{:S(2)}) collective-permute-start(bf16[224,544]{1,0:T(8,128)(2,1)} %get-tuple-element.108), channel_id=1, source_target_pairs={{0,8},{8,16},{16,24},{24,0},{32,40},{40,48},{48,56},{56,32},{64,72... | collective-permute-start | bytes 731144 | tf_op jit(solution)/shard_map/ppermute | solution.py:457
  172.9 12.4 %collective-permute-start.23 = (bf16[224,544]{1,0:T(8,128)(2,1)}, bf16[224,544]{1,0:T(8,128)(2,1)S(1)}, u32[]{:S(2)}, u32[]{:S(2)}) collective-permute-start(bf16[224,544]{1,0:T(8,128)(2,1)} %get-tuple-element.109), channel_id=1, source_target_pairs={{0,24},{8,0},{16,8},{24,16},{32,56},{40,32},{48,40},{56,48},{64,88... | collective-permute-start | bytes 731144 | tf_op jit(solution)/shard_map/ppermute | solution.py:458
  175.0 11.5 %copy-start.11 = (bf16[224,544]{1,0:T(8,128)(2,1)}, bf16[224,544]{1,0:T(8,128)(2,1)S(1)}, u32[]{:S(2)}) copy-start(bf16[224,544]{1,0:T(8,128)(2,1)S(1)} %collective-permute-done.17.a1) | copy-start | bytes 731140
  175.0 11.5 %collective-permute-start.24 = (bf16[224,544]{1,0:T(8,128)(2,1)}, bf16[224,544]{1,0:T(8,128)(2,1)S(1)}, u32[]{:S(2)}, u32[]{:S(2)}) collective-permute-start(bf16[224,544]{1,0:T(8,128)(2,1)} %get-tuple-element.110), channel_id=1, source_target_pairs={{0,16},{8,24},{16,0},{24,8},{32,48},{40,56},{48,32},{56,40},{64,80... | collective-permute-start | bytes 731144 | tf_op jit(solution)/shard_map/ppermute | solution.py:456
  177.3 9.2 %copy-start.12 = (bf16[224,544]{1,0:T(8,128)(2,1)}, bf16[224,544]{1,0:T(8,128)(2,1)S(1)}, u32[]{:S(2)}) copy-start(bf16[224,544]{1,0:T(8,128)(2,1)S(1)} %collective-permute-done.18.a2) | copy-start | bytes 731140
  181.0 5.6 %copy-start.13 = (bf16[224,544]{1,0:T(8,128)(2,1)}, bf16[224,544]{1,0:T(8,128)(2,1)S(1)}, u32[]{:S(2)}) copy-start(bf16[224,544]{1,0:T(8,128)(2,1)S(1)} %collective-permute-done.19.a3) | copy-start | bytes 731140
  181.0 5.6 %copy-start.14 = (bf16[224,544]{1,0:T(8,128)(2,1)}, bf16[224,544]{1,0:T(8,128)(2,1)S(1)}, u32[]{:S(2)}) copy-start(bf16[224,544]{1,0:T(8,128)(2,1)S(1)} %collective-permute-done.22.b1) | copy-start | bytes 731140
  185.3 1.2 copy-start.15
  (3 other events, 2.1 us)

commit v3 on v2

--- a/solution.py
+++ b/solution.py
@@ -11,6 +11,7 @@
 YN, XN = 4, 4
 TP = ZN * CN
 PARAMS = pltpu.CompilerParams(vmem_limit_bytes=56 * 1024 * 1024)
+SMALL = pltpu.CompilerParams(vmem_limit_bytes=20 * 1024 * 1024)
 
 CORE_SWAP = [(i, i ^ 1) for i in range(TP)]
 Z_GROUPS = [[z * CN + c for z in range(ZN)] for c in range(CN)]
@@ -185,7 +186,7 @@
         in_specs=[VMEM] * 4,
         out_specs=VMEM,
         scratch_shapes=[pltpu.VMEM((10, 192, 128), F32)],
-        compiler_params=PARAMS,
+        compiler_params=SMALL,
         cost_estimate=LONG,
     )(rows, normed, inverse, gain.reshape(1, 1280))
 
@@ -304,13 +305,14 @@
         out[:, 1280 + y * 224 : 1504 + y * 224] = og[y, :, x * 224 : x * 224 + 224]
 
 
-def weight_grad_kernel(ids, stk, stk_other, og, og_other, pre, hid, recv, *outs):
+def weight_grad_kernel(far, ids, stk, stk_other, og, og_other, pre, hid, recv, *outs):
     i = pl.program_id(0)
-    x_first, y_first = outs[:5], outs[5:10]
-    picked, picked_other = outs[10:]
+    turn = 2 if far else jnp.where(i == 2, 3, i)
+    x_at, y_at = lax.rem(ids[1] + turn, 4), lax.rem(ids[0] + turn, 4)
+    picked, picked_other = outs[-2:]
     for x in range(4):
 
-        @pl.when(i == x)
+        @pl.when(x_at == x)
         def _(x=x):
             x_columns(stk, og, x, picked)
             x_columns(stk_other, og_other, x, picked_other)
@@ -322,48 +324,50 @@
         ],
         axis=1,
     ).astype(BF16)
-    at = pl.ds(pl.multiple_of(i * 1280, 128), 1280)
+    at = pl.ds(pl.multiple_of(y_at * 1280, 128), 1280)
     down = jnp.concatenate(
         [
             mm(pre[224:448], stk[:, at]) + mm(recv[224:448], stk_other[:, at]),
-            mm(hid[224:448], og[i]) + mm(recv[672:896], og_other[i]),
+            mm(hid[224:448], og[y_at]) + mm(recv[672:896], og_other[y_at]),
         ],
         axis=1,
     ).astype(BF16)
-    x_turn = lax.rem(i - ids[1] + 4, 4)
-    y_turn = lax.rem(i - ids[0] + 4, 4)
-    for turn, dests, value in ((x_turn, x_first, across), (y_turn, y_first, down)):
-        for dest, k in ((0, 0), (1, 1), (2, 3)):
-
-            @pl.when(turn == k)
-            def _(dest=dests[dest], value=value):
-                dest[...] = value
-
-        @pl.when(turn == 2)
-        def _(dests=dests, value=value):
-            dests[3][...] = value[0:112]
-            dests[4][...] = value[112:224]
-
-
-def weight_grads_of(ids, stk, stk_other, og, og_other, pre, hid, recv):
+    if far:
+        outs[0][...] = across[0:112]
+        outs[1][...] = across[112:224]
+        outs[2][...] = down[0:112]
+        outs[3][...] = down[112:224]
+        return
+    for k in range(3):
+
+        @pl.when(i == k)
+        def _(k=k):
+            outs[k][...] = across
+            outs[3 + k][...] = down
+
+
+def weight_grads_of(far, ids, stk, stk_other, og, og_other, pre, hid, recv):
     once = pl.Buffered(buffer_count=1)
 
     def single(shape):
         return pl.BlockSpec(shape, lambda *_: (0,) * len(shape), pipeline_mode=once)
 
-    shapes = [(224, 2176)] * 3 + [(112, 2176)] * 2
-    return pl.pallas_call(
-        weight_grad_kernel,
-        out_shape=tuple(struct(shape, BF16) for shape in shapes * 2),
-        grid=(4,),
+    def kernel(*refs):
+        weight_grad_kernel(far, *refs)
+
+    shapes = [(112, 2176)] * 4 if far else [(224, 2176)] * 6
+    return pl.pallas_call(
+        kernel,
+        out_shape=tuple(struct(shape, BF16) for shape in shapes),
+        grid=(1 if far else 3,),
         in_specs=[SMEM]
         + [single((192, 5120))] * 2
         + [single((4, 192, 896))] * 2
         + [single((448, 192)), single((448, 192)), single((896, 192))],
-        out_specs=tuple(single(shape) for shape in shapes * 2),
+        out_specs=tuple(single(shape) for shape in shapes),
         scratch_shapes=[pltpu.VMEM((192, 2176), BF16)] * 2,
         compiler_params=PARAMS,
-        cost_estimate=LONG,
+        cost_estimate=HINT if far else LONG,
     )(ids, stk, stk_other, og, og_other, pre, hid, recv)
 
 
@@ -409,7 +413,7 @@
         in_specs=[SMEM] + [VMEM] * 3,
         out_specs=(VMEM,) * 4,
         compiler_params=PARAMS,
-        cost_estimate=HINT,
+        cost_estimate=LONG,
     )(where, *parts)
 
 
@@ -428,7 +432,7 @@
         in_specs=[VMEM] * 8,
         out_specs=(VMEM, VMEM),
         compiler_params=PARAMS,
-        cost_estimate=HINT,
+        cost_estimate=LONG,
     )(*first, *second)
 
 
@@ -447,7 +451,7 @@
         out_shape=struct((16, 16, 1280), BF16),
         in_specs=[VMEM],
         out_specs=VMEM,
-        compiler_params=PARAMS,
+        compiler_params=SMALL,
         cost_estimate=HINT,
     )(parts)
 
@@ -459,36 +463,42 @@
     return (parts[0], up, down, far)
 
 
-def order_kernel(target, context, out):
-    pick = jnp.where(iota((1280, 256), 0) == target[...], 1.0, 0.0).astype(BF16)
-    out[...] = mm(context[...], pick).astype(BF16)
+def order_kernel(target, target_other, context, out, out_other):
+    for where, to in ((target, out), (target_other, out_other)):
+        pick = jnp.where(iota((1280, 128), 0) == where[...], 1.0, 0.0).astype(BF16)
+        to[...] = mm(context[...], pick).T.astype(BF16)
 
 
 def order_of(target, context):
+    target = target.reshape(1, 1280)
     return pl.pallas_call(
         order_kernel,
-        out_shape=struct((192, 1280), BF16),
+        out_shape=(struct((640, 192), BF16),) * 2,
         grid=(5,),
-        in_specs=[pl.BlockSpec((1, 256), lambda i: (0, i)), whole((192, 1280))],
-        out_specs=pl.BlockSpec((192, 256), lambda i: (0, i)),
-        compiler_params=PARAMS,
+        in_specs=[
+            pl.BlockSpec((1, 128), lambda i: (0, i)),
+            pl.BlockSpec((1, 128), lambda i: (0, i + 5)),
+            whole((192, 1280)),
+        ],
+        out_specs=(pl.BlockSpec((128, 192), lambda i: (i, 0)),) * 2,
+        compiler_params=SMALL,
         cost_estimate=LONG,
-    )(target.reshape(1, 1280), context)
+    )(target, target, context)
 
 
 def out_weight_kernel(ctx, ctx_other, grad, grad_other, out):
-    out[...] = (mm(ctx[...], grad[...], 0, 0) + mm(ctx_other[...], grad_other[...], 0, 0)).astype(BF16)
+    out[...] = (mm(ctx[...], grad[...]) + mm(ctx_other[...], grad_other[...])).astype(BF16)
 
 
 def out_weight_of(ctx, ctx_other, grad, grad_other):
-    block = pl.BlockSpec((192, 128), lambda i: (0, i))
+    block = pl.BlockSpec((192, 256), lambda i: (0, i))
     return pl.pallas_call(
         out_weight_kernel,
         out_shape=struct((640, 1280), BF16),
         grid=(5,),
-        in_specs=[block, block, whole((192, 1280)), whole((192, 1280))],
-        out_specs=pl.BlockSpec((128, 1280), lambda i: (i, 0)),
-        compiler_params=PARAMS,
+        in_specs=[whole((640, 192)), whole((640, 192)), block, block],
+        out_specs=pl.BlockSpec((640, 256), lambda i: (0, i)),
+        compiler_params=SMALL,
         cost_estimate=HINT,
     )(ctx, ctx_other, grad, grad_other)
 
@@ -547,13 +557,13 @@
     place = jnp.arange(1280, dtype=jnp.int32)
     core = (place // 640 + c) % 2
     target = (2 * ((place % 640) // 160) + core) * 10 + ((place % 160) // 10) * 80 + place % 10
-    ordered = order_of(target, context)
-    context_keep, context_got = ordered[:, :640], swap(ordered[:, 640:])
+    context_keep, context_give = order_of(target, context)
+    context_got = swap(context_give)
 
     rows, _ = lax.optimization_barrier((rows, grad_pair))
     stk, hid_own, hid_other, slope_own, slope_other = preact_of(ids, rows, in_own, in_other)
     stk_other = swap(stk)
-    og, _ = lax.optimization_barrier((og, ordered))
+    og, _ = lax.optimization_barrier((og, context_give))
     og_other = swap(og)
     pre_own, send, pre_rows, pre_rows_other = pre_grad_of(
         og, adapter_out, out_other, hid_other, slope_own, slope_other
@@ -563,31 +573,40 @@
     row_parts = z_exchange(row_part.reshape(4, 48, 5120))
 
     pre_own, _ = lax.optimization_barrier((pre_own, row_part))
-    parts = weight_grads_of(ids, stk, stk_other, og, og_other, pre_own, hid_own, recv)
-    x_here, x_up, x_down, x_far, x_far2 = parts[:5]
-    y_here, y_up, y_down, y_far, y_far2 = parts[5:]
+    operands = (ids, stk, stk_other, og, og_other, pre_own, hid_own, recv)
+    x_far, x_far2, y_far, y_far2 = weight_grads_of(True, *operands)
     got = (
         lax.ppermute(x_far, "seq", x_shift(1)),
         lax.ppermute(x_far2, "seq", x_shift(-1)),
         lax.ppermute(y_far, "seq", y_shift(1)),
         lax.ppermute(y_far2, "seq", y_shift(-1)),
     )
-    row_parts, got = lax.optimization_barrier((row_parts, got))
+    pre_own, _ = lax.optimization_barrier((pre_own, x_far))
+    x_here, x_up, x_down, y_here, y_up, y_down = weight_grads_of(
+        False, ids, stk, stk_other, og, og_other, pre_own, hid_own, recv
+    )
+    x_up, x_down, y_up, y_down = bump_of(x_up, x_down, y_up, y_down, got)
+    row_parts, _ = lax.optimization_barrier((row_parts, x_up))
 
     d_residual = norm_back_of(row_parts, normed, inverse, final_norm_weight)
     residual_other = swap(d_residual)
     weight_part = out_weight_of(context_keep, context_got, d_residual, residual_other)
-    d_context = mm(d_residual, out_weight, 1, 1).astype(BF16)
-    weight_parts, _ = lax.optimization_barrier((z_exchange(weight_part.reshape(4, 160, 1280)), d_context))
+    residual_late, _ = lax.optimization_barrier((d_residual, weight_part))
+    d_context = mm(residual_late, out_weight, 1, 1).astype(BF16)
+    y_here, _ = lax.optimization_barrier((y_here, d_context))
+    y_next = spread_of(
+        ids[1:2], (y_here, lax.ppermute(y_up, "seq", y_shift(1)), lax.ppermute(y_down, "seq", y_shift(-1)))
+    )
+    x_sums = (x_here, lax.ppermute(x_up, "seq", x_shift(1)), lax.ppermute(x_down, "seq", x_shift(-1)))
+
+    weight_parts, _ = lax.optimization_barrier((z_exchange(weight_part.reshape(4, 160, 1280)), y_next[0]))
     weight_z = weight_sum_of(weight_parts)
     pieces = lax.all_to_all(weight_z, "seq", split_axis=0, concat_axis=0, tiled=True)
     d_out_weight = jnp.sum(pieces.astype(F32), axis=0)[:10]
 
-    x_up, x_down, y_up, y_down = bump_of(x_up, x_down, y_up, y_down, got)
-    x_sums = (x_here, lax.ppermute(x_up, "seq", x_shift(1)), lax.ppermute(x_down, "seq", x_shift(-1)))
-    y_sums = (y_here, lax.ppermute(y_up, "seq", y_shift(1)), lax.ppermute(y_down, "seq", y_shift(-1)))
-    first = ring_of(spread_of(ids[0:1], x_sums), y_shift)
-    second = ring_of(spread_of(ids[1:2], y_sums), x_shift)
+    x_next = spread_of(ids[0:1], x_sums)
+    first = ring_of(x_next, y_shift)
+    second = ring_of(y_next, x_shift)
     grad_in, grad_out = finish_of(first, second)
 
     return (

time: 192 us -> 170 us (0.89)
  waiting for transfers between devices: 41.7 us -> 27.2 us
  starting transfers between devices: 58.4 us -> 53 us
  Pallas kernels: 78.4 us -> 74.9 us
  matrix products: 2.01 us -> 3.93 us
    all_to_all x3, waiting for transfers between devices: 14.7 us -> 1.71 us  [z_exchange(): lax.all_to_all(parts, 'tp', split_axis=0, concat_axis=0, axis_index_group...]
    ppermute x2, waiting for transfers between devices: 4.89 us -> 0.01 us  [ring_of(): far = lax.ppermute(parts[2], 'seq', shift(2))]
    ppermute x2, waiting for transfers between devices: 0.36 us -> 4.13 us  [ring_of(): up = lax.ppermute(parts[1], 'seq', shift(1))]
    ppermute x1, waiting for transfers between devices: 3.5 us -> 0.01 us  [per_device(): lax.ppermute(x_far, 'seq', x_shift(1))]
    ppermute x2, starting transfers between devices: 4.49 us -> 1.43 us  [ring_of(): far = lax.ppermute(parts[2], 'seq', shift(2))]
    ppermute x2, waiting for transfers between devices: 4.34 us -> 7.39 us  [ring_of(): down = lax.ppermute(parts[3], 'seq', shift(-1))]
    ppermute x2, starting transfers between devices: 3.07 us -> 5.85 us  [ring_of(): down = lax.ppermute(parts[3], 'seq', shift(-1))]
    ppermute x2, starting transfers between devices: 3.4 us -> 0.62 us  [ring_of(): up = lax.ppermute(parts[1], 'seq', shift(1))]
  transfers between devices with their start and end apart: 30 -> 30, of which waited for: 15 -> 9; matrix products, arithmetic and copies ran while one was open for 3% -> 3% of each run, Pallas kernels for 37% -> 45%
where the time goes in v3:
time: 170 us; the launch traced here: 168 us
  Pallas kernels  74.9 us (44%)
  starting transfers between devices  53 us (31%)
  waiting for transfers between devices  27.2 us (16%)
  local copies, waits for them, and re-layouts  7.32 us (4%)
  matrix products  3.93 us (2%)
    pallas_call x2, Pallas kernels, weight_grads_of(): pl.pallas_call(kernel, out_shape=tuple((struct(shape, BF16) for shape in...  17.4 us
    all_to_all x3, starting transfers between devices, z_exchange(): lax.all_to_all(parts, 'tp', split_axis=0, concat_axis=0, axis_index_group...  13.8 us
    pallas_call x1, Pallas kernels, preact_of(): pl.pallas_call(preact_kernel, out_shape=(struct((192, 5120), BF16), struc...  9.22 us
    pallas_call x2, Pallas kernels, spread_of(): pl.pallas_call(spread_kernel, out_shape=(struct((224, 544), BF16),) * 4,...  7.64 us
    ppermute x2, waiting for transfers between devices, ring_of(): down = lax.ppermute(parts[3], 'seq', shift(-1))  7.39 us
    all_to_all x1, starting transfers between devices, per_device(): lax.all_to_all(parcels, 'seq', split_axis=0, concat_axis=0, tiled=True)  7.16 us
    pallas_call x1, Pallas kernels, pre_grad_of(): pl.pallas_call(pre_grad_kernel, out_shape=(struct((448, 192), BF16), stru...  6.99 us
    pallas_call x1, Pallas kernels, rows_of(): pl.pallas_call(row_kernel, out_shape=struct((192, 5120), BF16), grid=(4,)...  6.7 us
  transfers between devices with their start and end apart: 30, of which 9 were waited for; matrix products, arithmetic and copies ran while one was open for 3% of the time, Pallas kernels for 45%

profile of v3, /device:TPU:0, one launch (start us, length us, event | category | flops | bytes accessed | tf_op | source)
XLA Modules:
  0.0 168.1 jit_solution(10728878191267369209)
XLA Ops:
  1.8 2.3 %shard_map.146 = bf16[16,48,448]{2,1,0:T(8,128)(2,1)} custom-call(s32[5]{0:T(128)} %stack.23.ids.refs_0_, s32[128]{0:T(128)} %offsets.1, s32[128]{0:T(128)} %frames.1, s32[128]{0:T(128)} %owner.1, bf16[448,384]{1,0:T(8,128)(2,1)} %bitcast.26), custom_call_target="tpu_custom_call" | custom-call | flops 1 | bytes 1 | tf_op jit(solution)/shard_map/pallas_call | solution.py:79
  4.1 7.2 %all-to-all-start = ((bf16[16,48,448]{2,1,0:T(8,128)(2,1)}), bf16[16,48,448]{2,1,0:T(8,128)(2,1)}, u32[]{:S(2)}, u32[]{:S(2)}) async-start(bf16[16,48,448]{2,1,0:T(8,128)(2,1)} %shard_map.146), calls=%async_computation | async-start | bytes 1572864 | tf_op jit(solution)/shard_map/all_to_all | solution.py:546
  12.5 4.7 %shard_map.147 = (bf16[48,5120]{1,0:T(8,128)(2,1)}, f32[192,1280]{1,0:T(8,128)}, f32[192,128]{1,0:T(8,128)}) custom-call(bf16[192,1280]{1,0:T(8,128)(2,1)} %bitcast.18, bf16[192,1280]{1,0:T(8,128)(2,1)} %bitcast.24, bf16[1280,1280]{1,0:T(8,128)(2,1)} %weight.1, f32[1,1280]{1,0:T(1,128)} %reshape.232.gain, f32[1,1280]{1,0:T(1,128)} %reshape.233.bias), custom_call_target="tpu_custom_call" | custom-call | flops 1 | bytes 1 | tf_op jit(solution)/shard_map/pallas_call | solution.py:156
  17.2 1.9 %collective-permute-start.5 = (bf16[48,5120]{1,0:T(8,128)(2,1)}, bf16[48,5120]{1,0:T(8,128)(2,1)}, u32[]{:S(2)}, u32[]{:S(2)}) collective-permute-start(bf16[48,5120]{1,0:T(8,128)(2,1)} %get-tuple-element.68.b0), channel_id=1, source_target_pairs={{0,2},{1,3},{2,4},{3,5},{4,6},{5,7},{6,0},{7,1},{8,10},{9,11},{10,... | collective-permute-start | bytes 1474568 | tf_op jit(solution)/shard_map/ppermute | solution.py:512
  19.1 3.6 %collective-permute-start.4 = (bf16[48,5120]{1,0:T(8,128)(2,1)}, bf16[48,5120]{1,0:T(8,128)(2,1)}, u32[]{:S(2)}, u32[]{:S(2)}) collective-permute-start(bf16[48,5120]{1,0:T(8,128)(2,1)} %get-tuple-element.68.b0), channel_id=1, source_target_pairs={{0,4},{1,5},{2,6},{3,7},{4,0},{5,1},{6,2},{7,3},{8,12},{9,13},{10,... | collective-permute-start | bytes 1474568 | tf_op jit(solution)/shard_map/ppermute | solution.py:511
  22.7 1.0 collective-permute-start.3
  23.7 2.3 %all-to-all-done.arrived = bf16[16,48,448]{2,1,0:T(8,128)(2,1)} async-done(((bf16[16,48,448]{2,1,0:T(8,128)(2,1)}), bf16[16,48,448]{2,1,0:T(8,128)(2,1)}, u32[]{:S(2)}, u32[]{:S(2)}) %all-to-all-start) | async-done | bytes 688160 | tf_op jit(solution)/shard_map/all_to_all | solution.py:546
  26.0 3.1 %shard_map.148 = (bf16[192,448]{1,0:T(8,128)(2,1)}, bf16[192,448]{1,0:T(8,128)(2,1)}) custom-call(s32[5]{0:T(128)} %stack.23.ids.refs_0_, s32[1,128]{1,0:T(1,128)} %bitcast.28, bf16[16,48,448]{2,1,0:T(8,128)(2,1)} %all-to-all-done.arrived), custom_call_target="tpu_custom_call" | custom-call | flops 1 | bytes 1 | tf_op jit(solution)/shard_map/pallas_call | solution.py:109
  29.2 1.5 collective-permute-done.2.got
  31.4 2.3 %shard_map.149 = bf16[4,192,896]{2,1,0:T(8,128)(2,1)} custom-call(s32[5]{0:T(128)} %stack.23.ids.refs_0_, bf16[192,448]{1,0:T(8,128)(2,1)} %get-tuple-element.63.keep, bf16[192,448]{1,0:T(8,128)(2,1)} %copy-done.14), custom_call_target="tpu_custom_call" | custom-call | flops 1 | bytes 1 | tf_op jit(solution)/shard_map/pallas_call | solution.py:129
  33.7 5.3 %all-to-all-start.1 = ((bf16[4,192,896]{2,1,0:T(8,128)(2,1)}), bf16[4,192,896]{2,1,0:T(8,128)(2,1)}, u32[]{:S(2)}, u32[]{:S(2)}) async-start(bf16[4,192,896]{2,1,0:T(8,128)(2,1)} %shard_map.149), calls=%async_computation.1 | async-start | bytes 2752512 | tf_op jit(solution)/shard_map/all_to_all | solution.py:518
  39.0 6.6 %collective-permute-done.4.b2 = bf16[48,5120]{1,0:T(8,128)(2,1)} collective-permute-done((bf16[48,5120]{1,0:T(8,128)(2,1)}, bf16[48,5120]{1,0:T(8,128)(2,1)}, u32[]{:S(2)}, u32[]{:S(2)}) %collective-permute-start.4) | collective-permute-done | bytes 491552 | tf_op jit(solution)/shard_map/ppermute | solution.py:511
  45.6 9.2 %shard_map.151 = (bf16[192,5120]{1,0:T(8,128)(2,1)}, bf16[448,192]{1,0:T(8,128)(2,1)}, bf16[448,192]{1,0:T(8,128)(2,1)}, f32[448,192]{1,0:T(8,128)}, f32[448,192]{1,0:T(8,128)}) custom-call(s32[5]{0:T(128)} %stack.23.ids.refs_0_, bf16[48,5120]{1,0:T(8,128)(2,1)} %get-tuple-element.68.b0, bf16[48,5120]{1,0:T(8,128)(2,1)} %collective-permute-done.3.b1, ...), custom_call_target="tpu_custom_call" | custom-call | flops 1 | bytes 1 | tf_op jit(solution)/shard_map/pallas_call | solution.py:220
  54.9 2.5 %shard_map.150 = (bf16[640,192]{1,0:T(8,128)(2,1)S(1)}, bf16[640,192]{1,0:T(8,128)(2,1)S(1)}) custom-call(s32[1,1280]{1,0:T(1,128)S(1)} %fusion.1.target.target_other, s32[1,1280]{1,0:T(1,128)S(1)} %fusion.1.target.target_other, bf16[192,1280]{1,0:T(8,128)(2,1)S(1)} %bitcast.19), custom_call_target="tpu_custom_call" | custom-call | flops 40000000000 | bytes 100000000 | tf_op jit(solution)/shard_map/pallas_call | solution.py:474
  57.5 1.7 %all-to-all-done.1.og.refs_3_ = bf16[4,192,896]{2,1,0:T(8,128)(2,1)} async-done(((bf16[4,192,896]{2,1,0:T(8,128)(2,1)}), bf16[4,192,896]{2,1,0:T(8,128)(2,1)}, u32[]{:S(2)}, u32[]{:S(2)}) %all-to-all-start.1) | async-done | bytes 1376288 | tf_op jit(solution)/shard_map/all_to_all | solution.py:518
  59.2 7.0 %shard_map.152 = (bf16[448,192]{1,0:T(8,128)(2,1)}, bf16[896,192]{1,0:T(8,128)(2,1)}, bf16[192,448]{1,0:T(8,128)(2,1)}, bf16[192,448]{1,0:T(8,128)(2,1)}) custom-call(bf16[4,192,896]{2,1,0:T(8,128)(2,1)} %all-to-all-done.1.og.refs_3_, bf16[448,3584]{1,0:T(8,128)(2,1)} %out_own.1, bf16[448,3584]{1,0:T(8,128)(2,1)} %copy-done.8, ...), custom_call_target="tpu_custom_call" | custom-call | flops 1 | bytes 1 | tf_op jit(solution)/shard_map/pallas_call | solution.py:268
  66.7 6.7 %shard_map.153 = bf16[192,5120]{1,0:T(8,128)(2,1)} custom-call(bf16[192,448]{1,0:T(8,128)(2,1)} %get-tuple-element.76.pre, bf16[192,448]{1,0:T(8,128)(2,1)} %get-tuple-element.77.pre_other, bf16[448,5120]{1,0:T(8,128)(2,1)} %bitcast.22, bf16[448,5120]{1,0:T(8,128)(2,1)} %collective-permute-done.other_w.in_other), custom_call_target="tpu_custom_call" | custom-call | flops 1 | bytes 1 | tf_op jit(solution)/shard_map/pallas_call | solution.py:291
  73.4 3.6 %all-to-all-start.2 = ((bf16[4,48,5120]{2,1,0:T(8,128)(2,1)}), bf16[4,48,5120]{2,1,0:T(8,128)(2,1)S(1)}, u32[]{:S(2)}, u32[]{:S(2)}) async-start(bf16[4,48,5120]{2,1,0:T(8,128)(2,1)} %bitcast.23), calls=%async_computation.2 | async-start | bytes 3932160 | tf_op jit(solution)/shard_map/all_to_all | solution.py:518
  77.1 0.7 copy-done.13
  77.8 5.9 %shard_map.154 = (bf16[112,2176]{1,0:T(8,128)(2,1)}, bf16[112,2176]{1,0:T(8,128)(2,1)}, bf16[112,2176]{1,0:T(8,128)(2,1)}, bf16[112,2176]{1,0:T(8,128)(2,1)}) custom-call(s32[5]{0:T(128)} %stack.23.ids.refs_0_, bf16[192,5120]{1,0:T(8,128)(2,1)} %get-tuple-element.78.refs_1_, bf16[192,5120]{1,0:T(8,128)(2,1)} %collective-permute-done.6.refs_2_, ...), custom_call_target="tpu_custom_call" | custom-call | flops 1 | bytes 1 | tf_op jit(solution)/shard_map/pallas_call | solution.py:359
  83.7 1.4 collective-permute-start.9
  85.2 1.8 %collective-permute-start.10 = (bf16[112,2176]{1,0:T(8,128)(2,1)}, bf16[112,2176]{1,0:T(8,128)(2,1)S(1)}, u32[]{:S(2)}, u32[]{:S(2)}) collective-permute-start(bf16[112,2176]{1,0:T(8,128)(2,1)} %get-tuple-element.89), channel_id=1, source_target_pairs={{0,24},{8,0},{16,8},{24,16},{32,56},{40,32},{48,40},{56,48},{64,88... | collective-permute-start | bytes 1462280 | tf_op jit(solution)/shard_map/ppermute | solution.py:580
  87.0 1.6 collective-permute-start.11
  88.6 1.6 collective-permute-start.12
  90.2 11.4 %shard_map.155 = (bf16[224,2176]{1,0:T(8,128)(2,1)}, bf16[224,2176]{1,0:T(8,128)(2,1)}, bf16[224,2176]{1,0:T(8,128)(2,1)}, bf16[224,2176]{1,0:T(8,128)(2,1)}, bf...) custom-call(s32[5]{0:T(128)} %stack.23.ids.refs_0_, bf16[192,5120]{1,0:T(8,128)(2,1)} %get-tuple-element.78.refs_1_, ...), custom_call_target="tpu_custom_call" | custom-call | flops 40000000000 | bytes 100000000 | tf_op jit(solution)/shard_map/pallas_call | solution.py:359
  102.9 3.6 %shard_map.156 = (bf16[224,2176]{1,0:T(8,128)(2,1)}, bf16[224,2176]{1,0:T(8,128)(2,1)}, bf16[224,2176]{1,0:T(8,128)(2,1)}, bf16[224,2176]{1,0:T(8,128)(2,1)}) custom-call(bf16[224,2176]{1,0:T(8,128)(2,1)} %get-tuple-element.85.x_up, ...), custom_call_target="tpu_custom_call", output_to_operand_aliasing={{0}: (0, {}), {1}: (1, {}), {2}: (2, {}), {3}: (3, {})} | custom-call | flops 1 | bytes 1 | tf_op jit(solution)/shard_map/pallas_call | solution.py:383
  107.0 2.7 %collective-permute-start.16 = (bf16[224,2176]{1,0:T(8,128)(2,1)}, bf16[224,2176]{1,0:T(8,128)(2,1)}, u32[]{:S(2)}, u32[]{:S(2)}) collective-permute-start(bf16[224,2176]{1,0:T(8,128)(2,1)} %get-tuple-element.101), channel_id=1, source_target_pairs={{0,96},{8,104},{16,112},{24,120},{32,0},{40,8},{48,16},{56,24},{64... | collective-permute-start | bytes 2924552 | tf_op jit(solution)/shard_map/ppermute | solution.py:598
  109.8 1.5 shard_map.157.grad
  112.2 1.3 collective-permute-done.13.ctx_other
  113.4 1.6 collective-permute-start.18
  115.1 1.0 copy-done
  116.1 3.4 %shard_map.158 = bf16[640,1280]{1,0:T(8,128)(2,1)} custom-call(bf16[640,192]{1,0:T(8,128)(2,1)S(1)} %get-tuple-element.96.ctx, bf16[640,192]{1,0:T(8,128)(2,1)S(1)} %collective-permute-done.13.ctx_other, bf16[192,1280]{1,0:T(8,128)(2,1)S(1)} %copy-done, bf16[192,1280]{1,0:T(8,128)(2,1)S(1)} %collective-permute-done.14.grad_other), custom_call_target="tpu_custom_call" | custom-call | flops 1 | bytes 1 | tf_op jit(solution)/shard_map/pallas_call | solution.py:495
  119.4 4.9 %all-to-all-start.3 = ((bf16[4,160,1280]{2,1,0:T(8,128)(2,1)}), bf16[4,160,1280]{2,1,0:T(8,128)(2,1)S(1)}, u32[]{:S(2)}, u32[]{:S(2)}) async-start(bf16[4,160,1280]{2,1,0:T(8,128)(2,1)} %bitcast.13), calls=%async_computation.3 | async-start | bytes 3276800 | tf_op jit(solution)/shard_map/all_to_all | solution.py:518
  124.3 3.9 %convolution_convert_fusion = bf16[192,1280]{1,0:T(8,128)(2,1)} fusion(bf16[192,1280]{1,0:T(8,128)(2,1)S(1)} %copy-done.1, bf16[1280,1280]{1,0:T(8,128)(2,1)} %weight.1), kind=kOutput, calls=%fused_computation | convolution fusion | flops 629391360 | bytes 4259840 | tf_op jit(solution)/shard_map/dot_general | solution.py:39
  128.3 2.2 %collective-permute-done.15.b = bf16[224,2176]{1,0:T(8,128)(2,1)} collective-permute-done((bf16[224,2176]{1,0:T(8,128)(2,1)}, bf16[224,2176]{1,0:T(8,128)(2,1)}, u32[]{:S(2)}, u32[]{:S(2)}) %collective-permute-start.15) | collective-permute-done | bytes 974880 | tf_op jit(solution)/shard_map/ppermute | solution.py:598
  130.4 3.8 %shard_map.159 = (bf16[224,544]{1,0:T(8,128)(2,1)}, bf16[224,544]{1,0:T(8,128)(2,1)}, bf16[224,544]{1,0:T(8,128)(2,1)}, bf16[224,544]{1,0:T(8,128)(2,1)}) custom-call(s32[1]{0:T(128)} %bitcast.1.where, bf16[224,2176]{1,0:T(8,128)(2,1)} %get-tuple-element.99.a, bf16[224,2176]{1,0:T(8,128)(2,1)} %collective-permute-done.15.b, ...), custom_call_target="tpu_custom_call" | custom-call | flops 40000000000 | bytes 100000000 | tf_op jit(solution)/shard_map/pallas_call | solution.py:410
  134.6 2.9 %collective-permute-start.23 = (bf16[224,544]{1,0:T(8,128)(2,1)}, bf16[224,544]{1,0:T(8,128)(2,1)S(1)}, u32[]{:S(2)}, u32[]{:S(2)}) collective-permute-start(bf16[224,544]{1,0:T(8,128)(2,1)} %get-tuple-element.111), channel_id=1, source_target_pairs={{0,24},{8,0},{16,8},{24,16},{32,56},{40,32},{48,40},{56,48},{64,88... | collective-permute-start | bytes 731144 | tf_op jit(solution)/shard_map/ppermute | solution.py:462
  137.5 0.7 collective-permute-start.24
  138.2 1.0 copy-done.17
  139.2 3.8 %shard_map.161 = (bf16[224,544]{1,0:T(8,128)(2,1)}, bf16[224,544]{1,0:T(8,128)(2,1)}, bf16[224,544]{1,0:T(8,128)(2,1)}, bf16[224,544]{1,0:T(8,128)(2,1)}) custom-call(s32[1]{0:T(128)} %bitcast.where, bf16[224,2176]{1,0:T(8,128)(2,1)} %get-tuple-element.104.a, bf16[224,2176]{1,0:T(8,128)(2,1)} %copy-done.17, bf16[224,2176]{1,0:T(8,128)(2,1)} %collective-permute-done.18.c), custom_call_target="tpu_custom_call" | custom-call | flops 40000000000 | bytes 100000000 | tf_op jit(solution)/shard_map/pallas_call | solution.py:410
  143.2 3.0 %collective-permute-start.20 = (bf16[224,544]{1,0:T(8,128)(2,1)}, bf16[224,544]{1,0:T(8,128)(2,1)S(1)}, u32[]{:S(2)}, u32[]{:S(2)}) collective-permute-start(bf16[224,544]{1,0:T(8,128)(2,1)} %get-tuple-element.108), channel_id=1, source_target_pairs={{0,96},{8,104},{16,112},{24,120},{32,0},{40,8},{48,16},{56,24},{64... | collective-permute-start | bytes 731144 | tf_op jit(solution)/shard_map/ppermute | solution.py:462
  146.2 2.8 %collective-permute-done.22.b1 = bf16[224,544]{1,0:T(8,128)(2,1)S(1)} collective-permute-done((bf16[224,544]{1,0:T(8,128)(2,1)}, bf16[224,544]{1,0:T(8,128)(2,1)S(1)}, u32[]{:S(2)}, u32[]{:S(2)}) %collective-permute-start.22) | collective-permute-done | bytes 243744 | tf_op jit(solution)/shard_map/ppermute | solution.py:461
  149.7 1.1 shard_map.160
  150.8 4.2 %all-to-all-start.4 = ((bf16[16,16,1280]{2,1,0:T(8,128)(2,1)}), bf16[16,16,1280]{2,1,0:T(8,128)(2,1)S(1)}, u32[]{:S(2)}, u32[]{:S(2)}) async-start(bf16[16,16,1280]{2,1,0:T(8,128)(2,1)} %shard_map.160), calls=%async_computation.4 | async-start | bytes 1310720 | tf_op jit(solution)/shard_map/all_to_all | solution.py:604
  155.1 1.4 collective-permute-done.19.a1
  156.4 7.4 %collective-permute-done.20.a2 = bf16[224,544]{1,0:T(8,128)(2,1)S(1)} collective-permute-done((bf16[224,544]{1,0:T(8,128)(2,1)}, bf16[224,544]{1,0:T(8,128)(2,1)S(1)}, u32[]{:S(2)}, u32[]{:S(2)}) %collective-permute-start.20) | collective-permute-done | bytes 243744 | tf_op jit(solution)/shard_map/ppermute | solution.py:462
  164.7 2.7 %shard_map.162 = (bf16[320,448]{1,0:T(8,128)(2,1)}, bf16[448,224]{1,0:T(8,128)(2,1)}) custom-call(bf16[224,544]{1,0:T(8,128)(2,1)} %get-tuple-element.106.a0, bf16[224,544]{1,0:T(8,128)(2,1)} %copy-done.20, bf16[224,544]{1,0:T(8,128)(2,1)} %copy-done.21, bf16[224,544]{1,0:T(8,128)(2,1)} %copy-done.22, bf16[224,544]{1,0:T(8,128)(2,1)} %get-tuple-element.102.b0, ...), custom_call_target="tpu_custom_call" | custom-call | flops 40000000000 | bytes 100000000 | tf_op jit(solution)/shard_map/pallas_call | solution.py:429
  167.4 0.7 convert_reduce_fusion
  (81 shorter events, 8.7 us)
Async XLA Ops:
  0.6 10.7 %copy-start.15 = (f32[1280]{0:T(1024)S(1)}, f32[1280]{0:T(1024)}, u32[]{:S(2)}) copy-start(f32[1280]{0:T(1024)} %param.14) | copy-start | bytes 15364
  0.6 11.3 %copy-start.16 = (f32[1280]{0:T(1024)S(1)}, f32[1280]{0:T(1024)}, u32[]{:S(2)}) copy-start(f32[1280]{0:T(1024)} %param.15) | copy-start | bytes 15364
  0.7 25.3 %collective-permute-start = (bf16[448,5120]{1,0:T(8,128)(2,1)}, bf16[448,5120]{1,0:T(8,128)(2,1)}, u32[]{:S(2)}, u32[]{:S(2)}) collective-permute-start(bf16[448,5120]{1,0:T(8,128)(2,1)} %bitcast.20), channel_id=1, source_target_pairs={{0,1},{1,0},{2,3},{3,2},{4,5},{5,4},{6,7},{7,6},{8,9},{9,8},{10,11... | collective-permute-start | bytes 13762568 | tf_op jit(solution)/shard_map/ppermute | solution.py:507
  0.7 25.2 %collective-permute-start.1 = (bf16[448,3584]{1,0:T(8,128)(2,1)}, bf16[448,3584]{1,0:T(8,128)(2,1)S(1)}, u32[]{:S(2)}, u32[]{:S(2)}) collective-permute-start(bf16[448,3584]{1,0:T(8,128)(2,1)} %out_own.1), channel_id=1, source_target_pairs={{0,1},{1,0},{2,3},{3,2},{4,5},{5,4},{6,7},{7,6},{8,9},{9,8},{10,11... | collective-permute-start | bytes 9633800 | tf_op jit(solution)/shard_map/ppermute | solution.py:507
  4.1 21.9 %all-to-all-start = ((bf16[16,48,448]{2,1,0:T(8,128)(2,1)}), bf16[16,48,448]{2,1,0:T(8,128)(2,1)}, u32[]{:S(2)}, u32[]{:S(2)}) async-start(bf16[16,48,448]{2,1,0:T(8,128)(2,1)} %shard_map.146), calls=%async_computation | async-start | bytes 1572864 | tf_op jit(solution)/shard_map/all_to_all | solution.py:546
  17.2 21.8 %collective-permute-start.5 = (bf16[48,5120]{1,0:T(8,128)(2,1)}, bf16[48,5120]{1,0:T(8,128)(2,1)}, u32[]{:S(2)}, u32[]{:S(2)}) collective-permute-start(bf16[48,5120]{1,0:T(8,128)(2,1)} %get-tuple-element.68.b0), channel_id=1, source_target_pairs={{0,2},{1,3},{2,4},{3,5},{4,6},{5,7},{6,0},{7,1},{8,10},{9,11},{10,... | collective-permute-start | bytes 1474568 | tf_op jit(solution)/shard_map/ppermute | solution.py:512
  19.1 26.5 %collective-permute-start.4 = (bf16[48,5120]{1,0:T(8,128)(2,1)}, bf16[48,5120]{1,0:T(8,128)(2,1)}, u32[]{:S(2)}, u32[]{:S(2)}) collective-permute-start(bf16[48,5120]{1,0:T(8,128)(2,1)} %get-tuple-element.68.b0), channel_id=1, source_target_pairs={{0,4},{1,5},{2,6},{3,7},{4,0},{5,1},{6,2},{7,3},{8,12},{9,13},{10,... | collective-permute-start | bytes 1474568 | tf_op jit(solution)/shard_map/ppermute | solution.py:511
  22.7 22.9 %collective-permute-start.3 = (bf16[48,5120]{1,0:T(8,128)(2,1)}, bf16[48,5120]{1,0:T(8,128)(2,1)}, u32[]{:S(2)}, u32[]{:S(2)}) collective-permute-start(bf16[48,5120]{1,0:T(8,128)(2,1)} %get-tuple-element.68.b0), channel_id=1, source_target_pairs={{0,6},{1,7},{2,0},{3,1},{4,2},{5,3},{6,4},{7,5},{8,14},{9,15},{10,... | collective-permute-start | bytes 1474568 | tf_op jit(solution)/shard_map/ppermute | solution.py:513
  26.0 3.1 %copy-start.8 = (bf16[448,3584]{1,0:T(8,128)(2,1)}, bf16[448,3584]{1,0:T(8,128)(2,1)S(1)}, u32[]{:S(2)}) copy-start(bf16[448,3584]{1,0:T(8,128)(2,1)S(1)} %collective-permute-done.1.out_other) | copy-start | bytes 9633796
  29.1 1.7 collective-permute-start.2
  33.7 25.5 %all-to-all-start.1 = ((bf16[4,192,896]{2,1,0:T(8,128)(2,1)}), bf16[4,192,896]{2,1,0:T(8,128)(2,1)}, u32[]{:S(2)}, u32[]{:S(2)}) async-start(bf16[4,192,896]{2,1,0:T(8,128)(2,1)} %shard_map.149), calls=%async_computation.1 | async-start | bytes 2752512 | tf_op jit(solution)/shard_map/all_to_all | solution.py:518
  39.0 15.9 %copy-start.2 = (bf16[8,24,1280]{2,1,0:T(8,128)(2,1)S(1)}, bf16[8,24,1280]{2,1,0:T(8,128)(2,1)}, u32[]{:S(2)}) copy-start(bf16[8,24,1280]{2,1,0:T(8,128)(2,1)} %param.11) | copy-start | bytes 1474564
  54.8 22.2 %collective-permute-start.6 = (bf16[192,5120]{1,0:T(8,128)(2,1)}, bf16[192,5120]{1,0:T(8,128)(2,1)}, u32[]{:S(2)}, u32[]{:S(2)}) collective-permute-start(bf16[192,5120]{1,0:T(8,128)(2,1)} %get-tuple-element.78.refs_1_), channel_id=1, source_target_pairs={{0,1},{1,0},{2,3},{3,2},{4,5},{5,4},{6,7},{7,6},{8,9},{9,8},{10,11... | collective-permute-start | bytes 5898248 | tf_op jit(solution)/shard_map/ppermute | solution.py:507
  57.5 8.7 %copy-start.5 = (bf16[640,192]{1,0:T(8,128)(2,1)}, bf16[640,192]{1,0:T(8,128)(2,1)S(1)}, u32[]{:S(2)}) copy-start(bf16[640,192]{1,0:T(8,128)(2,1)S(1)} %get-tuple-element.65) | copy-start | bytes 737284
  59.2 17.9 %collective-permute-start.7 = (bf16[4,192,896]{2,1,0:T(8,128)(2,1)}, bf16[4,192,896]{2,1,0:T(8,128)(2,1)}, u32[]{:S(2)}, u32[]{:S(2)}) collective-permute-start(bf16[4,192,896]{2,1,0:T(8,128)(2,1)} %all-to-all-done.1.og.refs_3_), channel_id=1, source_target_pairs={{0,1},{1,0},{2,3},{3,2},{4,5},{5,4},{6,7},{7,6},{8,9},{9,8},{10,11... | collective-permute-start | bytes 4128776 | tf_op jit(solution)/shard_map/ppermute | solution.py:507
  66.2 10.9 %collective-permute-start.8 = (bf16[896,192]{1,0:T(8,128)(2,1)}, bf16[896,192]{1,0:T(8,128)(2,1)S(1)}, u32[]{:S(2)}, u32[]{:S(2)}) collective-permute-start(bf16[896,192]{1,0:T(8,128)(2,1)} %get-tuple-element.82), channel_id=1, source_target_pairs={{0,1},{1,0},{2,3},{3,2},{4,5},{5,4},{6,7},{7,6},{8,9},{9,8},{10,11... | collective-permute-start | bytes 1032200 | tf_op jit(solution)/shard_map/ppermute | solution.py:507
  73.4 33.1 %all-to-all-start.2 = ((bf16[4,48,5120]{2,1,0:T(8,128)(2,1)}), bf16[4,48,5120]{2,1,0:T(8,128)(2,1)S(1)}, u32[]{:S(2)}, u32[]{:S(2)}) async-start(bf16[4,48,5120]{2,1,0:T(8,128)(2,1)} %bitcast.23), calls=%async_computation.2 | async-start | bytes 3932160 | tf_op jit(solution)/shard_map/all_to_all | solution.py:518
  83.7 18.0 %collective-permute-start.9 = (bf16[112,2176]{1,0:T(8,128)(2,1)}, bf16[112,2176]{1,0:T(8,128)(2,1)S(1)}, u32[]{:S(2)}, u32[]{:S(2)}) collective-permute-start(bf16[112,2176]{1,0:T(8,128)(2,1)} %get-tuple-element.83), channel_id=1, source_target_pairs={{0,8},{8,16},{16,24},{24,0},{32,40},{40,48},{48,56},{56,32},{64,72... | collective-permute-start | bytes 1462280 | tf_op jit(solution)/shard_map/ppermute | solution.py:579
  85.2 16.5 %collective-permute-start.10 = (bf16[112,2176]{1,0:T(8,128)(2,1)}, bf16[112,2176]{1,0:T(8,128)(2,1)S(1)}, u32[]{:S(2)}, u32[]{:S(2)}) collective-permute-start(bf16[112,2176]{1,0:T(8,128)(2,1)} %get-tuple-element.89), channel_id=1, source_target_pairs={{0,24},{8,0},{16,8},{24,16},{32,56},{40,32},{48,40},{56,48},{64,88... | collective-permute-start | bytes 1462280 | tf_op jit(solution)/shard_map/ppermute | solution.py:580
  87.0 14.7 %collective-permute-start.11 = (bf16[112,2176]{1,0:T(8,128)(2,1)}, bf16[112,2176]{1,0:T(8,128)(2,1)S(1)}, u32[]{:S(2)}, u32[]{:S(2)}) collective-permute-start(bf16[112,2176]{1,0:T(8,128)(2,1)} %get-tuple-element.90), channel_id=1, source_target_pairs={{0,32},{8,40},{16,48},{24,56},{32,64},{40,72},{48,80},{56,88},{64,... | collective-permute-start | bytes 1462280 | tf_op jit(solution)/shard_map/ppermute | solution.py:581
  88.6 13.1 %collective-permute-start.12 = (bf16[112,2176]{1,0:T(8,128)(2,1)}, bf16[112,2176]{1,0:T(8,128)(2,1)S(1)}, u32[]{:S(2)}, u32[]{:S(2)}) collective-permute-start(bf16[112,2176]{1,0:T(8,128)(2,1)} %get-tuple-element.91), channel_id=1, source_target_pairs={{0,96},{8,104},{16,112},{24,120},{32,0},{40,8},{48,16},{56,24},{64... | collective-permute-start | bytes 1462280 | tf_op jit(solution)/shard_map/ppermute | solution.py:582
  101.7 0.9 copy-start.11
  101.7 1.1 copy-start.12
  101.7 1.2 copy-start.9
  102.9 6.8 %copy-start.3 = (f32[1,1280]{1,0:T(1,128)S(1)}, f32[1,1280]{1,0:T(1,128)}, u32[]{:S(2)}) copy-start(f32[1,1280]{1,0:T(1,128)} %reshape.232.gain) | copy-start | bytes 15364
  102.9 6.8 %copy-start.4 = (f32[192,1280]{1,0:T(8,128)S(1)}, f32[192,1280]{1,0:T(8,128)}, u32[]{:S(2)}) copy-start(f32[192,1280]{1,0:T(8,128)} %get-tuple-element.94.normed) | copy-start | bytes 2949124
  102.9 6.8 %copy-start.7 = (f32[192,128]{1,0:T(8,128)S(1)}, f32[192,128]{1,0:T(8,128)}, u32[]{:S(2)}) copy-start(f32[192,128]{1,0:T(8,128)} %get-tuple-element.95.inverse) | copy-start | bytes 294916
  106.5 23.9 %collective-permute-start.15 = (bf16[224,2176]{1,0:T(8,128)(2,1)}, bf16[224,2176]{1,0:T(8,128)(2,1)}, u32[]{:S(2)}, u32[]{:S(2)}) collective-permute-start(bf16[224,2176]{1,0:T(8,128)(2,1)} %get-tuple-element.100), channel_id=1, source_target_pairs={{0,32},{8,40},{16,48},{24,56},{32,64},{40,72},{48,80},{56,88},{64,... | collective-permute-start | bytes 2924552 | tf_op jit(solution)/shard_map/ppermute | solution.py:598
  107.0 23.4 %collective-permute-start.16 = (bf16[224,2176]{1,0:T(8,128)(2,1)}, bf16[224,2176]{1,0:T(8,128)(2,1)}, u32[]{:S(2)}, u32[]{:S(2)}) collective-permute-start(bf16[224,2176]{1,0:T(8,128)(2,1)} %get-tuple-element.101), channel_id=1, source_target_pairs={{0,96},{8,104},{16,112},{24,120},{32,0},{40,8},{48,16},{56,24},{64... | collective-permute-start | bytes 2924552 | tf_op jit(solution)/shard_map/ppermute | solution.py:598
  109.8 1.5 copy-start.6
  111.3 3.8 %collective-permute-start.14 = (bf16[192,1280]{1,0:T(8,128)(2,1)}, bf16[192,1280]{1,0:T(8,128)(2,1)S(1)}, u32[]{:S(2)}, u32[]{:S(2)}) collective-permute-start(bf16[192,1280]{1,0:T(8,128)(2,1)} %shard_map.157.grad), channel_id=1, source_target_pairs={{0,1},{1,0},{2,3},{3,2},{4,5},{5,4},{6,7},{7,6},{8,9},{9,8},{10,11... | collective-permute-start | bytes 1474568 | tf_op jit(solution)/shard_map/ppermute | solution.py:507
  111.3 2.2 %collective-permute-start.13 = (bf16[640,192]{1,0:T(8,128)(2,1)S(1)}, bf16[640,192]{1,0:T(8,128)(2,1)S(1)}, u32[]{:S(2)}, u32[]{:S(2)}) collective-permute-start(bf16[640,192]{1,0:T(8,128)(2,1)S(1)} %copy-done.6), channel_id=1, source_target_pairs={{0,1},{1,0},{2,3},{3,2},{4,5},{5,4},{6,7},{7,6},{8,9},{9,8},{10,11... | collective-permute-start | bytes 737288 | tf_op jit(solution)/shard_map/ppermute | solution.py:507
  111.8 26.4 %collective-permute-start.17 = (bf16[224,2176]{1,0:T(8,128)(2,1)}, bf16[224,2176]{1,0:T(8,128)(2,1)S(1)}, u32[]{:S(2)}, u32[]{:S(2)}) collective-permute-start(bf16[224,2176]{1,0:T(8,128)(2,1)} %get-tuple-element.92), channel_id=1, source_target_pairs={{0,8},{8,16},{16,24},{24,0},{32,40},{40,48},{48,56},{56,32},{64,72... | collective-permute-start | bytes 2924552 | tf_op jit(solution)/shard_map/ppermute | solution.py:600
  113.4 24.8 %collective-permute-start.18 = (bf16[224,2176]{1,0:T(8,128)(2,1)}, bf16[224,2176]{1,0:T(8,128)(2,1)}, u32[]{:S(2)}, u32[]{:S(2)}) collective-permute-start(bf16[224,2176]{1,0:T(8,128)(2,1)} %get-tuple-element.105), channel_id=1, source_target_pairs={{0,24},{8,0},{16,8},{24,16},{32,56},{40,32},{48,40},{56,48},{64,88... | collective-permute-start | bytes 2924552 | tf_op jit(solution)/shard_map/ppermute | solution.py:600
  115.1 1.0 copy-start
  119.4 4.9 %copy-start.1 = (bf16[192,1280]{1,0:T(8,128)(2,1)S(1)}, bf16[192,1280]{1,0:T(8,128)(2,1)}, u32[]{:S(2)}) copy-start(bf16[192,1280]{1,0:T(8,128)(2,1)} %shard_map.157.grad) | copy-start | bytes 1474564
  119.4 30.3 %all-to-all-start.3 = ((bf16[4,160,1280]{2,1,0:T(8,128)(2,1)}), bf16[4,160,1280]{2,1,0:T(8,128)(2,1)S(1)}, u32[]{:S(2)}, u32[]{:S(2)}) async-start(bf16[4,160,1280]{2,1,0:T(8,128)(2,1)} %bitcast.13), calls=%async_computation.3 | async-start | bytes 3276800 | tf_op jit(solution)/shard_map/all_to_all | solution.py:518
  134.2 14.7 %collective-permute-start.22 = (bf16[224,544]{1,0:T(8,128)(2,1)}, bf16[224,544]{1,0:T(8,128)(2,1)S(1)}, u32[]{:S(2)}, u32[]{:S(2)}) collective-permute-start(bf16[224,544]{1,0:T(8,128)(2,1)} %get-tuple-element.110), channel_id=1, source_target_pairs={{0,8},{8,16},{16,24},{24,0},{32,40},{40,48},{48,56},{56,32},{64,72... | collective-permute-start | bytes 731144 | tf_op jit(solution)/shard_map/ppermute | solution.py:461
  134.6 20.4 %collective-permute-start.23 = (bf16[224,544]{1,0:T(8,128)(2,1)}, bf16[224,544]{1,0:T(8,128)(2,1)S(1)}, u32[]{:S(2)}, u32[]{:S(2)}) collective-permute-start(bf16[224,544]{1,0:T(8,128)(2,1)} %get-tuple-element.111), channel_id=1, source_target_pairs={{0,24},{8,0},{16,8},{24,16},{32,56},{40,32},{48,40},{56,48},{64,88... | collective-permute-start | bytes 731144 | tf_op jit(solution)/shard_map/ppermute | solution.py:462
  137.5 17.6 %collective-permute-start.24 = (bf16[224,544]{1,0:T(8,128)(2,1)}, bf16[224,544]{1,0:T(8,128)(2,1)}, u32[]{:S(2)}, u32[]{:S(2)}) collective-permute-start(bf16[224,544]{1,0:T(8,128)(2,1)} %get-tuple-element.112), channel_id=1, source_target_pairs={{0,16},{8,24},{16,0},{24,8},{32,48},{40,56},{48,32},{56,40},{64,80... | collective-permute-start | bytes 731144 | tf_op jit(solution)/shard_map/ppermute | solution.py:460
  138.2 1.0 copy-start.17
  143.0 13.4 %collective-permute-start.19 = (bf16[224,544]{1,0:T(8,128)(2,1)}, bf16[224,544]{1,0:T(8,128)(2,1)S(1)}, u32[]{:S(2)}, u32[]{:S(2)}) collective-permute-start(bf16[224,544]{1,0:T(8,128)(2,1)} %get-tuple-element.107), channel_id=1, source_target_pairs={{0,32},{8,40},{16,48},{24,56},{32,64},{40,72},{48,80},{56,88},{64,... | collective-permute-start | bytes 731144 | tf_op jit(solution)/shard_map/ppermute | solution.py:461
  143.2 20.6 %collective-permute-start.20 = (bf16[224,544]{1,0:T(8,128)(2,1)}, bf16[224,544]{1,0:T(8,128)(2,1)S(1)}, u32[]{:S(2)}, u32[]{:S(2)}) collective-permute-start(bf16[224,544]{1,0:T(8,128)(2,1)} %get-tuple-element.108), channel_id=1, source_target_pairs={{0,96},{8,104},{16,112},{24,120},{32,0},{40,8},{48,16},{56,24},{64... | collective-permute-start | bytes 731144 | tf_op jit(solution)/shard_map/ppermute | solution.py:462
  149.0 14.9 %copy-start.18 = (bf16[224,544]{1,0:T(8,128)(2,1)}, bf16[224,544]{1,0:T(8,128)(2,1)S(1)}, u32[]{:S(2)}) copy-start(bf16[224,544]{1,0:T(8,128)(2,1)S(1)} %collective-permute-done.22.b1) | copy-start | bytes 731140
  149.0 14.9 %collective-permute-start.21 = (bf16[224,544]{1,0:T(8,128)(2,1)}, bf16[224,544]{1,0:T(8,128)(2,1)S(1)}, u32[]{:S(2)}, u32[]{:S(2)}) collective-permute-start(bf16[224,544]{1,0:T(8,128)(2,1)} %get-tuple-element.109), channel_id=1, source_target_pairs={{0,64},{8,72},{16,80},{24,88},{32,96},{40,104},{48,112},{56,120},{... | collective-permute-start | bytes 731144 | tf_op jit(solution)/shard_map/ppermute | solution.py:460
  150.8 16.6 %all-to-all-start.4 = ((bf16[16,16,1280]{2,1,0:T(8,128)(2,1)}), bf16[16,16,1280]{2,1,0:T(8,128)(2,1)S(1)}, u32[]{:S(2)}, u32[]{:S(2)}) async-start(bf16[16,16,1280]{2,1,0:T(8,128)(2,1)} %shard_map.160), calls=%async_computation.4 | async-start | bytes 1310720 | tf_op jit(solution)/shard_map/all_to_all | solution.py:604
  155.0 8.8 %copy-start.19 = (bf16[224,544]{1,0:T(8,128)(2,1)}, bf16[224,544]{1,0:T(8,128)(2,1)S(1)}, u32[]{:S(2)}) copy-start(bf16[224,544]{1,0:T(8,128)(2,1)S(1)} %collective-permute-done.23.b2) | copy-start | bytes 731140
  156.4 7.4 %copy-start.20 = (bf16[224,544]{1,0:T(8,128)(2,1)}, bf16[224,544]{1,0:T(8,128)(2,1)S(1)}, u32[]{:S(2)}) copy-start(bf16[224,544]{1,0:T(8,128)(2,1)S(1)} %collective-permute-done.19.a1) | copy-start | bytes 731140
  (5 other events, 3.8 us)

commit v4 on v3

--- a/solution.py
+++ b/solution.py
@@ -238,65 +238,79 @@
 
 
 def pre_grad_kernel(
-    og, out_own, out_other, hid_other, slope_own, slope_other,
-    pre_own, send, turned, turned_other, acc, acc_other,
+    og, out_own, out_other, in_own, in_other, hid_other, slope_own, slope_other,
+    row_part, pre_own, send, out_w, in_w, og_w, slope_w, row_w, out_sem, in_sem, og_sem, slope_sem, row_sem,
 ):
-    i = pl.program_id(0)
-
-    @pl.when(i == 0)
-    def _():
-        acc[...] = jnp.zeros_like(acc)
-        acc_other[...] = jnp.zeros_like(acc_other)
-
-    piece = og[0]
-    acc[...] += mm(out_own[...], piece, 1, 1)
-    acc_other[...] += mm(out_other[...], piece, 1, 1)
-
-    @pl.when(i == 3)
-    def _():
-        own = acc[...] * slope_own[...]
-        other = acc_other[...] * slope_other[...]
-        pre_own[...] = own.astype(BF16)
-        send[0:448, :] = other.astype(BF16)
-        send[448:896, :] = hid_other[...]
-        turned[...] = own.T.astype(BF16)
-        turned_other[...] = other.T.astype(BF16)
-
-
-def pre_grad_of(og, out_own, out_other, hid_other, slope_own, slope_other):
-    wide = pl.BlockSpec((448, 896), lambda i: (0, i))
+    copy = pltpu.make_async_copy
+
+    def load(source, to, sem, w, j, width):
+        at = pl.ds(j * width, width)
+        return copy(source.at[:, at], to.at[w, :, at], sem.at[w, j])
+
+    outs, ins = (out_own, out_other), (in_own, in_other)
+    pieces = [copy(og.at[j], og_w.at[j], og_sem.at[j]) for j in range(4)]
+    slopes = [copy(ref, slope_w.at[w], slope_sem.at[w]) for w, ref in enumerate((slope_own, slope_other))]
+    queue = [[pieces[j]] + [load(outs[w], out_w, out_sem, w, j, 896) for w in range(2)] for j in range(4)]
+    queue[3] += slopes
+    queue += [[load(ins[w], in_w, in_sem, w, j, 1280) for w in range(2)] for j in range(4)]
+
+    def begin(n):
+        if n < len(queue):
+            for part in queue[n]:
+                part.start()
+
+    def arrive(n):
+        for part in queue[n]:
+            part.wait()
+        begin(n + 4)
+
+    for n in range(4):
+        begin(n)
+    sums = [jnp.zeros((448, 192), F32)] * 2
+    for j in range(4):
+        arrive(j)
+        for w in range(2):
+            sums[w] = sums[w] + mm(out_w[w, :, j * 896 : j * 896 + 896], og_w[j], 1, 1)
+    own = sums[0] * slope_w[0]
+    other = sums[1] * slope_w[1]
+    pre_own[...] = own.astype(BF16)
+    send[0:448, :] = other.astype(BF16)
+    send[448:896, :] = hid_other[...]
+    turned = (own.T.astype(BF16), other.T.astype(BF16))
+    stores = []
+    for j in range(4):
+        arrive(4 + j)
+        at = slice(j * 1280, j * 1280 + 1280)
+        row_w[:, at] = (mm(turned[0], in_w[0, :, at]) + mm(turned[1], in_w[1, :, at])).astype(BF16)
+        span = pl.ds(j * 1280, 1280)
+        stores.append(copy(row_w.at[:, span], row_part.at[:, span], row_sem.at[j]))
+        stores[-1].start()
+    for store in stores:
+        store.wait()
+
+
+def pre_grad_of(og, out_own, out_other, in_own, in_other, hid_other, slope_own, slope_other):
+    held = pl.BlockSpec(memory_space=pl.ANY)
     return pl.pallas_call(
         pre_grad_kernel,
-        out_shape=(
-            struct((448, 192), BF16),
-            struct((896, 192), BF16),
-            struct((192, 448), BF16),
-            struct((192, 448), BF16),
-        ),
-        grid=(4,),
-        in_specs=[pl.BlockSpec((1, 192, 896), lambda i: (i, 0, 0)), wide, wide] + [whole((448, 192))] * 3,
-        out_specs=(whole((448, 192)), whole((896, 192)), whole((192, 448)), whole((192, 448))),
-        scratch_shapes=[pltpu.VMEM((448, 192), F32)] * 2,
-        compiler_params=PARAMS,
-        cost_estimate=HINT,
-    )(og, out_own, out_other, hid_other, slope_own, slope_other)
-
-
-def row_kernel(pre, pre_other, in_own, in_other, out):
-    out[...] = (mm(pre[...], in_own[...]) + mm(pre_other[...], in_other[...])).astype(BF16)
-
-
-def rows_of(pre, pre_other, in_own, in_other):
-    wide = pl.BlockSpec((448, 1280), lambda i: (0, i))
-    return pl.pallas_call(
-        row_kernel,
-        out_shape=struct((192, 5120), BF16),
-        grid=(4,),
-        in_specs=[whole((192, 448))] * 2 + [wide] * 2,
-        out_specs=pl.BlockSpec((192, 1280), lambda i: (0, i)),
-        compiler_params=PARAMS,
-        cost_estimate=HINT,
-    )(pre, pre_other, in_own, in_other)
+        out_shape=(struct((192, 5120), BF16), struct((448, 192), BF16), struct((896, 192), BF16)),
+        in_specs=[held] * 5 + [VMEM, held, held],
+        out_specs=(held, VMEM, VMEM),
+        scratch_shapes=[
+            pltpu.VMEM((2, 448, 3584), BF16),
+            pltpu.VMEM((2, 448, 5120), BF16),
+            pltpu.VMEM((4, 192, 896), BF16),
+            pltpu.VMEM((2, 448, 192), F32),
+            pltpu.VMEM((192, 5120), BF16),
+            pltpu.SemaphoreType.DMA((2, 4)),
+            pltpu.SemaphoreType.DMA((2, 4)),
+            pltpu.SemaphoreType.DMA((4,)),
+            pltpu.SemaphoreType.DMA((2,)),
+            pltpu.SemaphoreType.DMA((4,)),
+        ],
+        compiler_params=PARAMS,
+        cost_estimate=HINT,
+    )(og, out_own, out_other, in_own, in_other, hid_other, slope_own, slope_other)
 
 
 def x_columns(stk, og, x, out):
@@ -565,11 +579,10 @@
     stk_other = swap(stk)
     og, _ = lax.optimization_barrier((og, context_give))
     og_other = swap(og)
-    pre_own, send, pre_rows, pre_rows_other = pre_grad_of(
-        og, adapter_out, out_other, hid_other, slope_own, slope_other
+    row_part, pre_own, send = pre_grad_of(
+        og, adapter_out, out_other, in_own, in_other, hid_other, slope_own, slope_other
     )
     recv = swap(send)
-    row_part = rows_of(pre_rows, pre_rows_other, in_own, in_other)
     row_parts = z_exchange(row_part.reshape(4, 48, 5120))
 
     pre_own, _ = lax.optimization_barrier((pre_own, row_part))

time: 170 us -> 167 us (0.982)
  Pallas kernels: 74.9 us -> 72.4 us
    pallas_call x2 -> x1, Pallas kernels: 13.7 us -> 10.6 us  [pre_grad_of(): pl.pallas_call(pre_grad_kernel, out_shape=(struct((192, 5120), BF16), str...]
  transfers between devices with their start and end apart: 30 -> 30, of which waited for: 9 -> 9; matrix products, arithmetic and copies ran while one was open for 3% -> 4% of each run, Pallas kernels for 45% -> 44%
where the time goes in v4:
time: 167 us; the launch traced here: 165 us
  Pallas kernels  72.4 us (43%)
  starting transfers between devices  53.1 us (32%)
  waiting for transfers between devices  26.9 us (16%)
  local copies, waits for them, and re-layouts  7.32 us (4%)
  matrix products  3.93 us (2%)
    pallas_call x2, Pallas kernels, weight_grads_of(): pl.pallas_call(kernel, out_shape=tuple((struct(shape, BF16) for shape in...  17.6 us
    all_to_all x3, starting transfers between devices, z_exchange(): lax.all_to_all(parts, 'tp', split_axis=0, concat_axis=0, axis_index_group...  13.8 us
    pallas_call x1, Pallas kernels, pre_grad_of(): pl.pallas_call(pre_grad_kernel, out_shape=(struct((192, 5120), BF16), str...  10.6 us
    pallas_call x1, Pallas kernels, preact_of(): pl.pallas_call(preact_kernel, out_shape=(struct((192, 5120), BF16), struc...  9.2 us
    pallas_call x2, Pallas kernels, spread_of(): pl.pallas_call(spread_kernel, out_shape=(struct((224, 544), BF16),) * 4,...  7.86 us
    ppermute x2, waiting for transfers between devices, ring_of(): down = lax.ppermute(parts[3], 'seq', shift(-1))  7.37 us
    all_to_all x1, starting transfers between devices, per_device(): lax.all_to_all(parcels, 'seq', split_axis=0, concat_axis=0, tiled=True)  7.16 us
    ppermute x1, waiting for transfers between devices, z_blocks(): far = lax.ppermute(block, 'tp', z_shift(2))  6.47 us
  transfers between devices with their start and end apart: 30, of which 9 were waited for; matrix products, arithmetic and copies ran while one was open for 4% of the time, Pallas kernels for 44%

profile of v4, /device:TPU:0, one launch (start us, length us, event | category | flops | bytes accessed | tf_op | source)
XLA Modules:
  0.0 165.3 jit_solution(4714953680565223776)
XLA Ops:
  1.9 2.3 %shard_map.146 = bf16[16,48,448]{2,1,0:T(8,128)(2,1)} custom-call(s32[5]{0:T(128)} %stack.23.ids.refs_0_, s32[128]{0:T(128)} %offsets.1, s32[128]{0:T(128)} %frames.1, s32[128]{0:T(128)} %owner.1, bf16[448,384]{1,0:T(8,128)(2,1)} %bitcast.26), custom_call_target="tpu_custom_call" | custom-call | flops 1 | bytes 1 | tf_op jit(solution)/shard_map/pallas_call | solution.py:79
  4.2 7.2 %all-to-all-start = ((bf16[16,48,448]{2,1,0:T(8,128)(2,1)}), bf16[16,48,448]{2,1,0:T(8,128)(2,1)}, u32[]{:S(2)}, u32[]{:S(2)}) async-start(bf16[16,48,448]{2,1,0:T(8,128)(2,1)} %shard_map.146), calls=%async_computation | async-start | bytes 1572864 | tf_op jit(solution)/shard_map/all_to_all | solution.py:560
  12.6 4.7 %shard_map.147 = (bf16[48,5120]{1,0:T(8,128)(2,1)}, f32[192,1280]{1,0:T(8,128)}, f32[192,128]{1,0:T(8,128)}) custom-call(bf16[192,1280]{1,0:T(8,128)(2,1)} %bitcast.18, bf16[192,1280]{1,0:T(8,128)(2,1)} %bitcast.24, bf16[1280,1280]{1,0:T(8,128)(2,1)} %weight.1, f32[1,1280]{1,0:T(1,128)} %reshape.232.gain, f32[1,1280]{1,0:T(1,128)} %reshape.233.bias), custom_call_target="tpu_custom_call" | custom-call | flops 1 | bytes 1 | tf_op jit(solution)/shard_map/pallas_call | solution.py:156
  17.2 1.9 %collective-permute-start.5 = (bf16[48,5120]{1,0:T(8,128)(2,1)}, bf16[48,5120]{1,0:T(8,128)(2,1)}, u32[]{:S(2)}, u32[]{:S(2)}) collective-permute-start(bf16[48,5120]{1,0:T(8,128)(2,1)} %get-tuple-element.68.b0), channel_id=1, source_target_pairs={{0,2},{1,3},{2,4},{3,5},{4,6},{5,7},{6,0},{7,1},{8,10},{9,11},{10,... | collective-permute-start | bytes 1474568 | tf_op jit(solution)/shard_map/ppermute | solution.py:526
  19.1 3.6 %collective-permute-start.4 = (bf16[48,5120]{1,0:T(8,128)(2,1)}, bf16[48,5120]{1,0:T(8,128)(2,1)}, u32[]{:S(2)}, u32[]{:S(2)}) collective-permute-start(bf16[48,5120]{1,0:T(8,128)(2,1)} %get-tuple-element.68.b0), channel_id=1, source_target_pairs={{0,4},{1,5},{2,6},{3,7},{4,0},{5,1},{6,2},{7,3},{8,12},{9,13},{10,... | collective-permute-start | bytes 1474568 | tf_op jit(solution)/shard_map/ppermute | solution.py:525
  22.7 1.0 collective-permute-start.3
  23.7 2.3 %all-to-all-done.arrived = bf16[16,48,448]{2,1,0:T(8,128)(2,1)} async-done(((bf16[16,48,448]{2,1,0:T(8,128)(2,1)}), bf16[16,48,448]{2,1,0:T(8,128)(2,1)}, u32[]{:S(2)}, u32[]{:S(2)}) %all-to-all-start) | async-done | bytes 688160 | tf_op jit(solution)/shard_map/all_to_all | solution.py:560
  26.1 3.1 %shard_map.148 = (bf16[192,448]{1,0:T(8,128)(2,1)}, bf16[192,448]{1,0:T(8,128)(2,1)}) custom-call(s32[5]{0:T(128)} %stack.23.ids.refs_0_, s32[1,128]{1,0:T(1,128)} %bitcast.28, bf16[16,48,448]{2,1,0:T(8,128)(2,1)} %all-to-all-done.arrived), custom_call_target="tpu_custom_call" | custom-call | flops 1 | bytes 1 | tf_op jit(solution)/shard_map/pallas_call | solution.py:109
  29.3 1.5 collective-permute-done.2.got
  31.5 2.3 %shard_map.149 = bf16[4,192,896]{2,1,0:T(8,128)(2,1)} custom-call(s32[5]{0:T(128)} %stack.23.ids.refs_0_, bf16[192,448]{1,0:T(8,128)(2,1)} %get-tuple-element.62.keep, bf16[192,448]{1,0:T(8,128)(2,1)} %copy-done.14), custom_call_target="tpu_custom_call" | custom-call | flops 1 | bytes 1 | tf_op jit(solution)/shard_map/pallas_call | solution.py:129
  33.8 5.3 %all-to-all-start.1 = ((bf16[4,192,896]{2,1,0:T(8,128)(2,1)}), bf16[4,192,896]{2,1,0:T(8,128)(2,1)}, u32[]{:S(2)}, u32[]{:S(2)}) async-start(bf16[4,192,896]{2,1,0:T(8,128)(2,1)} %shard_map.149), calls=%async_computation.1 | async-start | bytes 2752512 | tf_op jit(solution)/shard_map/all_to_all | solution.py:532
  39.1 6.5 %collective-permute-done.4.b2 = bf16[48,5120]{1,0:T(8,128)(2,1)} collective-permute-done((bf16[48,5120]{1,0:T(8,128)(2,1)}, bf16[48,5120]{1,0:T(8,128)(2,1)}, u32[]{:S(2)}, u32[]{:S(2)}) %collective-permute-start.4) | collective-permute-done | bytes 491552 | tf_op jit(solution)/shard_map/ppermute | solution.py:525
  45.6 9.2 %shard_map.151 = (bf16[192,5120]{1,0:T(8,128)(2,1)}, bf16[448,192]{1,0:T(8,128)(2,1)}, bf16[448,192]{1,0:T(8,128)(2,1)}, f32[448,192]{1,0:T(8,128)}, f32[448,192]{1,0:T(8,128)}) custom-call(s32[5]{0:T(128)} %stack.23.ids.refs_0_, bf16[48,5120]{1,0:T(8,128)(2,1)} %get-tuple-element.68.b0, bf16[48,5120]{1,0:T(8,128)(2,1)} %collective-permute-done.3.b1, ...), custom_call_target="tpu_custom_call" | custom-call | flops 1 | bytes 1 | tf_op jit(solution)/shard_map/pallas_call | solution.py:220
  54.9 2.5 %shard_map.150 = (bf16[640,192]{1,0:T(8,128)(2,1)S(1)}, bf16[640,192]{1,0:T(8,128)(2,1)S(1)}) custom-call(s32[1,1280]{1,0:T(1,128)S(1)} %fusion.1.target.target_other, s32[1,1280]{1,0:T(1,128)S(1)} %fusion.1.target.target_other, bf16[192,1280]{1,0:T(8,128)(2,1)S(1)} %bitcast.19), custom_call_target="tpu_custom_call" | custom-call | flops 40000000000 | bytes 100000000 | tf_op jit(solution)/shard_map/pallas_call | solution.py:488
  57.4 1.8 %all-to-all-done.1.og.refs_3_ = bf16[4,192,896]{2,1,0:T(8,128)(2,1)} async-done(((bf16[4,192,896]{2,1,0:T(8,128)(2,1)}), bf16[4,192,896]{2,1,0:T(8,128)(2,1)}, u32[]{:S(2)}, u32[]{:S(2)}) %all-to-all-start.1) | async-done | bytes 1376288 | tf_op jit(solution)/shard_map/all_to_all | solution.py:532
  59.2 10.6 %shard_map.152 = (bf16[192,5120]{1,0:T(8,128)(2,1)}, bf16[448,192]{1,0:T(8,128)(2,1)}, bf16[896,192]{1,0:T(8,128)(2,1)}) custom-call(bf16[4,192,896]{2,1,0:T(8,128)(2,1)} %all-to-all-done.1.og.refs_3_, bf16[448,3584]{1,0:T(8,128)(2,1)} %out_own.1, bf16[448,3584]{1,0:T(8,128)(2,1)} %copy-done.8, bf16[448,5120]{1,0:T(8,128)(2,1)} %bitcast.22, ...), custom_call_target="tpu_custom_call" | custom-call | flops 1 | bytes 1 | tf_op jit(solution)/shard_map/pallas_call | solution.py:294
  70.4 3.6 %all-to-all-start.2 = ((bf16[4,48,5120]{2,1,0:T(8,128)(2,1)}), bf16[4,48,5120]{2,1,0:T(8,128)(2,1)S(1)}, u32[]{:S(2)}, u32[]{:S(2)}) async-start(bf16[4,48,5120]{2,1,0:T(8,128)(2,1)} %bitcast.23), calls=%async_computation.2 | async-start | bytes 3932160 | tf_op jit(solution)/shard_map/all_to_all | solution.py:532
  74.1 0.7 copy-done.13
  74.8 6.1 %shard_map.153 = (bf16[112,2176]{1,0:T(8,128)(2,1)}, bf16[112,2176]{1,0:T(8,128)(2,1)}, bf16[112,2176]{1,0:T(8,128)(2,1)}, bf16[112,2176]{1,0:T(8,128)(2,1)}) custom-call(s32[5]{0:T(128)} %stack.23.ids.refs_0_, bf16[192,5120]{1,0:T(8,128)(2,1)} %get-tuple-element.76.refs_1_, bf16[192,5120]{1,0:T(8,128)(2,1)} %collective-permute-done.6.refs_2_, ...), custom_call_target="tpu_custom_call" | custom-call | flops 1 | bytes 1 | tf_op jit(solution)/shard_map/pallas_call | solution.py:373
  80.9 1.5 collective-permute-start.9
  82.4 1.8 %collective-permute-start.10 = (bf16[112,2176]{1,0:T(8,128)(2,1)}, bf16[112,2176]{1,0:T(8,128)(2,1)S(1)}, u32[]{:S(2)}, u32[]{:S(2)}) collective-permute-start(bf16[112,2176]{1,0:T(8,128)(2,1)} %get-tuple-element.87), channel_id=1, source_target_pairs={{0,24},{8,0},{16,8},{24,16},{32,56},{40,32},{48,40},{56,48},{64,88... | collective-permute-start | bytes 1462280 | tf_op jit(solution)/shard_map/ppermute | solution.py:593
  84.2 1.6 collective-permute-start.11
  85.8 1.6 collective-permute-start.12
  87.4 11.5 %shard_map.154 = (bf16[224,2176]{1,0:T(8,128)(2,1)}, bf16[224,2176]{1,0:T(8,128)(2,1)}, bf16[224,2176]{1,0:T(8,128)(2,1)}, bf16[224,2176]{1,0:T(8,128)(2,1)}, bf...) custom-call(s32[5]{0:T(128)} %stack.23.ids.refs_0_, bf16[192,5120]{1,0:T(8,128)(2,1)} %get-tuple-element.76.refs_1_, ...), custom_call_target="tpu_custom_call" | custom-call | flops 40000000000 | bytes 100000000 | tf_op jit(solution)/shard_map/pallas_call | solution.py:373
  100.2 3.6 %shard_map.155 = (bf16[224,2176]{1,0:T(8,128)(2,1)}, bf16[224,2176]{1,0:T(8,128)(2,1)}, bf16[224,2176]{1,0:T(8,128)(2,1)}, bf16[224,2176]{1,0:T(8,128)(2,1)}) custom-call(bf16[224,2176]{1,0:T(8,128)(2,1)} %get-tuple-element.83.x_up, ...), custom_call_target="tpu_custom_call", output_to_operand_aliasing={{0}: (0, {}), {1}: (1, {}), {2}: (2, {}), {3}: (3, {})} | custom-call | flops 1 | bytes 1 | tf_op jit(solution)/shard_map/pallas_call | solution.py:397
  104.2 2.8 %collective-permute-start.16 = (bf16[224,2176]{1,0:T(8,128)(2,1)}, bf16[224,2176]{1,0:T(8,128)(2,1)}, u32[]{:S(2)}, u32[]{:S(2)}) collective-permute-start(bf16[224,2176]{1,0:T(8,128)(2,1)} %get-tuple-element.99), channel_id=1, source_target_pairs={{0,96},{8,104},{16,112},{24,120},{32,0},{40,8},{48,16},{56,24},{64... | collective-permute-start | bytes 2924552 | tf_op jit(solution)/shard_map/ppermute | solution.py:611
  107.0 1.5 shard_map.156.grad
  109.4 1.3 collective-permute-done.13.ctx_other
  110.7 1.6 collective-permute-start.18
  112.3 1.0 copy-done
  113.4 3.4 %shard_map.157 = bf16[640,1280]{1,0:T(8,128)(2,1)} custom-call(bf16[640,192]{1,0:T(8,128)(2,1)S(1)} %get-tuple-element.94.ctx, bf16[640,192]{1,0:T(8,128)(2,1)S(1)} %collective-permute-done.13.ctx_other, bf16[192,1280]{1,0:T(8,128)(2,1)S(1)} %copy-done, bf16[192,1280]{1,0:T(8,128)(2,1)S(1)} %collective-permute-done.14.grad_other), custom_call_target="tpu_custom_call" | custom-call | flops 1 | bytes 1 | tf_op jit(solution)/shard_map/pallas_call | solution.py:509
  116.7 4.9 %all-to-all-start.3 = ((bf16[4,160,1280]{2,1,0:T(8,128)(2,1)}), bf16[4,160,1280]{2,1,0:T(8,128)(2,1)S(1)}, u32[]{:S(2)}, u32[]{:S(2)}) async-start(bf16[4,160,1280]{2,1,0:T(8,128)(2,1)} %bitcast.13), calls=%async_computation.3 | async-start | bytes 3276800 | tf_op jit(solution)/shard_map/all_to_all | solution.py:532
  121.6 3.9 %convolution_convert_fusion = bf16[192,1280]{1,0:T(8,128)(2,1)} fusion(bf16[192,1280]{1,0:T(8,128)(2,1)S(1)} %copy-done.1, bf16[1280,1280]{1,0:T(8,128)(2,1)} %weight.1), kind=kOutput, calls=%fused_computation | convolution fusion | flops 629391360 | bytes 4259840 | tf_op jit(solution)/shard_map/dot_general | solution.py:39
  125.5 2.1 %collective-permute-done.15.b = bf16[224,2176]{1,0:T(8,128)(2,1)} collective-permute-done((bf16[224,2176]{1,0:T(8,128)(2,1)}, bf16[224,2176]{1,0:T(8,128)(2,1)}, u32[]{:S(2)}, u32[]{:S(2)}) %collective-permute-start.15) | collective-permute-done | bytes 974880 | tf_op jit(solution)/shard_map/ppermute | solution.py:611
  127.7 4.1 %shard_map.158 = (bf16[224,544]{1,0:T(8,128)(2,1)}, bf16[224,544]{1,0:T(8,128)(2,1)}, bf16[224,544]{1,0:T(8,128)(2,1)}, bf16[224,544]{1,0:T(8,128)(2,1)}) custom-call(s32[1]{0:T(128)} %bitcast.1.where, bf16[224,2176]{1,0:T(8,128)(2,1)} %get-tuple-element.97.a, bf16[224,2176]{1,0:T(8,128)(2,1)} %collective-permute-done.15.b, ...), custom_call_target="tpu_custom_call" | custom-call | flops 40000000000 | bytes 100000000 | tf_op jit(solution)/shard_map/pallas_call | solution.py:424
  132.1 2.8 %collective-permute-start.23 = (bf16[224,544]{1,0:T(8,128)(2,1)}, bf16[224,544]{1,0:T(8,128)(2,1)S(1)}, u32[]{:S(2)}, u32[]{:S(2)}) collective-permute-start(bf16[224,544]{1,0:T(8,128)(2,1)} %get-tuple-element.109), channel_id=1, source_target_pairs={{0,24},{8,0},{16,8},{24,16},{32,56},{40,32},{48,40},{56,48},{64,88... | collective-permute-start | bytes 731144 | tf_op jit(solution)/shard_map/ppermute | solution.py:476
  135.0 0.7 collective-permute-start.24
  135.7 0.9 copy-done.17
  136.7 3.8 %shard_map.160 = (bf16[224,544]{1,0:T(8,128)(2,1)}, bf16[224,544]{1,0:T(8,128)(2,1)}, bf16[224,544]{1,0:T(8,128)(2,1)}, bf16[224,544]{1,0:T(8,128)(2,1)}) custom-call(s32[1]{0:T(128)} %bitcast.where, bf16[224,2176]{1,0:T(8,128)(2,1)} %get-tuple-element.102.a, bf16[224,2176]{1,0:T(8,128)(2,1)} %copy-done.17, bf16[224,2176]{1,0:T(8,128)(2,1)} %collective-permute-done.18.c), custom_call_target="tpu_custom_call" | custom-call | flops 40000000000 | bytes 100000000 | tf_op jit(solution)/shard_map/pallas_call | solution.py:424
  140.7 3.0 %collective-permute-start.20 = (bf16[224,544]{1,0:T(8,128)(2,1)}, bf16[224,544]{1,0:T(8,128)(2,1)S(1)}, u32[]{:S(2)}, u32[]{:S(2)}) collective-permute-start(bf16[224,544]{1,0:T(8,128)(2,1)} %get-tuple-element.106), channel_id=1, source_target_pairs={{0,96},{8,104},{16,112},{24,120},{32,0},{40,8},{48,16},{56,24},{64... | collective-permute-start | bytes 731144 | tf_op jit(solution)/shard_map/ppermute | solution.py:476
  143.7 2.6 %collective-permute-done.22.b1 = bf16[224,544]{1,0:T(8,128)(2,1)S(1)} collective-permute-done((bf16[224,544]{1,0:T(8,128)(2,1)}, bf16[224,544]{1,0:T(8,128)(2,1)S(1)}, u32[]{:S(2)}, u32[]{:S(2)}) %collective-permute-start.22) | collective-permute-done | bytes 243744 | tf_op jit(solution)/shard_map/ppermute | solution.py:475
  146.3 0.9 collective-permute-start.21
  147.2 1.1 shard_map.159
  148.3 4.0 %all-to-all-start.4 = ((bf16[16,16,1280]{2,1,0:T(8,128)(2,1)}), bf16[16,16,1280]{2,1,0:T(8,128)(2,1)S(1)}, u32[]{:S(2)}, u32[]{:S(2)}) async-start(bf16[16,16,1280]{2,1,0:T(8,128)(2,1)} %shard_map.159), calls=%async_computation.4 | async-start | bytes 1310720 | tf_op jit(solution)/shard_map/all_to_all | solution.py:617
  152.3 1.4 collective-permute-done.19.a1
  153.7 7.4 %collective-permute-done.20.a2 = bf16[224,544]{1,0:T(8,128)(2,1)S(1)} collective-permute-done((bf16[224,544]{1,0:T(8,128)(2,1)}, bf16[224,544]{1,0:T(8,128)(2,1)S(1)}, u32[]{:S(2)}, u32[]{:S(2)}) %collective-permute-start.20) | collective-permute-done | bytes 243744 | tf_op jit(solution)/shard_map/ppermute | solution.py:476
  161.9 2.7 %shard_map.161 = (bf16[320,448]{1,0:T(8,128)(2,1)}, bf16[448,224]{1,0:T(8,128)(2,1)}) custom-call(bf16[224,544]{1,0:T(8,128)(2,1)} %get-tuple-element.104.a0, bf16[224,544]{1,0:T(8,128)(2,1)} %copy-done.20, bf16[224,544]{1,0:T(8,128)(2,1)} %copy-done.21, bf16[224,544]{1,0:T(8,128)(2,1)} %copy-done.22, bf16[224,544]{1,0:T(8,128)(2,1)} %get-tuple-element.100.b0, ...), custom_call_target="tpu_custom_call" | custom-call | flops 40000000000 | bytes 100000000 | tf_op jit(solution)/shard_map/pallas_call | solution.py:443
  164.6 0.7 convert_reduce_fusion
  (80 shorter events, 8.0 us)
Async XLA Ops:
  0.6 10.7 %copy-start.15 = (f32[1280]{0:T(1024)S(1)}, f32[1280]{0:T(1024)}, u32[]{:S(2)}) copy-start(f32[1280]{0:T(1024)} %param.14) | copy-start | bytes 15364
  0.6 11.3 %copy-start.16 = (f32[1280]{0:T(1024)S(1)}, f32[1280]{0:T(1024)}, u32[]{:S(2)}) copy-start(f32[1280]{0:T(1024)} %param.15) | copy-start | bytes 15364
  0.7 25.4 %collective-permute-start = (bf16[448,5120]{1,0:T(8,128)(2,1)}, bf16[448,5120]{1,0:T(8,128)(2,1)}, u32[]{:S(2)}, u32[]{:S(2)}) collective-permute-start(bf16[448,5120]{1,0:T(8,128)(2,1)} %bitcast.20), channel_id=1, source_target_pairs={{0,1},{1,0},{2,3},{3,2},{4,5},{5,4},{6,7},{7,6},{8,9},{9,8},{10,11... | collective-permute-start | bytes 13762568 | tf_op jit(solution)/shard_map/ppermute | solution.py:521
  0.7 25.3 %collective-permute-start.1 = (bf16[448,3584]{1,0:T(8,128)(2,1)}, bf16[448,3584]{1,0:T(8,128)(2,1)S(1)}, u32[]{:S(2)}, u32[]{:S(2)}) collective-permute-start(bf16[448,3584]{1,0:T(8,128)(2,1)} %out_own.1), channel_id=1, source_target_pairs={{0,1},{1,0},{2,3},{3,2},{4,5},{5,4},{6,7},{7,6},{8,9},{9,8},{10,11... | collective-permute-start | bytes 9633800 | tf_op jit(solution)/shard_map/ppermute | solution.py:521
  4.2 21.9 %all-to-all-start = ((bf16[16,48,448]{2,1,0:T(8,128)(2,1)}), bf16[16,48,448]{2,1,0:T(8,128)(2,1)}, u32[]{:S(2)}, u32[]{:S(2)}) async-start(bf16[16,48,448]{2,1,0:T(8,128)(2,1)} %shard_map.146), calls=%async_computation | async-start | bytes 1572864 | tf_op jit(solution)/shard_map/all_to_all | solution.py:560
  17.2 21.9 %collective-permute-start.5 = (bf16[48,5120]{1,0:T(8,128)(2,1)}, bf16[48,5120]{1,0:T(8,128)(2,1)}, u32[]{:S(2)}, u32[]{:S(2)}) collective-permute-start(bf16[48,5120]{1,0:T(8,128)(2,1)} %get-tuple-element.68.b0), channel_id=1, source_target_pairs={{0,2},{1,3},{2,4},{3,5},{4,6},{5,7},{6,0},{7,1},{8,10},{9,11},{10,... | collective-permute-start | bytes 1474568 | tf_op jit(solution)/shard_map/ppermute | solution.py:526
  19.1 26.4 %collective-permute-start.4 = (bf16[48,5120]{1,0:T(8,128)(2,1)}, bf16[48,5120]{1,0:T(8,128)(2,1)}, u32[]{:S(2)}, u32[]{:S(2)}) collective-permute-start(bf16[48,5120]{1,0:T(8,128)(2,1)} %get-tuple-element.68.b0), channel_id=1, source_target_pairs={{0,4},{1,5},{2,6},{3,7},{4,0},{5,1},{6,2},{7,3},{8,12},{9,13},{10,... | collective-permute-start | bytes 1474568 | tf_op jit(solution)/shard_map/ppermute | solution.py:525
  22.7 22.8 %collective-permute-start.3 = (bf16[48,5120]{1,0:T(8,128)(2,1)}, bf16[48,5120]{1,0:T(8,128)(2,1)}, u32[]{:S(2)}, u32[]{:S(2)}) collective-permute-start(bf16[48,5120]{1,0:T(8,128)(2,1)} %get-tuple-element.68.b0), channel_id=1, source_target_pairs={{0,6},{1,7},{2,0},{3,1},{4,2},{5,3},{6,4},{7,5},{8,14},{9,15},{10,... | collective-permute-start | bytes 1474568 | tf_op jit(solution)/shard_map/ppermute | solution.py:527
  26.1 3.1 %copy-start.8 = (bf16[448,3584]{1,0:T(8,128)(2,1)}, bf16[448,3584]{1,0:T(8,128)(2,1)S(1)}, u32[]{:S(2)}) copy-start(bf16[448,3584]{1,0:T(8,128)(2,1)S(1)} %collective-permute-done.1.out_other) | copy-start | bytes 9633796
  29.1 1.7 collective-permute-start.2
  33.8 25.5 %all-to-all-start.1 = ((bf16[4,192,896]{2,1,0:T(8,128)(2,1)}), bf16[4,192,896]{2,1,0:T(8,128)(2,1)}, u32[]{:S(2)}, u32[]{:S(2)}) async-start(bf16[4,192,896]{2,1,0:T(8,128)(2,1)} %shard_map.149), calls=%async_computation.1 | async-start | bytes 2752512 | tf_op jit(solution)/shard_map/all_to_all | solution.py:532
  39.1 15.8 %copy-start.2 = (bf16[8,24,1280]{2,1,0:T(8,128)(2,1)S(1)}, bf16[8,24,1280]{2,1,0:T(8,128)(2,1)}, u32[]{:S(2)}) copy-start(bf16[8,24,1280]{2,1,0:T(8,128)(2,1)} %param.11) | copy-start | bytes 1474564
  54.8 19.3 %collective-permute-start.6 = (bf16[192,5120]{1,0:T(8,128)(2,1)}, bf16[192,5120]{1,0:T(8,128)(2,1)}, u32[]{:S(2)}, u32[]{:S(2)}) collective-permute-start(bf16[192,5120]{1,0:T(8,128)(2,1)} %get-tuple-element.76.refs_1_), channel_id=1, source_target_pairs={{0,1},{1,0},{2,3},{3,2},{4,5},{5,4},{6,7},{7,6},{8,9},{9,8},{10,11... | collective-permute-start | bytes 5898248 | tf_op jit(solution)/shard_map/ppermute | solution.py:521
  57.4 12.5 %copy-start.5 = (bf16[640,192]{1,0:T(8,128)(2,1)}, bf16[640,192]{1,0:T(8,128)(2,1)S(1)}, u32[]{:S(2)}) copy-start(bf16[640,192]{1,0:T(8,128)(2,1)S(1)} %get-tuple-element.64) | copy-start | bytes 737284
  59.2 14.8 %collective-permute-start.7 = (bf16[4,192,896]{2,1,0:T(8,128)(2,1)}, bf16[4,192,896]{2,1,0:T(8,128)(2,1)}, u32[]{:S(2)}, u32[]{:S(2)}) collective-permute-start(bf16[4,192,896]{2,1,0:T(8,128)(2,1)} %all-to-all-done.1.og.refs_3_), channel_id=1, source_target_pairs={{0,1},{1,0},{2,3},{3,2},{4,5},{5,4},{6,7},{7,6},{8,9},{9,8},{10,11... | collective-permute-start | bytes 4128776 | tf_op jit(solution)/shard_map/ppermute | solution.py:521
  69.9 4.2 %collective-permute-start.8 = (bf16[896,192]{1,0:T(8,128)(2,1)}, bf16[896,192]{1,0:T(8,128)(2,1)S(1)}, u32[]{:S(2)}, u32[]{:S(2)}) collective-permute-start(bf16[896,192]{1,0:T(8,128)(2,1)} %get-tuple-element.80), channel_id=1, source_target_pairs={{0,1},{1,0},{2,3},{3,2},{4,5},{5,4},{6,7},{7,6},{8,9},{9,8},{10,11... | collective-permute-start | bytes 1032200 | tf_op jit(solution)/shard_map/ppermute | solution.py:521
  70.4 33.3 %all-to-all-start.2 = ((bf16[4,48,5120]{2,1,0:T(8,128)(2,1)}), bf16[4,48,5120]{2,1,0:T(8,128)(2,1)S(1)}, u32[]{:S(2)}, u32[]{:S(2)}) async-start(bf16[4,48,5120]{2,1,0:T(8,128)(2,1)} %bitcast.23), calls=%async_computation.2 | async-start | bytes 3932160 | tf_op jit(solution)/shard_map/all_to_all | solution.py:532
  80.9 18.0 %collective-permute-start.9 = (bf16[112,2176]{1,0:T(8,128)(2,1)}, bf16[112,2176]{1,0:T(8,128)(2,1)S(1)}, u32[]{:S(2)}, u32[]{:S(2)}) collective-permute-start(bf16[112,2176]{1,0:T(8,128)(2,1)} %get-tuple-element.81), channel_id=1, source_target_pairs={{0,8},{8,16},{16,24},{24,0},{32,40},{40,48},{48,56},{56,32},{64,72... | collective-permute-start | bytes 1462280 | tf_op jit(solution)/shard_map/ppermute | solution.py:592
  82.4 16.5 %collective-permute-start.10 = (bf16[112,2176]{1,0:T(8,128)(2,1)}, bf16[112,2176]{1,0:T(8,128)(2,1)S(1)}, u32[]{:S(2)}, u32[]{:S(2)}) collective-permute-start(bf16[112,2176]{1,0:T(8,128)(2,1)} %get-tuple-element.87), channel_id=1, source_target_pairs={{0,24},{8,0},{16,8},{24,16},{32,56},{40,32},{48,40},{56,48},{64,88... | collective-permute-start | bytes 1462280 | tf_op jit(solution)/shard_map/ppermute | solution.py:593
  84.2 14.8 %collective-permute-start.11 = (bf16[112,2176]{1,0:T(8,128)(2,1)}, bf16[112,2176]{1,0:T(8,128)(2,1)S(1)}, u32[]{:S(2)}, u32[]{:S(2)}) collective-permute-start(bf16[112,2176]{1,0:T(8,128)(2,1)} %get-tuple-element.88), channel_id=1, source_target_pairs={{0,32},{8,40},{16,48},{24,56},{32,64},{40,72},{48,80},{56,88},{64,... | collective-permute-start | bytes 1462280 | tf_op jit(solution)/shard_map/ppermute | solution.py:594
  85.8 13.2 %collective-permute-start.12 = (bf16[112,2176]{1,0:T(8,128)(2,1)}, bf16[112,2176]{1,0:T(8,128)(2,1)S(1)}, u32[]{:S(2)}, u32[]{:S(2)}) collective-permute-start(bf16[112,2176]{1,0:T(8,128)(2,1)} %get-tuple-element.89), channel_id=1, source_target_pairs={{0,96},{8,104},{16,112},{24,120},{32,0},{40,8},{48,16},{56,24},{64... | collective-permute-start | bytes 1462280 | tf_op jit(solution)/shard_map/ppermute | solution.py:595
  98.9 0.9 copy-start.11
  99.0 1.1 copy-start.12
  99.0 1.2 copy-start.9
  100.2 6.8 %copy-start.3 = (f32[1,1280]{1,0:T(1,128)S(1)}, f32[1,1280]{1,0:T(1,128)}, u32[]{:S(2)}) copy-start(f32[1,1280]{1,0:T(1,128)} %reshape.232.gain) | copy-start | bytes 15364
  100.2 6.8 %copy-start.4 = (f32[192,1280]{1,0:T(8,128)S(1)}, f32[192,1280]{1,0:T(8,128)}, u32[]{:S(2)}) copy-start(f32[192,1280]{1,0:T(8,128)} %get-tuple-element.92.normed) | copy-start | bytes 2949124
  100.2 6.8 %copy-start.7 = (f32[192,128]{1,0:T(8,128)S(1)}, f32[192,128]{1,0:T(8,128)}, u32[]{:S(2)}) copy-start(f32[192,128]{1,0:T(8,128)} %get-tuple-element.93.inverse) | copy-start | bytes 294916
  103.8 23.9 %collective-permute-start.15 = (bf16[224,2176]{1,0:T(8,128)(2,1)}, bf16[224,2176]{1,0:T(8,128)(2,1)}, u32[]{:S(2)}, u32[]{:S(2)}) collective-permute-start(bf16[224,2176]{1,0:T(8,128)(2,1)} %get-tuple-element.98), channel_id=1, source_target_pairs={{0,32},{8,40},{16,48},{24,56},{32,64},{40,72},{48,80},{56,88},{64,... | collective-permute-start | bytes 2924552 | tf_op jit(solution)/shard_map/ppermute | solution.py:611
  104.2 23.5 %collective-permute-start.16 = (bf16[224,2176]{1,0:T(8,128)(2,1)}, bf16[224,2176]{1,0:T(8,128)(2,1)}, u32[]{:S(2)}, u32[]{:S(2)}) collective-permute-start(bf16[224,2176]{1,0:T(8,128)(2,1)} %get-tuple-element.99), channel_id=1, source_target_pairs={{0,96},{8,104},{16,112},{24,120},{32,0},{40,8},{48,16},{56,24},{64... | collective-permute-start | bytes 2924552 | tf_op jit(solution)/shard_map/ppermute | solution.py:611
  107.0 1.5 copy-start.6
  108.5 3.8 %collective-permute-start.14 = (bf16[192,1280]{1,0:T(8,128)(2,1)}, bf16[192,1280]{1,0:T(8,128)(2,1)S(1)}, u32[]{:S(2)}, u32[]{:S(2)}) collective-permute-start(bf16[192,1280]{1,0:T(8,128)(2,1)} %shard_map.156.grad), channel_id=1, source_target_pairs={{0,1},{1,0},{2,3},{3,2},{4,5},{5,4},{6,7},{7,6},{8,9},{9,8},{10,11... | collective-permute-start | bytes 1474568 | tf_op jit(solution)/shard_map/ppermute | solution.py:521
  108.5 2.2 %collective-permute-start.13 = (bf16[640,192]{1,0:T(8,128)(2,1)S(1)}, bf16[640,192]{1,0:T(8,128)(2,1)S(1)}, u32[]{:S(2)}, u32[]{:S(2)}) collective-permute-start(bf16[640,192]{1,0:T(8,128)(2,1)S(1)} %copy-done.6), channel_id=1, source_target_pairs={{0,1},{1,0},{2,3},{3,2},{4,5},{5,4},{6,7},{7,6},{8,9},{9,8},{10,11... | collective-permute-start | bytes 737288 | tf_op jit(solution)/shard_map/ppermute | solution.py:521
  109.1 26.7 %collective-permute-start.17 = (bf16[224,2176]{1,0:T(8,128)(2,1)}, bf16[224,2176]{1,0:T(8,128)(2,1)S(1)}, u32[]{:S(2)}, u32[]{:S(2)}) collective-permute-start(bf16[224,2176]{1,0:T(8,128)(2,1)} %get-tuple-element.90), channel_id=1, source_target_pairs={{0,8},{8,16},{16,24},{24,0},{32,40},{40,48},{48,56},{56,32},{64,72... | collective-permute-start | bytes 2924552 | tf_op jit(solution)/shard_map/ppermute | solution.py:613
  110.7 25.0 %collective-permute-start.18 = (bf16[224,2176]{1,0:T(8,128)(2,1)}, bf16[224,2176]{1,0:T(8,128)(2,1)}, u32[]{:S(2)}, u32[]{:S(2)}) collective-permute-start(bf16[224,2176]{1,0:T(8,128)(2,1)} %get-tuple-element.103), channel_id=1, source_target_pairs={{0,24},{8,0},{16,8},{24,16},{32,56},{40,32},{48,40},{56,48},{64,88... | collective-permute-start | bytes 2924552 | tf_op jit(solution)/shard_map/ppermute | solution.py:613
  112.3 1.0 copy-start
  116.7 4.9 %copy-start.1 = (bf16[192,1280]{1,0:T(8,128)(2,1)S(1)}, bf16[192,1280]{1,0:T(8,128)(2,1)}, u32[]{:S(2)}) copy-start(bf16[192,1280]{1,0:T(8,128)(2,1)} %shard_map.156.grad) | copy-start | bytes 1474564
  116.7 30.4 %all-to-all-start.3 = ((bf16[4,160,1280]{2,1,0:T(8,128)(2,1)}), bf16[4,160,1280]{2,1,0:T(8,128)(2,1)S(1)}, u32[]{:S(2)}, u32[]{:S(2)}) async-start(bf16[4,160,1280]{2,1,0:T(8,128)(2,1)} %bitcast.13), calls=%async_computation.3 | async-start | bytes 3276800 | tf_op jit(solution)/shard_map/all_to_all | solution.py:532
  131.7 14.5 %collective-permute-start.22 = (bf16[224,544]{1,0:T(8,128)(2,1)}, bf16[224,544]{1,0:T(8,128)(2,1)S(1)}, u32[]{:S(2)}, u32[]{:S(2)}) collective-permute-start(bf16[224,544]{1,0:T(8,128)(2,1)} %get-tuple-element.108), channel_id=1, source_target_pairs={{0,8},{8,16},{16,24},{24,0},{32,40},{40,48},{48,56},{56,32},{64,72... | collective-permute-start | bytes 731144 | tf_op jit(solution)/shard_map/ppermute | solution.py:475
  132.1 20.2 %collective-permute-start.23 = (bf16[224,544]{1,0:T(8,128)(2,1)}, bf16[224,544]{1,0:T(8,128)(2,1)S(1)}, u32[]{:S(2)}, u32[]{:S(2)}) collective-permute-start(bf16[224,544]{1,0:T(8,128)(2,1)} %get-tuple-element.109), channel_id=1, source_target_pairs={{0,24},{8,0},{16,8},{24,16},{32,56},{40,32},{48,40},{56,48},{64,88... | collective-permute-start | bytes 731144 | tf_op jit(solution)/shard_map/ppermute | solution.py:476
  135.0 17.4 %collective-permute-start.24 = (bf16[224,544]{1,0:T(8,128)(2,1)}, bf16[224,544]{1,0:T(8,128)(2,1)}, u32[]{:S(2)}, u32[]{:S(2)}) collective-permute-start(bf16[224,544]{1,0:T(8,128)(2,1)} %get-tuple-element.110), channel_id=1, source_target_pairs={{0,16},{8,24},{16,0},{24,8},{32,48},{40,56},{48,32},{56,40},{64,80... | collective-permute-start | bytes 731144 | tf_op jit(solution)/shard_map/ppermute | solution.py:474
  135.7 0.9 copy-start.17
  140.5 13.2 %collective-permute-start.19 = (bf16[224,544]{1,0:T(8,128)(2,1)}, bf16[224,544]{1,0:T(8,128)(2,1)S(1)}, u32[]{:S(2)}, u32[]{:S(2)}) collective-permute-start(bf16[224,544]{1,0:T(8,128)(2,1)} %get-tuple-element.105), channel_id=1, source_target_pairs={{0,32},{8,40},{16,48},{24,56},{32,64},{40,72},{48,80},{56,88},{64,... | collective-permute-start | bytes 731144 | tf_op jit(solution)/shard_map/ppermute | solution.py:475
  140.7 20.4 %collective-permute-start.20 = (bf16[224,544]{1,0:T(8,128)(2,1)}, bf16[224,544]{1,0:T(8,128)(2,1)S(1)}, u32[]{:S(2)}, u32[]{:S(2)}) collective-permute-start(bf16[224,544]{1,0:T(8,128)(2,1)} %get-tuple-element.106), channel_id=1, source_target_pairs={{0,96},{8,104},{16,112},{24,120},{32,0},{40,8},{48,16},{56,24},{64... | collective-permute-start | bytes 731144 | tf_op jit(solution)/shard_map/ppermute | solution.py:476
  146.3 14.8 %copy-start.18 = (bf16[224,544]{1,0:T(8,128)(2,1)}, bf16[224,544]{1,0:T(8,128)(2,1)S(1)}, u32[]{:S(2)}) copy-start(bf16[224,544]{1,0:T(8,128)(2,1)S(1)} %collective-permute-done.22.b1) | copy-start | bytes 731140
  146.3 14.8 %collective-permute-start.21 = (bf16[224,544]{1,0:T(8,128)(2,1)}, bf16[224,544]{1,0:T(8,128)(2,1)S(1)}, u32[]{:S(2)}, u32[]{:S(2)}) collective-permute-start(bf16[224,544]{1,0:T(8,128)(2,1)} %get-tuple-element.107), channel_id=1, source_target_pairs={{0,64},{8,72},{16,80},{24,88},{32,96},{40,104},{48,112},{56,120},{... | collective-permute-start | bytes 731144 | tf_op jit(solution)/shard_map/ppermute | solution.py:474
  148.3 16.3 %all-to-all-start.4 = ((bf16[16,16,1280]{2,1,0:T(8,128)(2,1)}), bf16[16,16,1280]{2,1,0:T(8,128)(2,1)S(1)}, u32[]{:S(2)}, u32[]{:S(2)}) async-start(bf16[16,16,1280]{2,1,0:T(8,128)(2,1)} %shard_map.159), calls=%async_computation.4 | async-start | bytes 1310720 | tf_op jit(solution)/shard_map/all_to_all | solution.py:617
  152.3 8.8 %copy-start.19 = (bf16[224,544]{1,0:T(8,128)(2,1)}, bf16[224,544]{1,0:T(8,128)(2,1)S(1)}, u32[]{:S(2)}) copy-start(bf16[224,544]{1,0:T(8,128)(2,1)S(1)} %collective-permute-done.23.b2) | copy-start | bytes 731140
  153.7 7.4 %copy-start.20 = (bf16[224,544]{1,0:T(8,128)(2,1)}, bf16[224,544]{1,0:T(8,128)(2,1)S(1)}, u32[]{:S(2)}) copy-start(bf16[224,544]{1,0:T(8,128)(2,1)S(1)} %collective-permute-done.19.a1) | copy-start | bytes 731140
  (5 other events, 3.8 us)

commit v5 on v4

--- a/solution.py
+++ b/solution.py
@@ -59,9 +59,9 @@
 LONG = pl.CostEstimate(flops=40_000_000_000, bytes_accessed=100_000_000, transcendentals=1_000_000)
 
 
-def parcel_kernel(ids, offsets, frames, owner, grad_t, out):
+def parcel_kernel(offsets, frames, owner, grad_t, out):
     out[...] = jnp.zeros_like(out)
-    s = ids[4]
+    s = lax.axis_index("seq")
     row, col = iota((48, 384), 0), iota((48, 384), 1)
     picks, dests = [], []
     for k in range(8):
@@ -75,15 +75,15 @@
         out[dests[k]] = tokens[k * 48 : k * 48 + 48]
 
 
-def parcels_of(ids, offsets, frames, owner, grad_t):
+def parcels_of(offsets, frames, owner, grad_t):
     return pl.pallas_call(
         parcel_kernel,
         out_shape=struct((16, 48, 448), BF16),
-        in_specs=[SMEM, SMEM, SMEM, SMEM, VMEM],
+        in_specs=[SMEM, SMEM, SMEM, VMEM],
         out_specs=VMEM,
         compiler_params=PARAMS,
         cost_estimate=HINT,
-    )(ids, offsets, frames, owner, grad_t)
+    )(offsets, frames, owner, grad_t)
 
 
 def select_kernel(ids, owner, arrived, keep, give):
@@ -226,11 +226,11 @@
             struct((448, 192), F32),
             struct((448, 192), F32),
         ),
-        grid=(5,),
+        grid=(2,),
         in_specs=[SMEM]
-        + [pl.BlockSpec((48, 1024), lambda i: (0, i))] * 4
-        + [pl.BlockSpec((448, 1024), lambda i: (0, i))] * 2,
-        out_specs=(pl.BlockSpec((192, 1024), lambda i: (0, i)),) + (whole((448, 192)),) * 4,
+        + [pl.BlockSpec((48, 2560), lambda i: (0, i))] * 4
+        + [pl.BlockSpec((448, 2560), lambda i: (0, i))] * 2,
+        out_specs=(pl.BlockSpec((192, 2560), lambda i: (0, i)),) + (whole((448, 192)),) * 4,
         scratch_shapes=[pltpu.VMEM((448, 192), F32)] * 2,
         compiler_params=PARAMS,
         cost_estimate=HINT,
@@ -424,8 +424,9 @@
     return pl.pallas_call(
         spread_kernel,
         out_shape=(struct((224, 544), BF16),) * 4,
-        in_specs=[SMEM] + [VMEM] * 3,
-        out_specs=(VMEM,) * 4,
+        grid=(2,),
+        in_specs=[SMEM] + [pl.BlockSpec((112, 2176), lambda i: (i, 0))] * 3,
+        out_specs=(pl.BlockSpec((112, 544), lambda i: (i, 0)),) * 4,
         compiler_params=PARAMS,
         cost_estimate=LONG,
     )(where, *parts)
@@ -556,7 +557,7 @@
     in_other = swap(in_own)
     out_other = swap(adapter_out)
 
-    parcels = parcels_of(ids, group_offsets, group_frames, group_owner, emb_grad.T)
+    parcels = parcels_of(group_offsets, group_frames, group_owner, emb_grad.T)
     arrived = lax.all_to_all(parcels, "seq", split_axis=0, concat_axis=0, tiled=True)
     context, _ = lax.optimization_barrier((context, parcels))
     stacked_here, normed, inverse = encode_of(context, residual_in, out_weight, final_norm_weight, final_norm_bias)

time: 167 us -> 166 us (level)
  Pallas kernels: 72.4 us -> 69.7 us
  transfers between devices with their start and end apart: 30 -> 30, of which waited for: 9 -> 9; matrix products, arithmetic and copies ran while one was open for 4% -> 4% of each run, Pallas kernels for 44% -> 42%
where the time goes in v5:
time: 166 us; the launch traced here: 164 us
  Pallas kernels  69.7 us (42%)
  starting transfers between devices  53.2 us (32%)
  waiting for transfers between devices  28.2 us (17%)
  local copies, waits for them, and re-layouts  7.32 us (4%)
  matrix products  3.93 us (2%)
    pallas_call x2, Pallas kernels, weight_grads_of(): pl.pallas_call(kernel, out_shape=tuple((struct(shape, BF16) for shape in...  17.6 us
    all_to_all x3, starting transfers between devices, z_exchange(): lax.all_to_all(parts, 'tp', split_axis=0, concat_axis=0, axis_index_group...  13.8 us
    pallas_call x1, Pallas kernels, pre_grad_of(): pl.pallas_call(pre_grad_kernel, out_shape=(struct((192, 5120), BF16), str...  10.6 us
    ppermute x2, waiting for transfers between devices, ring_of(): down = lax.ppermute(parts[3], 'seq', shift(-1))  8.25 us
    pallas_call x1, Pallas kernels, preact_of(): pl.pallas_call(preact_kernel, out_shape=(struct((192, 5120), BF16), struc...  7.66 us
    all_to_all x1, starting transfers between devices, per_device(): lax.all_to_all(parcels, 'seq', split_axis=0, concat_axis=0, tiled=True)  7.16 us
    pallas_call x2, Pallas kernels, spread_of(): pl.pallas_call(spread_kernel, out_shape=(struct((224, 544), BF16),) * 4,...  6.71 us
    ppermute x1, waiting for transfers between devices, z_blocks(): far = lax.ppermute(block, 'tp', z_shift(2))  6.47 us
  transfers between devices with their start and end apart: 30, of which 9 were waited for; matrix products, arithmetic and copies ran while one was open for 4% of the time, Pallas kernels for 42%

profile of v5, /device:TPU:0, one launch (start us, length us, event | category | flops | bytes accessed | tf_op | source)
XLA Modules:
  0.0 164.2 jit_solution(16919249148964849498)
XLA Ops:
  1.2 2.3 %shard_map.146 = bf16[16,48,448]{2,1,0:T(8,128)(2,1)} custom-call(s32[128]{0:T(128)} %offsets.1, s32[128]{0:T(128)} %frames.1, s32[128]{0:T(128)} %owner.1, bf16[448,384]{1,0:T(8,128)(2,1)} %bitcast.26), custom_call_target="tpu_custom_call" | custom-call | flops 1 | bytes 1 | tf_op jit(solution)/shard_map/pallas_call | solution.py:79
  3.5 7.2 %all-to-all-start = ((bf16[16,48,448]{2,1,0:T(8,128)(2,1)}), bf16[16,48,448]{2,1,0:T(8,128)(2,1)}, u32[]{:S(2)}, u32[]{:S(2)}) async-start(bf16[16,48,448]{2,1,0:T(8,128)(2,1)} %shard_map.146), calls=%async_computation | async-start | bytes 1572864 | tf_op jit(solution)/shard_map/all_to_all | solution.py:561
  11.9 4.7 %shard_map.147 = (bf16[48,5120]{1,0:T(8,128)(2,1)}, f32[192,1280]{1,0:T(8,128)}, f32[192,128]{1,0:T(8,128)}) custom-call(bf16[192,1280]{1,0:T(8,128)(2,1)} %bitcast.18, bf16[192,1280]{1,0:T(8,128)(2,1)} %bitcast.24, bf16[1280,1280]{1,0:T(8,128)(2,1)} %weight.1, f32[1,1280]{1,0:T(1,128)} %reshape.232.gain, f32[1,1280]{1,0:T(1,128)} %reshape.233.bias), custom_call_target="tpu_custom_call" | custom-call | flops 1 | bytes 1 | tf_op jit(solution)/shard_map/pallas_call | solution.py:156
  16.6 1.9 %collective-permute-start.5 = (bf16[48,5120]{1,0:T(8,128)(2,1)}, bf16[48,5120]{1,0:T(8,128)(2,1)}, u32[]{:S(2)}, u32[]{:S(2)}) collective-permute-start(bf16[48,5120]{1,0:T(8,128)(2,1)} %get-tuple-element.68.b0), channel_id=1, source_target_pairs={{0,2},{1,3},{2,4},{3,5},{4,6},{5,7},{6,0},{7,1},{8,10},{9,11},{10,... | collective-permute-start | bytes 1474568 | tf_op jit(solution)/shard_map/ppermute | solution.py:527
  18.5 3.6 %collective-permute-start.4 = (bf16[48,5120]{1,0:T(8,128)(2,1)}, bf16[48,5120]{1,0:T(8,128)(2,1)}, u32[]{:S(2)}, u32[]{:S(2)}) collective-permute-start(bf16[48,5120]{1,0:T(8,128)(2,1)} %get-tuple-element.68.b0), channel_id=1, source_target_pairs={{0,4},{1,5},{2,6},{3,7},{4,0},{5,1},{6,2},{7,3},{8,12},{9,13},{10,... | collective-permute-start | bytes 1474568 | tf_op jit(solution)/shard_map/ppermute | solution.py:526
  22.1 1.0 collective-permute-start.3
  23.7 1.6 all-to-all-done.arrived
  25.4 3.1 %shard_map.148 = (bf16[192,448]{1,0:T(8,128)(2,1)}, bf16[192,448]{1,0:T(8,128)(2,1)}) custom-call(s32[5]{0:T(128)} %stack.23.ids.refs_0_, s32[1,128]{1,0:T(1,128)} %bitcast.28, bf16[16,48,448]{2,1,0:T(8,128)(2,1)} %all-to-all-done.arrived), custom_call_target="tpu_custom_call" | custom-call | flops 1 | bytes 1 | tf_op jit(solution)/shard_map/pallas_call | solution.py:109
  28.6 1.5 collective-permute-done.2.got
  30.8 2.3 %shard_map.149 = bf16[4,192,896]{2,1,0:T(8,128)(2,1)} custom-call(s32[5]{0:T(128)} %stack.23.ids.refs_0_, bf16[192,448]{1,0:T(8,128)(2,1)} %get-tuple-element.62.keep, bf16[192,448]{1,0:T(8,128)(2,1)} %copy-done.14), custom_call_target="tpu_custom_call" | custom-call | flops 1 | bytes 1 | tf_op jit(solution)/shard_map/pallas_call | solution.py:129
  33.1 5.3 %all-to-all-start.1 = ((bf16[4,192,896]{2,1,0:T(8,128)(2,1)}), bf16[4,192,896]{2,1,0:T(8,128)(2,1)}, u32[]{:S(2)}, u32[]{:S(2)}) async-start(bf16[4,192,896]{2,1,0:T(8,128)(2,1)} %shard_map.149), calls=%async_computation.1 | async-start | bytes 2752512 | tf_op jit(solution)/shard_map/all_to_all | solution.py:533
  38.4 6.5 %collective-permute-done.4.b2 = bf16[48,5120]{1,0:T(8,128)(2,1)} collective-permute-done((bf16[48,5120]{1,0:T(8,128)(2,1)}, bf16[48,5120]{1,0:T(8,128)(2,1)}, u32[]{:S(2)}, u32[]{:S(2)}) %collective-permute-start.4) | collective-permute-done | bytes 491552 | tf_op jit(solution)/shard_map/ppermute | solution.py:526
  44.9 7.7 %shard_map.151 = (bf16[192,5120]{1,0:T(8,128)(2,1)}, bf16[448,192]{1,0:T(8,128)(2,1)}, bf16[448,192]{1,0:T(8,128)(2,1)}, f32[448,192]{1,0:T(8,128)}, f32[448,192]{1,0:T(8,128)}) custom-call(s32[5]{0:T(128)} %stack.23.ids.refs_0_, bf16[48,5120]{1,0:T(8,128)(2,1)} %get-tuple-element.68.b0, bf16[48,5120]{1,0:T(8,128)(2,1)} %collective-permute-done.3.b1, ...), custom_call_target="tpu_custom_call" | custom-call | flops 1 | bytes 1 | tf_op jit(solution)/shard_map/pallas_call | solution.py:220
  52.7 2.5 %shard_map.150 = (bf16[640,192]{1,0:T(8,128)(2,1)S(1)}, bf16[640,192]{1,0:T(8,128)(2,1)S(1)}) custom-call(s32[1,1280]{1,0:T(1,128)S(1)} %fusion.1.target.target_other, s32[1,1280]{1,0:T(1,128)S(1)} %fusion.1.target.target_other, bf16[192,1280]{1,0:T(8,128)(2,1)S(1)} %bitcast.19), custom_call_target="tpu_custom_call" | custom-call | flops 40000000000 | bytes 100000000 | tf_op jit(solution)/shard_map/pallas_call | solution.py:489
  55.2 3.4 %all-to-all-done.1.og.refs_3_ = bf16[4,192,896]{2,1,0:T(8,128)(2,1)} async-done(((bf16[4,192,896]{2,1,0:T(8,128)(2,1)}), bf16[4,192,896]{2,1,0:T(8,128)(2,1)}, u32[]{:S(2)}, u32[]{:S(2)}) %all-to-all-start.1) | async-done | bytes 1376288 | tf_op jit(solution)/shard_map/all_to_all | solution.py:533
  58.6 10.6 %shard_map.152 = (bf16[192,5120]{1,0:T(8,128)(2,1)}, bf16[448,192]{1,0:T(8,128)(2,1)}, bf16[896,192]{1,0:T(8,128)(2,1)}) custom-call(bf16[4,192,896]{2,1,0:T(8,128)(2,1)} %all-to-all-done.1.og.refs_3_, bf16[448,3584]{1,0:T(8,128)(2,1)} %out_own.1, bf16[448,3584]{1,0:T(8,128)(2,1)} %copy-done.8, bf16[448,5120]{1,0:T(8,128)(2,1)} %bitcast.22, ...), custom_call_target="tpu_custom_call" | custom-call | flops 1 | bytes 1 | tf_op jit(solution)/shard_map/pallas_call | solution.py:294
  69.8 3.6 %all-to-all-start.2 = ((bf16[4,48,5120]{2,1,0:T(8,128)(2,1)}), bf16[4,48,5120]{2,1,0:T(8,128)(2,1)S(1)}, u32[]{:S(2)}, u32[]{:S(2)}) async-start(bf16[4,48,5120]{2,1,0:T(8,128)(2,1)} %bitcast.23), calls=%async_computation.2 | async-start | bytes 3932160 | tf_op jit(solution)/shard_map/all_to_all | solution.py:533
  73.4 0.7 copy-done.13
  74.2 6.1 %shard_map.153 = (bf16[112,2176]{1,0:T(8,128)(2,1)}, bf16[112,2176]{1,0:T(8,128)(2,1)}, bf16[112,2176]{1,0:T(8,128)(2,1)}, bf16[112,2176]{1,0:T(8,128)(2,1)}) custom-call(s32[5]{0:T(128)} %stack.23.ids.refs_0_, bf16[192,5120]{1,0:T(8,128)(2,1)} %get-tuple-element.76.refs_1_, bf16[192,5120]{1,0:T(8,128)(2,1)} %collective-permute-done.6.refs_2_, ...), custom_call_target="tpu_custom_call" | custom-call | flops 1 | bytes 1 | tf_op jit(solution)/shard_map/pallas_call | solution.py:373
  80.3 1.5 collective-permute-start.9
  81.7 1.8 %collective-permute-start.10 = (bf16[112,2176]{1,0:T(8,128)(2,1)}, bf16[112,2176]{1,0:T(8,128)(2,1)S(1)}, u32[]{:S(2)}, u32[]{:S(2)}) collective-permute-start(bf16[112,2176]{1,0:T(8,128)(2,1)} %get-tuple-element.87), channel_id=1, source_target_pairs={{0,24},{8,0},{16,8},{24,16},{32,56},{40,32},{48,40},{56,48},{64,88... | collective-permute-start | bytes 1462280 | tf_op jit(solution)/shard_map/ppermute | solution.py:594
  83.5 1.6 collective-permute-start.11
  85.1 1.6 collective-permute-start.12
  86.7 11.5 %shard_map.154 = (bf16[224,2176]{1,0:T(8,128)(2,1)}, bf16[224,2176]{1,0:T(8,128)(2,1)}, bf16[224,2176]{1,0:T(8,128)(2,1)}, bf16[224,2176]{1,0:T(8,128)(2,1)}, bf...) custom-call(s32[5]{0:T(128)} %stack.23.ids.refs_0_, bf16[192,5120]{1,0:T(8,128)(2,1)} %get-tuple-element.76.refs_1_, ...), custom_call_target="tpu_custom_call" | custom-call | flops 40000000000 | bytes 100000000 | tf_op jit(solution)/shard_map/pallas_call | solution.py:373
  98.3 0.7 copy-done.10
  99.5 3.6 %shard_map.155 = (bf16[224,2176]{1,0:T(8,128)(2,1)}, bf16[224,2176]{1,0:T(8,128)(2,1)}, bf16[224,2176]{1,0:T(8,128)(2,1)}, bf16[224,2176]{1,0:T(8,128)(2,1)}) custom-call(bf16[224,2176]{1,0:T(8,128)(2,1)} %get-tuple-element.83.x_up, ...), custom_call_target="tpu_custom_call", output_to_operand_aliasing={{0}: (0, {}), {1}: (1, {}), {2}: (2, {}), {3}: (3, {})} | custom-call | flops 1 | bytes 1 | tf_op jit(solution)/shard_map/pallas_call | solution.py:397
  103.6 2.8 %collective-permute-start.16 = (bf16[224,2176]{1,0:T(8,128)(2,1)}, bf16[224,2176]{1,0:T(8,128)(2,1)}, u32[]{:S(2)}, u32[]{:S(2)}) collective-permute-start(bf16[224,2176]{1,0:T(8,128)(2,1)} %get-tuple-element.99), channel_id=1, source_target_pairs={{0,96},{8,104},{16,112},{24,120},{32,0},{40,8},{48,16},{56,24},{64... | collective-permute-start | bytes 2924552 | tf_op jit(solution)/shard_map/ppermute | solution.py:612
  106.4 1.5 shard_map.156.grad
  108.8 1.3 collective-permute-done.13.ctx_other
  110.0 1.6 collective-permute-start.18
  111.7 1.0 copy-done
  112.7 3.4 %shard_map.157 = bf16[640,1280]{1,0:T(8,128)(2,1)} custom-call(bf16[640,192]{1,0:T(8,128)(2,1)S(1)} %get-tuple-element.94.ctx, bf16[640,192]{1,0:T(8,128)(2,1)S(1)} %collective-permute-done.13.ctx_other, bf16[192,1280]{1,0:T(8,128)(2,1)S(1)} %copy-done, bf16[192,1280]{1,0:T(8,128)(2,1)S(1)} %collective-permute-done.14.grad_other), custom_call_target="tpu_custom_call" | custom-call | flops 1 | bytes 1 | tf_op jit(solution)/shard_map/pallas_call | solution.py:510
  116.1 4.9 %all-to-all-start.3 = ((bf16[4,160,1280]{2,1,0:T(8,128)(2,1)}), bf16[4,160,1280]{2,1,0:T(8,128)(2,1)S(1)}, u32[]{:S(2)}, u32[]{:S(2)}) async-start(bf16[4,160,1280]{2,1,0:T(8,128)(2,1)} %bitcast.13), calls=%async_computation.3 | async-start | bytes 3276800 | tf_op jit(solution)/shard_map/all_to_all | solution.py:533
  120.9 3.9 %convolution_convert_fusion = bf16[192,1280]{1,0:T(8,128)(2,1)} fusion(bf16[192,1280]{1,0:T(8,128)(2,1)S(1)} %copy-done.1, bf16[1280,1280]{1,0:T(8,128)(2,1)} %weight.1), kind=kOutput, calls=%fused_computation | convolution fusion | flops 629391360 | bytes 4259840 | tf_op jit(solution)/shard_map/dot_general | solution.py:39
  124.9 2.1 %collective-permute-done.15.b = bf16[224,2176]{1,0:T(8,128)(2,1)} collective-permute-done((bf16[224,2176]{1,0:T(8,128)(2,1)}, bf16[224,2176]{1,0:T(8,128)(2,1)}, u32[]{:S(2)}, u32[]{:S(2)}) %collective-permute-start.15) | collective-permute-done | bytes 974880 | tf_op jit(solution)/shard_map/ppermute | solution.py:612
  127.0 3.4 %shard_map.158 = (bf16[224,544]{1,0:T(8,128)(2,1)}, bf16[224,544]{1,0:T(8,128)(2,1)}, bf16[224,544]{1,0:T(8,128)(2,1)}, bf16[224,544]{1,0:T(8,128)(2,1)}) custom-call(s32[1]{0:T(128)} %bitcast.1.where, bf16[224,2176]{1,0:T(8,128)(2,1)} %get-tuple-element.97.a, bf16[224,2176]{1,0:T(8,128)(2,1)} %collective-permute-done.15.b, ...), custom_call_target="tpu_custom_call" | custom-call | flops 40000000000 | bytes 100000000 | tf_op jit(solution)/shard_map/pallas_call | solution.py:424
  131.0 2.8 %collective-permute-start.23 = (bf16[224,544]{1,0:T(8,128)(2,1)}, bf16[224,544]{1,0:T(8,128)(2,1)S(1)}, u32[]{:S(2)}, u32[]{:S(2)}) collective-permute-start(bf16[224,544]{1,0:T(8,128)(2,1)} %get-tuple-element.109), channel_id=1, source_target_pairs={{0,24},{8,0},{16,8},{24,16},{32,56},{40,32},{48,40},{56,48},{64,88... | collective-permute-start | bytes 731144 | tf_op jit(solution)/shard_map/ppermute | solution.py:477
  133.8 0.7 collective-permute-start.24
  134.8 0.9 copy-done.17
  135.7 3.3 %shard_map.160 = (bf16[224,544]{1,0:T(8,128)(2,1)}, bf16[224,544]{1,0:T(8,128)(2,1)}, bf16[224,544]{1,0:T(8,128)(2,1)}, bf16[224,544]{1,0:T(8,128)(2,1)}) custom-call(s32[1]{0:T(128)} %bitcast.where, bf16[224,2176]{1,0:T(8,128)(2,1)} %get-tuple-element.102.a, bf16[224,2176]{1,0:T(8,128)(2,1)} %copy-done.17, bf16[224,2176]{1,0:T(8,128)(2,1)} %collective-permute-done.18.c), custom_call_target="tpu_custom_call" | custom-call | flops 40000000000 | bytes 100000000 | tf_op jit(solution)/shard_map/pallas_call | solution.py:424
  139.1 3.2 %collective-permute-start.20 = (bf16[224,544]{1,0:T(8,128)(2,1)}, bf16[224,544]{1,0:T(8,128)(2,1)S(1)}, u32[]{:S(2)}, u32[]{:S(2)}) collective-permute-start(bf16[224,544]{1,0:T(8,128)(2,1)} %get-tuple-element.106), channel_id=1, source_target_pairs={{0,96},{8,104},{16,112},{24,120},{32,0},{40,8},{48,16},{56,24},{64... | collective-permute-start | bytes 731144 | tf_op jit(solution)/shard_map/ppermute | solution.py:477
  142.3 3.3 %collective-permute-done.22.b1 = bf16[224,544]{1,0:T(8,128)(2,1)S(1)} collective-permute-done((bf16[224,544]{1,0:T(8,128)(2,1)}, bf16[224,544]{1,0:T(8,128)(2,1)S(1)}, u32[]{:S(2)}, u32[]{:S(2)}) %collective-permute-start.22) | collective-permute-done | bytes 243744 | tf_op jit(solution)/shard_map/ppermute | solution.py:476
  145.6 0.7 collective-permute-start.21
  146.3 1.1 shard_map.159
  147.4 4.2 %all-to-all-start.4 = ((bf16[16,16,1280]{2,1,0:T(8,128)(2,1)}), bf16[16,16,1280]{2,1,0:T(8,128)(2,1)S(1)}, u32[]{:S(2)}, u32[]{:S(2)}) async-start(bf16[16,16,1280]{2,1,0:T(8,128)(2,1)} %shard_map.159), calls=%async_computation.4 | async-start | bytes 1310720 | tf_op jit(solution)/shard_map/all_to_all | solution.py:618
  151.7 8.2 %collective-permute-done.20.a2 = bf16[224,544]{1,0:T(8,128)(2,1)S(1)} collective-permute-done((bf16[224,544]{1,0:T(8,128)(2,1)}, bf16[224,544]{1,0:T(8,128)(2,1)S(1)}, u32[]{:S(2)}, u32[]{:S(2)}) %collective-permute-start.20) | collective-permute-done | bytes 243744 | tf_op jit(solution)/shard_map/ppermute | solution.py:477
  160.8 2.7 %shard_map.161 = (bf16[320,448]{1,0:T(8,128)(2,1)}, bf16[448,224]{1,0:T(8,128)(2,1)}) custom-call(bf16[224,544]{1,0:T(8,128)(2,1)} %get-tuple-element.104.a0, bf16[224,544]{1,0:T(8,128)(2,1)} %copy-done.20, bf16[224,544]{1,0:T(8,128)(2,1)} %copy-done.21, bf16[224,544]{1,0:T(8,128)(2,1)} %copy-done.22, bf16[224,544]{1,0:T(8,128)(2,1)} %get-tuple-element.100.b0, ...), custom_call_target="tpu_custom_call" | custom-call | flops 40000000000 | bytes 100000000 | tf_op jit(solution)/shard_map/pallas_call | solution.py:444
  163.4 0.7 convert_reduce_fusion
  (80 shorter events, 7.5 us)
Async XLA Ops:
  0.6 10.1 %copy-start.15 = (f32[1280]{0:T(1024)S(1)}, f32[1280]{0:T(1024)}, u32[]{:S(2)}) copy-start(f32[1280]{0:T(1024)} %param.14) | copy-start | bytes 15364
  0.6 10.7 %copy-start.16 = (f32[1280]{0:T(1024)S(1)}, f32[1280]{0:T(1024)}, u32[]{:S(2)}) copy-start(f32[1280]{0:T(1024)} %param.15) | copy-start | bytes 15364
  0.7 24.7 %collective-permute-start = (bf16[448,5120]{1,0:T(8,128)(2,1)}, bf16[448,5120]{1,0:T(8,128)(2,1)}, u32[]{:S(2)}, u32[]{:S(2)}) collective-permute-start(bf16[448,5120]{1,0:T(8,128)(2,1)} %bitcast.20), channel_id=1, source_target_pairs={{0,1},{1,0},{2,3},{3,2},{4,5},{5,4},{6,7},{7,6},{8,9},{9,8},{10,11... | collective-permute-start | bytes 13762568 | tf_op jit(solution)/shard_map/ppermute | solution.py:522
  0.7 24.6 %collective-permute-start.1 = (bf16[448,3584]{1,0:T(8,128)(2,1)}, bf16[448,3584]{1,0:T(8,128)(2,1)S(1)}, u32[]{:S(2)}, u32[]{:S(2)}) collective-permute-start(bf16[448,3584]{1,0:T(8,128)(2,1)} %out_own.1), channel_id=1, source_target_pairs={{0,1},{1,0},{2,3},{3,2},{4,5},{5,4},{6,7},{7,6},{8,9},{9,8},{10,11... | collective-permute-start | bytes 9633800 | tf_op jit(solution)/shard_map/ppermute | solution.py:522
  3.5 21.9 %all-to-all-start = ((bf16[16,48,448]{2,1,0:T(8,128)(2,1)}), bf16[16,48,448]{2,1,0:T(8,128)(2,1)}, u32[]{:S(2)}, u32[]{:S(2)}) async-start(bf16[16,48,448]{2,1,0:T(8,128)(2,1)} %shard_map.146), calls=%async_computation | async-start | bytes 1572864 | tf_op jit(solution)/shard_map/all_to_all | solution.py:561
  16.6 21.9 %collective-permute-start.5 = (bf16[48,5120]{1,0:T(8,128)(2,1)}, bf16[48,5120]{1,0:T(8,128)(2,1)}, u32[]{:S(2)}, u32[]{:S(2)}) collective-permute-start(bf16[48,5120]{1,0:T(8,128)(2,1)} %get-tuple-element.68.b0), channel_id=1, source_target_pairs={{0,2},{1,3},{2,4},{3,5},{4,6},{5,7},{6,0},{7,1},{8,10},{9,11},{10,... | collective-permute-start | bytes 1474568 | tf_op jit(solution)/shard_map/ppermute | solution.py:527
  18.5 26.4 %collective-permute-start.4 = (bf16[48,5120]{1,0:T(8,128)(2,1)}, bf16[48,5120]{1,0:T(8,128)(2,1)}, u32[]{:S(2)}, u32[]{:S(2)}) collective-permute-start(bf16[48,5120]{1,0:T(8,128)(2,1)} %get-tuple-element.68.b0), channel_id=1, source_target_pairs={{0,4},{1,5},{2,6},{3,7},{4,0},{5,1},{6,2},{7,3},{8,12},{9,13},{10,... | collective-permute-start | bytes 1474568 | tf_op jit(solution)/shard_map/ppermute | solution.py:526
  22.1 22.8 %collective-permute-start.3 = (bf16[48,5120]{1,0:T(8,128)(2,1)}, bf16[48,5120]{1,0:T(8,128)(2,1)}, u32[]{:S(2)}, u32[]{:S(2)}) collective-permute-start(bf16[48,5120]{1,0:T(8,128)(2,1)} %get-tuple-element.68.b0), channel_id=1, source_target_pairs={{0,6},{1,7},{2,0},{3,1},{4,2},{5,3},{6,4},{7,5},{8,14},{9,15},{10,... | collective-permute-start | bytes 1474568 | tf_op jit(solution)/shard_map/ppermute | solution.py:528
  25.4 3.1 %copy-start.8 = (bf16[448,3584]{1,0:T(8,128)(2,1)}, bf16[448,3584]{1,0:T(8,128)(2,1)S(1)}, u32[]{:S(2)}) copy-start(bf16[448,3584]{1,0:T(8,128)(2,1)S(1)} %collective-permute-done.1.out_other) | copy-start | bytes 9633796
  28.5 1.7 %collective-permute-start.2 = (bf16[192,448]{1,0:T(8,128)(2,1)}, bf16[192,448]{1,0:T(8,128)(2,1)S(1)}, u32[]{:S(2)}, u32[]{:S(2)}) collective-permute-start(bf16[192,448]{1,0:T(8,128)(2,1)} %get-tuple-element.63), channel_id=1, source_target_pairs={{0,1},{1,0},{2,3},{3,2},{4,5},{5,4},{6,7},{7,6},{8,9},{9,8},{10,11... | collective-permute-start | bytes 516104 | tf_op jit(solution)/shard_map/ppermute | solution.py:522
  33.1 25.5 %all-to-all-start.1 = ((bf16[4,192,896]{2,1,0:T(8,128)(2,1)}), bf16[4,192,896]{2,1,0:T(8,128)(2,1)}, u32[]{:S(2)}, u32[]{:S(2)}) async-start(bf16[4,192,896]{2,1,0:T(8,128)(2,1)} %shard_map.149), calls=%async_computation.1 | async-start | bytes 2752512 | tf_op jit(solution)/shard_map/all_to_all | solution.py:533
  38.4 14.2 %copy-start.2 = (bf16[8,24,1280]{2,1,0:T(8,128)(2,1)S(1)}, bf16[8,24,1280]{2,1,0:T(8,128)(2,1)}, u32[]{:S(2)}) copy-start(bf16[8,24,1280]{2,1,0:T(8,128)(2,1)} %param.11) | copy-start | bytes 1474564
  52.6 20.9 %collective-permute-start.6 = (bf16[192,5120]{1,0:T(8,128)(2,1)}, bf16[192,5120]{1,0:T(8,128)(2,1)}, u32[]{:S(2)}, u32[]{:S(2)}) collective-permute-start(bf16[192,5120]{1,0:T(8,128)(2,1)} %get-tuple-element.76.refs_1_), channel_id=1, source_target_pairs={{0,1},{1,0},{2,3},{3,2},{4,5},{5,4},{6,7},{7,6},{8,9},{9,8},{10,11... | collective-permute-start | bytes 5898248 | tf_op jit(solution)/shard_map/ppermute | solution.py:522
  55.2 14.0 %copy-start.5 = (bf16[640,192]{1,0:T(8,128)(2,1)}, bf16[640,192]{1,0:T(8,128)(2,1)S(1)}, u32[]{:S(2)}) copy-start(bf16[640,192]{1,0:T(8,128)(2,1)S(1)} %get-tuple-element.64) | copy-start | bytes 737284
  58.6 14.9 %collective-permute-start.7 = (bf16[4,192,896]{2,1,0:T(8,128)(2,1)}, bf16[4,192,896]{2,1,0:T(8,128)(2,1)}, u32[]{:S(2)}, u32[]{:S(2)}) collective-permute-start(bf16[4,192,896]{2,1,0:T(8,128)(2,1)} %all-to-all-done.1.og.refs_3_), channel_id=1, source_target_pairs={{0,1},{1,0},{2,3},{3,2},{4,5},{5,4},{6,7},{7,6},{8,9},{9,8},{10,11... | collective-permute-start | bytes 4128776 | tf_op jit(solution)/shard_map/ppermute | solution.py:522
  69.2 4.2 %collective-permute-start.8 = (bf16[896,192]{1,0:T(8,128)(2,1)}, bf16[896,192]{1,0:T(8,128)(2,1)S(1)}, u32[]{:S(2)}, u32[]{:S(2)}) collective-permute-start(bf16[896,192]{1,0:T(8,128)(2,1)} %get-tuple-element.80), channel_id=1, source_target_pairs={{0,1},{1,0},{2,3},{3,2},{4,5},{5,4},{6,7},{7,6},{8,9},{9,8},{10,11... | collective-permute-start | bytes 1032200 | tf_op jit(solution)/shard_map/ppermute | solution.py:522
  69.8 33.3 %all-to-all-start.2 = ((bf16[4,48,5120]{2,1,0:T(8,128)(2,1)}), bf16[4,48,5120]{2,1,0:T(8,128)(2,1)S(1)}, u32[]{:S(2)}, u32[]{:S(2)}) async-start(bf16[4,48,5120]{2,1,0:T(8,128)(2,1)} %bitcast.23), calls=%async_computation.2 | async-start | bytes 3932160 | tf_op jit(solution)/shard_map/all_to_all | solution.py:533
  80.3 18.0 %collective-permute-start.9 = (bf16[112,2176]{1,0:T(8,128)(2,1)}, bf16[112,2176]{1,0:T(8,128)(2,1)S(1)}, u32[]{:S(2)}, u32[]{:S(2)}) collective-permute-start(bf16[112,2176]{1,0:T(8,128)(2,1)} %get-tuple-element.81), channel_id=1, source_target_pairs={{0,8},{8,16},{16,24},{24,0},{32,40},{40,48},{48,56},{56,32},{64,72... | collective-permute-start | bytes 1462280 | tf_op jit(solution)/shard_map/ppermute | solution.py:593
  81.7 16.5 %collective-permute-start.10 = (bf16[112,2176]{1,0:T(8,128)(2,1)}, bf16[112,2176]{1,0:T(8,128)(2,1)S(1)}, u32[]{:S(2)}, u32[]{:S(2)}) collective-permute-start(bf16[112,2176]{1,0:T(8,128)(2,1)} %get-tuple-element.87), channel_id=1, source_target_pairs={{0,24},{8,0},{16,8},{24,16},{32,56},{40,32},{48,40},{56,48},{64,88... | collective-permute-start | bytes 1462280 | tf_op jit(solution)/shard_map/ppermute | solution.py:594
  83.5 14.8 %collective-permute-start.11 = (bf16[112,2176]{1,0:T(8,128)(2,1)}, bf16[112,2176]{1,0:T(8,128)(2,1)S(1)}, u32[]{:S(2)}, u32[]{:S(2)}) collective-permute-start(bf16[112,2176]{1,0:T(8,128)(2,1)} %get-tuple-element.88), channel_id=1, source_target_pairs={{0,32},{8,40},{16,48},{24,56},{32,64},{40,72},{48,80},{56,88},{64,... | collective-permute-start | bytes 1462280 | tf_op jit(solution)/shard_map/ppermute | solution.py:595
  85.1 13.2 %collective-permute-start.12 = (bf16[112,2176]{1,0:T(8,128)(2,1)}, bf16[112,2176]{1,0:T(8,128)(2,1)S(1)}, u32[]{:S(2)}, u32[]{:S(2)}) collective-permute-start(bf16[112,2176]{1,0:T(8,128)(2,1)} %get-tuple-element.89), channel_id=1, source_target_pairs={{0,96},{8,104},{16,112},{24,120},{32,0},{40,8},{48,16},{56,24},{64... | collective-permute-start | bytes 1462280 | tf_op jit(solution)/shard_map/ppermute | solution.py:596
  98.3 0.9 copy-start.11
  98.3 1.1 copy-start.12
  98.3 1.2 copy-start.9
  99.5 6.8 %copy-start.3 = (f32[1,1280]{1,0:T(1,128)S(1)}, f32[1,1280]{1,0:T(1,128)}, u32[]{:S(2)}) copy-start(f32[1,1280]{1,0:T(1,128)} %reshape.232.gain) | copy-start | bytes 15364
  99.5 6.8 %copy-start.4 = (f32[192,1280]{1,0:T(8,128)S(1)}, f32[192,1280]{1,0:T(8,128)}, u32[]{:S(2)}) copy-start(f32[192,1280]{1,0:T(8,128)} %get-tuple-element.92.normed) | copy-start | bytes 2949124
  99.5 6.8 %copy-start.7 = (f32[192,128]{1,0:T(8,128)S(1)}, f32[192,128]{1,0:T(8,128)}, u32[]{:S(2)}) copy-start(f32[192,128]{1,0:T(8,128)} %get-tuple-element.93.inverse) | copy-start | bytes 294916
  103.1 23.9 %collective-permute-start.15 = (bf16[224,2176]{1,0:T(8,128)(2,1)}, bf16[224,2176]{1,0:T(8,128)(2,1)}, u32[]{:S(2)}, u32[]{:S(2)}) collective-permute-start(bf16[224,2176]{1,0:T(8,128)(2,1)} %get-tuple-element.98), channel_id=1, source_target_pairs={{0,32},{8,40},{16,48},{24,56},{32,64},{40,72},{48,80},{56,88},{64,... | collective-permute-start | bytes 2924552 | tf_op jit(solution)/shard_map/ppermute | solution.py:612
  103.6 23.5 %collective-permute-start.16 = (bf16[224,2176]{1,0:T(8,128)(2,1)}, bf16[224,2176]{1,0:T(8,128)(2,1)}, u32[]{:S(2)}, u32[]{:S(2)}) collective-permute-start(bf16[224,2176]{1,0:T(8,128)(2,1)} %get-tuple-element.99), channel_id=1, source_target_pairs={{0,96},{8,104},{16,112},{24,120},{32,0},{40,8},{48,16},{56,24},{64... | collective-permute-start | bytes 2924552 | tf_op jit(solution)/shard_map/ppermute | solution.py:612
  106.4 1.5 copy-start.6
  107.9 3.8 %collective-permute-start.14 = (bf16[192,1280]{1,0:T(8,128)(2,1)}, bf16[192,1280]{1,0:T(8,128)(2,1)S(1)}, u32[]{:S(2)}, u32[]{:S(2)}) collective-permute-start(bf16[192,1280]{1,0:T(8,128)(2,1)} %shard_map.156.grad), channel_id=1, source_target_pairs={{0,1},{1,0},{2,3},{3,2},{4,5},{5,4},{6,7},{7,6},{8,9},{9,8},{10,11... | collective-permute-start | bytes 1474568 | tf_op jit(solution)/shard_map/ppermute | solution.py:522
  107.9 2.2 %collective-permute-start.13 = (bf16[640,192]{1,0:T(8,128)(2,1)S(1)}, bf16[640,192]{1,0:T(8,128)(2,1)S(1)}, u32[]{:S(2)}, u32[]{:S(2)}) collective-permute-start(bf16[640,192]{1,0:T(8,128)(2,1)S(1)} %copy-done.6), channel_id=1, source_target_pairs={{0,1},{1,0},{2,3},{3,2},{4,5},{5,4},{6,7},{7,6},{8,9},{9,8},{10,11... | collective-permute-start | bytes 737288 | tf_op jit(solution)/shard_map/ppermute | solution.py:522
  108.4 26.4 %collective-permute-start.17 = (bf16[224,2176]{1,0:T(8,128)(2,1)}, bf16[224,2176]{1,0:T(8,128)(2,1)S(1)}, u32[]{:S(2)}, u32[]{:S(2)}) collective-permute-start(bf16[224,2176]{1,0:T(8,128)(2,1)} %get-tuple-element.90), channel_id=1, source_target_pairs={{0,8},{8,16},{16,24},{24,0},{32,40},{40,48},{48,56},{56,32},{64,72... | collective-permute-start | bytes 2924552 | tf_op jit(solution)/shard_map/ppermute | solution.py:614
  110.0 24.7 %collective-permute-start.18 = (bf16[224,2176]{1,0:T(8,128)(2,1)}, bf16[224,2176]{1,0:T(8,128)(2,1)}, u32[]{:S(2)}, u32[]{:S(2)}) collective-permute-start(bf16[224,2176]{1,0:T(8,128)(2,1)} %get-tuple-element.103), channel_id=1, source_target_pairs={{0,24},{8,0},{16,8},{24,16},{32,56},{40,32},{48,40},{56,48},{64,88... | collective-permute-start | bytes 2924552 | tf_op jit(solution)/shard_map/ppermute | solution.py:614
  111.7 1.0 copy-start
  116.0 4.9 %copy-start.1 = (bf16[192,1280]{1,0:T(8,128)(2,1)S(1)}, bf16[192,1280]{1,0:T(8,128)(2,1)}, u32[]{:S(2)}) copy-start(bf16[192,1280]{1,0:T(8,128)(2,1)} %shard_map.156.grad) | copy-start | bytes 1474564
  116.1 30.3 %all-to-all-start.3 = ((bf16[4,160,1280]{2,1,0:T(8,128)(2,1)}), bf16[4,160,1280]{2,1,0:T(8,128)(2,1)S(1)}, u32[]{:S(2)}, u32[]{:S(2)}) async-start(bf16[4,160,1280]{2,1,0:T(8,128)(2,1)} %bitcast.13), calls=%async_computation.3 | async-start | bytes 3276800 | tf_op jit(solution)/shard_map/all_to_all | solution.py:533
  130.4 15.2 %collective-permute-start.22 = (bf16[224,544]{1,0:T(8,128)(2,1)}, bf16[224,544]{1,0:T(8,128)(2,1)S(1)}, u32[]{:S(2)}, u32[]{:S(2)}) collective-permute-start(bf16[224,544]{1,0:T(8,128)(2,1)} %get-tuple-element.108), channel_id=1, source_target_pairs={{0,8},{8,16},{16,24},{24,0},{32,40},{40,48},{48,56},{56,32},{64,72... | collective-permute-start | bytes 731144 | tf_op jit(solution)/shard_map/ppermute | solution.py:476
  131.0 20.7 %collective-permute-start.23 = (bf16[224,544]{1,0:T(8,128)(2,1)}, bf16[224,544]{1,0:T(8,128)(2,1)S(1)}, u32[]{:S(2)}, u32[]{:S(2)}) collective-permute-start(bf16[224,544]{1,0:T(8,128)(2,1)} %get-tuple-element.109), channel_id=1, source_target_pairs={{0,24},{8,0},{16,8},{24,16},{32,56},{40,32},{48,40},{56,48},{64,88... | collective-permute-start | bytes 731144 | tf_op jit(solution)/shard_map/ppermute | solution.py:477
  133.8 17.8 %collective-permute-start.24 = (bf16[224,544]{1,0:T(8,128)(2,1)}, bf16[224,544]{1,0:T(8,128)(2,1)}, u32[]{:S(2)}, u32[]{:S(2)}) collective-permute-start(bf16[224,544]{1,0:T(8,128)(2,1)} %get-tuple-element.110), channel_id=1, source_target_pairs={{0,16},{8,24},{16,0},{24,8},{32,48},{40,56},{48,32},{56,40},{64,80... | collective-permute-start | bytes 731144 | tf_op jit(solution)/shard_map/ppermute | solution.py:475
  134.8 0.9 copy-start.17
  139.1 12.6 %collective-permute-start.19 = (bf16[224,544]{1,0:T(8,128)(2,1)}, bf16[224,544]{1,0:T(8,128)(2,1)S(1)}, u32[]{:S(2)}, u32[]{:S(2)}) collective-permute-start(bf16[224,544]{1,0:T(8,128)(2,1)} %get-tuple-element.105), channel_id=1, source_target_pairs={{0,32},{8,40},{16,48},{24,56},{32,64},{40,72},{48,80},{56,88},{64,... | collective-permute-start | bytes 731144 | tf_op jit(solution)/shard_map/ppermute | solution.py:476
  139.1 20.9 %collective-permute-start.20 = (bf16[224,544]{1,0:T(8,128)(2,1)}, bf16[224,544]{1,0:T(8,128)(2,1)S(1)}, u32[]{:S(2)}, u32[]{:S(2)}) collective-permute-start(bf16[224,544]{1,0:T(8,128)(2,1)} %get-tuple-element.106), channel_id=1, source_target_pairs={{0,96},{8,104},{16,112},{24,120},{32,0},{40,8},{48,16},{56,24},{64... | collective-permute-start | bytes 731144 | tf_op jit(solution)/shard_map/ppermute | solution.py:477
  145.6 14.4 %copy-start.18 = (bf16[224,544]{1,0:T(8,128)(2,1)}, bf16[224,544]{1,0:T(8,128)(2,1)S(1)}, u32[]{:S(2)}) copy-start(bf16[224,544]{1,0:T(8,128)(2,1)S(1)} %collective-permute-done.22.b1) | copy-start | bytes 731140
  145.6 14.4 %collective-permute-start.21 = (bf16[224,544]{1,0:T(8,128)(2,1)}, bf16[224,544]{1,0:T(8,128)(2,1)S(1)}, u32[]{:S(2)}, u32[]{:S(2)}) collective-permute-start(bf16[224,544]{1,0:T(8,128)(2,1)} %get-tuple-element.107), channel_id=1, source_target_pairs={{0,64},{8,72},{16,80},{24,88},{32,96},{40,104},{48,112},{56,120},{... | collective-permute-start | bytes 731144 | tf_op jit(solution)/shard_map/ppermute | solution.py:475
  147.4 16.0 %all-to-all-start.4 = ((bf16[16,16,1280]{2,1,0:T(8,128)(2,1)}), bf16[16,16,1280]{2,1,0:T(8,128)(2,1)S(1)}, u32[]{:S(2)}, u32[]{:S(2)}) async-start(bf16[16,16,1280]{2,1,0:T(8,128)(2,1)} %shard_map.159), calls=%async_computation.4 | async-start | bytes 1310720 | tf_op jit(solution)/shard_map/all_to_all | solution.py:618
  151.7 8.3 %copy-start.19 = (bf16[224,544]{1,0:T(8,128)(2,1)}, bf16[224,544]{1,0:T(8,128)(2,1)S(1)}, u32[]{:S(2)}) copy-start(bf16[224,544]{1,0:T(8,128)(2,1)S(1)} %collective-permute-done.23.b2) | copy-start | bytes 731140
  151.7 8.3 %copy-start.20 = (bf16[224,544]{1,0:T(8,128)(2,1)}, bf16[224,544]{1,0:T(8,128)(2,1)S(1)}, u32[]{:S(2)}) copy-start(bf16[224,544]{1,0:T(8,128)(2,1)S(1)} %collective-permute-done.19.a1) | copy-start | bytes 731140
  (5 other events, 3.8 us)

commit v6 on v5

--- a/solution.py
+++ b/solution.py
@@ -10,7 +10,7 @@
 ZN, CN = 4, 2
 YN, XN = 4, 4
 TP = ZN * CN
-PARAMS = pltpu.CompilerParams(vmem_limit_bytes=56 * 1024 * 1024)
+PARAMS = pltpu.CompilerParams(vmem_limit_bytes=62 * 1024 * 1024)
 SMALL = pltpu.CompilerParams(vmem_limit_bytes=20 * 1024 * 1024)
 
 CORE_SWAP = [(i, i ^ 1) for i in range(TP)]

time: 166 us -> 164 us (0.988)
  local copies, waits for them, and re-layouts: 7.32 us -> 10 us
  Pallas kernels: 69.7 us -> 67.4 us
    ppermute x2, waiting for transfers between devices: 8.25 us -> 4.74 us  [ring_of(): down = lax.ppermute(parts[3], 'seq', shift(-1))]
    unnamed x46 -> x36, local copies, waits for them, and re-layouts: 5.45 us -> 8.22 us
    all_to_all x1, waiting for transfers between devices: 0.01 us -> 2.25 us  [per_device(): lax.all_to_all(weight_z, 'seq', split_axis=0, concat_axis=0, tiled=True)]
    ppermute x1, waiting for transfers between devices: 0.24 us -> 2.27 us  [per_device(): lax.ppermute(x_down, 'seq', x_shift(-1))]
    all_to_all x3, waiting for transfers between devices: 3.36 us -> 1.54 us  [z_exchange(): lax.all_to_all(parts, 'tp', split_axis=0, concat_axis=0, axis_index_group...]
    ppermute x1, waiting for transfers between devices: 2.14 us -> 0.38 us  [per_device(): lax.ppermute(y_up, 'seq', y_shift(1))]
  transfers between devices with their start and end apart: 30 -> 30, of which waited for: 9 -> 11; matrix products, arithmetic and copies ran while one was open for 4% -> 4% of each run, Pallas kernels for 42% -> 41%
where the time goes in v6:
time: 164 us; the launch traced here: 163 us
  Pallas kernels  67.4 us (41%)
  starting transfers between devices  53.3 us (32%)
  waiting for transfers between devices  26.8 us (16%)
  local copies, waits for them, and re-layouts  10 us (6%)
  matrix products  3.93 us (2%)
    pallas_call x2, Pallas kernels, weight_grads_of(): pl.pallas_call(kernel, out_shape=tuple((struct(shape, BF16) for shape in...  17.6 us
    all_to_all x3, starting transfers between devices, z_exchange(): lax.all_to_all(parts, 'tp', split_axis=0, concat_axis=0, axis_index_group...  13.8 us
    pallas_call x1, Pallas kernels, pre_grad_of(): pl.pallas_call(pre_grad_kernel, out_shape=(struct((192, 5120), BF16), str...  10.6 us
    unnamed x36, local copies, waits for them, and re-layouts  8.22 us
    pallas_call x1, Pallas kernels, preact_of(): pl.pallas_call(preact_kernel, out_shape=(struct((192, 5120), BF16), struc...  7.65 us
    all_to_all x1, starting transfers between devices, per_device(): lax.all_to_all(parcels, 'seq', split_axis=0, concat_axis=0, tiled=True)  7.12 us
    pallas_call x2, Pallas kernels, spread_of(): pl.pallas_call(spread_kernel, out_shape=(struct((224, 544), BF16),) * 4,...  6.73 us
    ppermute x2, starting transfers between devices, ring_of(): down = lax.ppermute(parts[3], 'seq', shift(-1))  6.05 us
  transfers between devices with their start and end apart: 30, of which 11 were waited for; matrix products, arithmetic and copies ran while one was open for 4% of the time, Pallas kernels for 41%

profile of v6, /device:TPU:0, one launch (start us, length us, event | category | flops | bytes accessed | tf_op | source)
XLA Modules:
  0.0 163.2 jit_solution(2296120381507473160)
XLA Ops:
  1.2 2.4 %shard_map.146 = bf16[16,48,448]{2,1,0:T(8,128)(2,1)} custom-call(s32[128]{0:T(128)} %offsets.1, s32[128]{0:T(128)} %frames.1, s32[128]{0:T(128)} %owner.1, bf16[448,384]{1,0:T(8,128)(2,1)} %bitcast.27), custom_call_target="tpu_custom_call" | custom-call | flops 1 | bytes 1 | tf_op jit(solution)/shard_map/pallas_call | solution.py:79
  3.6 7.1 %all-to-all-start = ((bf16[16,48,448]{2,1,0:T(8,128)(2,1)}), bf16[16,48,448]{2,1,0:T(8,128)(2,1)S(1)}, u32[]{:S(2)}, u32[]{:S(2)}) async-start(bf16[16,48,448]{2,1,0:T(8,128)(2,1)} %shard_map.146), calls=%async_computation | async-start | bytes 1572864 | tf_op jit(solution)/shard_map/all_to_all | solution.py:561
  11.9 4.7 %shard_map.147 = (bf16[48,5120]{1,0:T(8,128)(2,1)}, f32[192,1280]{1,0:T(8,128)}, f32[192,128]{1,0:T(8,128)}) custom-call(bf16[192,1280]{1,0:T(8,128)(2,1)} %bitcast.19, bf16[192,1280]{1,0:T(8,128)(2,1)} %bitcast.25, bf16[1280,1280]{1,0:T(8,128)(2,1)} %weight.1, f32[1,1280]{1,0:T(1,128)} %reshape.232.gain, f32[1,1280]{1,0:T(1,128)} %reshape.233.bias), custom_call_target="tpu_custom_call" | custom-call | flops 1 | bytes 1 | tf_op jit(solution)/shard_map/pallas_call | solution.py:156
  16.6 1.9 %collective-permute-start.5 = (bf16[48,5120]{1,0:T(8,128)(2,1)}, bf16[48,5120]{1,0:T(8,128)(2,1)S(1)}, u32[]{:S(2)}, u32[]{:S(2)}) collective-permute-start(bf16[48,5120]{1,0:T(8,128)(2,1)} %get-tuple-element.68.b0), channel_id=1, source_target_pairs={{0,2},{1,3},{2,4},{3,5},{4,6},{5,7},{6,0},{7,1},{8,10},{9,11},{10,... | collective-permute-start | bytes 1474568 | tf_op jit(solution)/shard_map/ppermute | solution.py:527
  18.5 3.6 %collective-permute-start.4 = (bf16[48,5120]{1,0:T(8,128)(2,1)}, bf16[48,5120]{1,0:T(8,128)(2,1)S(1)}, u32[]{:S(2)}, u32[]{:S(2)}) collective-permute-start(bf16[48,5120]{1,0:T(8,128)(2,1)} %get-tuple-element.68.b0), channel_id=1, source_target_pairs={{0,4},{1,5},{2,6},{3,7},{4,0},{5,1},{6,2},{7,3},{8,12},{9,13},{10,... | collective-permute-start | bytes 1474568 | tf_op jit(solution)/shard_map/ppermute | solution.py:526
  22.1 1.0 collective-permute-start.3
  23.7 1.6 %all-to-all-done.arrived = bf16[16,48,448]{2,1,0:T(8,128)(2,1)S(1)} async-done(((bf16[16,48,448]{2,1,0:T(8,128)(2,1)}), bf16[16,48,448]{2,1,0:T(8,128)(2,1)S(1)}, u32[]{:S(2)}, u32[]{:S(2)}) %all-to-all-start) | async-done | bytes 688160 | tf_op jit(solution)/shard_map/all_to_all | solution.py:561
  25.4 1.0 copy-done.11
  26.3 2.4 %shard_map.148 = (bf16[192,448]{1,0:T(8,128)(2,1)}, bf16[192,448]{1,0:T(8,128)(2,1)}) custom-call(s32[5]{0:T(128)} %stack.23.ids.refs_0_, s32[1,128]{1,0:T(1,128)} %bitcast.29, bf16[16,48,448]{2,1,0:T(8,128)(2,1)} %copy-done.11), custom_call_target="tpu_custom_call" | custom-call | flops 1 | bytes 1 | tf_op jit(solution)/shard_map/pallas_call | solution.py:109
  28.9 1.5 collective-permute-done.2.got
  31.1 2.3 %shard_map.149 = bf16[4,192,896]{2,1,0:T(8,128)(2,1)} custom-call(s32[5]{0:T(128)} %stack.23.ids.refs_0_, bf16[192,448]{1,0:T(8,128)(2,1)} %get-tuple-element.62.keep, bf16[192,448]{1,0:T(8,128)(2,1)} %copy-done.14), custom_call_target="tpu_custom_call" | custom-call | flops 1 | bytes 1 | tf_op jit(solution)/shard_map/pallas_call | solution.py:129
  33.4 5.3 %all-to-all-start.1 = ((bf16[4,192,896]{2,1,0:T(8,128)(2,1)}), bf16[4,192,896]{2,1,0:T(8,128)(2,1)}, u32[]{:S(2)}, u32[]{:S(2)}) async-start(bf16[4,192,896]{2,1,0:T(8,128)(2,1)} %shard_map.149), calls=%async_computation.1 | async-start | bytes 2752512 | tf_op jit(solution)/shard_map/all_to_all | solution.py:533
  38.7 5.8 %collective-permute-done.4.b2 = bf16[48,5120]{1,0:T(8,128)(2,1)S(1)} collective-permute-done((bf16[48,5120]{1,0:T(8,128)(2,1)}, bf16[48,5120]{1,0:T(8,128)(2,1)S(1)}, u32[]{:S(2)}, u32[]{:S(2)}) %collective-permute-start.4) | collective-permute-done | bytes 491552 | tf_op jit(solution)/shard_map/ppermute | solution.py:526
  45.3 7.7 %shard_map.151 = (bf16[192,5120]{1,0:T(8,128)(2,1)}, bf16[448,192]{1,0:T(8,128)(2,1)}, bf16[448,192]{1,0:T(8,128)(2,1)}, f32[448,192]{1,0:T(8,128)}, f32[448,192]{1,0:T(8,128)}) custom-call(s32[5]{0:T(128)} %stack.23.ids.refs_0_, bf16[48,5120]{1,0:T(8,128)(2,1)} %get-tuple-element.68.b0, bf16[48,5120]{1,0:T(8,128)(2,1)} %collective-permute-done.3.b1, ...), custom_call_target="tpu_custom_call" | custom-call | flops 1 | bytes 1 | tf_op jit(solution)/shard_map/pallas_call | solution.py:220
  53.1 2.5 %shard_map.150 = (bf16[640,192]{1,0:T(8,128)(2,1)S(1)}, bf16[640,192]{1,0:T(8,128)(2,1)S(1)}) custom-call(s32[1,1280]{1,0:T(1,128)S(1)} %fusion.1.target.target_other, s32[1,1280]{1,0:T(1,128)S(1)} %fusion.1.target.target_other, bf16[192,1280]{1,0:T(8,128)(2,1)S(1)} %bitcast.20), custom_call_target="tpu_custom_call" | custom-call | flops 40000000000 | bytes 100000000 | tf_op jit(solution)/shard_map/pallas_call | solution.py:489
  57.1 1.5 all-to-all-done.1.og.refs_3_
  58.6 10.6 %shard_map.152 = (bf16[192,5120]{1,0:T(8,128)(2,1)}, bf16[448,192]{1,0:T(8,128)(2,1)}, bf16[896,192]{1,0:T(8,128)(2,1)}) custom-call(bf16[4,192,896]{2,1,0:T(8,128)(2,1)} %all-to-all-done.1.og.refs_3_, bf16[448,3584]{1,0:T(8,128)(2,1)} %out_own.1, bf16[448,3584]{1,0:T(8,128)(2,1)} %collective-permute-done.1.out_other, bf16[448,5120]{1,0:T(8,128)(2,1)} %bitcast.23, ...), custom_call_target="tpu_custom_call" | custom-call | flops 1 | bytes 1 | tf_op jit(solution)/shard_map/pallas_call | solution.py:294
  69.8 3.6 %all-to-all-start.2 = ((bf16[4,48,5120]{2,1,0:T(8,128)(2,1)}), bf16[4,48,5120]{2,1,0:T(8,128)(2,1)S(1)}, u32[]{:S(2)}, u32[]{:S(2)}) async-start(bf16[4,48,5120]{2,1,0:T(8,128)(2,1)} %bitcast.24), calls=%async_computation.2 | async-start | bytes 3932160 | tf_op jit(solution)/shard_map/all_to_all | solution.py:533
  73.5 6.1 %shard_map.153 = (bf16[112,2176]{1,0:T(8,128)(2,1)}, bf16[112,2176]{1,0:T(8,128)(2,1)}, bf16[112,2176]{1,0:T(8,128)(2,1)}, bf16[112,2176]{1,0:T(8,128)(2,1)}) custom-call(s32[5]{0:T(128)} %stack.23.ids.refs_0_, bf16[192,5120]{1,0:T(8,128)(2,1)} %get-tuple-element.76.refs_1_, bf16[192,5120]{1,0:T(8,128)(2,1)} %collective-permute-done.6.refs_2_, ...), custom_call_target="tpu_custom_call" | custom-call | flops 1 | bytes 1 | tf_op jit(solution)/shard_map/pallas_call | solution.py:373
  79.6 1.5 collective-permute-start.9
  81.0 1.8 %collective-permute-start.10 = (bf16[112,2176]{1,0:T(8,128)(2,1)}, bf16[112,2176]{1,0:T(8,128)(2,1)}, u32[]{:S(2)}, u32[]{:S(2)}) collective-permute-start(bf16[112,2176]{1,0:T(8,128)(2,1)} %get-tuple-element.87), channel_id=1, source_target_pairs={{0,24},{8,0},{16,8},{24,16},{32,56},{40,32},{48,40},{56,48},{64,88... | collective-permute-start | bytes 1462280 | tf_op jit(solution)/shard_map/ppermute | solution.py:594
  82.8 1.6 collective-permute-start.11
  84.4 1.6 collective-permute-start.12
  86.0 11.5 %shard_map.154 = (bf16[224,2176]{1,0:T(8,128)(2,1)}, bf16[224,2176]{1,0:T(8,128)(2,1)}, bf16[224,2176]{1,0:T(8,128)(2,1)}, bf16[224,2176]{1,0:T(8,128)(2,1)}, bf...) custom-call(s32[5]{0:T(128)} %stack.23.ids.refs_0_, bf16[192,5120]{1,0:T(8,128)(2,1)} %get-tuple-element.76.refs_1_, ...), custom_call_target="tpu_custom_call" | custom-call | flops 40000000000 | bytes 100000000 | tf_op jit(solution)/shard_map/pallas_call | solution.py:373
  97.6 3.5 %shard_map.155 = (bf16[224,2176]{1,0:T(8,128)(2,1)}, bf16[224,2176]{1,0:T(8,128)(2,1)}, bf16[224,2176]{1,0:T(8,128)(2,1)}, bf16[224,2176]{1,0:T(8,128)(2,1)}) custom-call(bf16[224,2176]{1,0:T(8,128)(2,1)} %get-tuple-element.83.x_up, ...), custom_call_target="tpu_custom_call", output_to_operand_aliasing={{0}: (0, {}), {1}: (1, {}), {2}: (2, {}), {3}: (3, {})} | custom-call | flops 1 | bytes 1 | tf_op jit(solution)/shard_map/pallas_call | solution.py:397
  101.9 2.4 %collective-permute-start.16 = (bf16[224,2176]{1,0:T(8,128)(2,1)}, bf16[224,2176]{1,0:T(8,128)(2,1)}, u32[]{:S(2)}, u32[]{:S(2)}) collective-permute-start(bf16[224,2176]{1,0:T(8,128)(2,1)} %get-tuple-element.99), channel_id=1, source_target_pairs={{0,96},{8,104},{16,112},{24,120},{32,0},{40,8},{48,16},{56,24},{64... | collective-permute-start | bytes 2924552 | tf_op jit(solution)/shard_map/ppermute | solution.py:612
  104.3 1.2 copy-done.7
  105.5 0.9 copy-done.10
  106.4 1.5 shard_map.156.grad
  108.9 1.2 collective-permute-done.13.ctx_other
  110.1 1.7 %collective-permute-start.18 = (bf16[224,2176]{1,0:T(8,128)(2,1)}, bf16[224,2176]{1,0:T(8,128)(2,1)}, u32[]{:S(2)}, u32[]{:S(2)}) collective-permute-start(bf16[224,2176]{1,0:T(8,128)(2,1)} %get-tuple-element.103), channel_id=1, source_target_pairs={{0,24},{8,0},{16,8},{24,16},{32,56},{40,32},{48,40},{56,48},{64,88... | collective-permute-start | bytes 2924552 | tf_op jit(solution)/shard_map/ppermute | solution.py:614
  111.8 1.0 copy-done.1
  112.8 1.8 %shard_map.157 = bf16[640,1280]{1,0:T(8,128)(2,1)S(1)} custom-call(bf16[640,192]{1,0:T(8,128)(2,1)S(1)} %copy-done.5, bf16[640,192]{1,0:T(8,128)(2,1)S(1)} %collective-permute-done.13.ctx_other, bf16[192,1280]{1,0:T(8,128)(2,1)S(1)} %copy-done.1, bf16[192,1280]{1,0:T(8,128)(2,1)S(1)} %collective-permute-done.14.grad_other), custom_call_target="tpu_custom_call" | custom-call | flops 1 | bytes 1 | tf_op jit(solution)/shard_map/pallas_call | solution.py:510
  114.6 1.2 copy-done
  115.8 4.9 %all-to-all-start.3 = ((bf16[4,160,1280]{2,1,0:T(8,128)(2,1)}), bf16[4,160,1280]{2,1,0:T(8,128)(2,1)S(1)}, u32[]{:S(2)}, u32[]{:S(2)}) async-start(bf16[4,160,1280]{2,1,0:T(8,128)(2,1)} %bitcast.17), calls=%async_computation.3 | async-start | bytes 3276800 | tf_op jit(solution)/shard_map/all_to_all | solution.py:533
  120.7 3.9 %convolution_convert_fusion = bf16[192,1280]{1,0:T(8,128)(2,1)} fusion(bf16[192,1280]{1,0:T(8,128)(2,1)S(1)} %copy-done.2, bf16[1280,1280]{1,0:T(8,128)(2,1)} %weight.1), kind=kOutput, calls=%fused_computation | convolution fusion | flops 629391360 | bytes 4259840 | tf_op jit(solution)/shard_map/dot_general | solution.py:39
  125.0 3.4 %shard_map.158 = (bf16[224,544]{1,0:T(8,128)(2,1)}, bf16[224,544]{1,0:T(8,128)(2,1)}, bf16[224,544]{1,0:T(8,128)(2,1)}, bf16[224,544]{1,0:T(8,128)(2,1)}) custom-call(s32[1]{0:T(128)} %bitcast.1.where, bf16[224,2176]{1,0:T(8,128)(2,1)} %get-tuple-element.97.a, bf16[224,2176]{1,0:T(8,128)(2,1)} %collective-permute-done.15.b, ...), custom_call_target="tpu_custom_call" | custom-call | flops 40000000000 | bytes 100000000 | tf_op jit(solution)/shard_map/pallas_call | solution.py:424
  129.0 2.8 %collective-permute-start.23 = (bf16[224,544]{1,0:T(8,128)(2,1)}, bf16[224,544]{1,0:T(8,128)(2,1)}, u32[]{:S(2)}, u32[]{:S(2)}) collective-permute-start(bf16[224,544]{1,0:T(8,128)(2,1)} %get-tuple-element.109), channel_id=1, source_target_pairs={{0,24},{8,0},{16,8},{24,16},{32,56},{40,32},{48,40},{56,48},{64,88... | collective-permute-start | bytes 731144 | tf_op jit(solution)/shard_map/ppermute | solution.py:477
  132.5 2.3 %collective-permute-done.18.c = bf16[224,2176]{1,0:T(8,128)(2,1)} collective-permute-done((bf16[224,2176]{1,0:T(8,128)(2,1)}, bf16[224,2176]{1,0:T(8,128)(2,1)}, u32[]{:S(2)}, u32[]{:S(2)}) %collective-permute-start.18) | collective-permute-done | bytes 974880 | tf_op jit(solution)/shard_map/ppermute | solution.py:614
  134.8 3.4 %shard_map.160 = (bf16[224,544]{1,0:T(8,128)(2,1)}, bf16[224,544]{1,0:T(8,128)(2,1)}, bf16[224,544]{1,0:T(8,128)(2,1)}, bf16[224,544]{1,0:T(8,128)(2,1)}) custom-call(s32[1]{0:T(128)} %bitcast.where, bf16[224,2176]{1,0:T(8,128)(2,1)} %get-tuple-element.102.a, bf16[224,2176]{1,0:T(8,128)(2,1)} %collective-permute-done.17.b, ...), custom_call_target="tpu_custom_call" | custom-call | flops 40000000000 | bytes 100000000 | tf_op jit(solution)/shard_map/pallas_call | solution.py:424
  138.2 3.2 %collective-permute-start.20 = (bf16[224,544]{1,0:T(8,128)(2,1)}, bf16[224,544]{1,0:T(8,128)(2,1)}, u32[]{:S(2)}, u32[]{:S(2)}) collective-permute-start(bf16[224,544]{1,0:T(8,128)(2,1)} %get-tuple-element.106), channel_id=1, source_target_pairs={{0,96},{8,104},{16,112},{24,120},{32,0},{40,8},{48,16},{56,24},{64... | collective-permute-start | bytes 731144 | tf_op jit(solution)/shard_map/ppermute | solution.py:477
  141.4 4.2 %collective-permute-done.22.b1 = bf16[224,544]{1,0:T(8,128)(2,1)S(1)} collective-permute-done((bf16[224,544]{1,0:T(8,128)(2,1)}, bf16[224,544]{1,0:T(8,128)(2,1)S(1)}, u32[]{:S(2)}, u32[]{:S(2)}) %collective-permute-start.22) | collective-permute-done | bytes 243744 | tf_op jit(solution)/shard_map/ppermute | solution.py:476
  146.5 1.1 shard_map.159
  147.6 4.0 %all-to-all-start.4 = ((bf16[16,16,1280]{2,1,0:T(8,128)(2,1)}), bf16[16,16,1280]{2,1,0:T(8,128)(2,1)S(1)}, u32[]{:S(2)}, u32[]{:S(2)}) async-start(bf16[16,16,1280]{2,1,0:T(8,128)(2,1)} %shard_map.159), calls=%async_computation.4 | async-start | bytes 1310720 | tf_op jit(solution)/shard_map/all_to_all | solution.py:618
  151.7 4.7 %collective-permute-done.20.a2 = bf16[224,544]{1,0:T(8,128)(2,1)} collective-permute-done((bf16[224,544]{1,0:T(8,128)(2,1)}, bf16[224,544]{1,0:T(8,128)(2,1)}, u32[]{:S(2)}, u32[]{:S(2)}) %collective-permute-start.20) | collective-permute-done | bytes 243744 | tf_op jit(solution)/shard_map/ppermute | solution.py:477
  156.4 1.1 collective-permute-done.21.a3
  157.6 2.7 %shard_map.161 = (bf16[320,448]{1,0:T(8,128)(2,1)}, bf16[448,224]{1,0:T(8,128)(2,1)}) custom-call(bf16[224,544]{1,0:T(8,128)(2,1)} %get-tuple-element.104.a0, bf16[224,544]{1,0:T(8,128)(2,1)} %collective-permute-done.19.a1, bf16[224,544]{1,0:T(8,128)(2,1)} %collective-permute-done.20.a2, bf16[224,544]{1,0:T(8,128)(2,1)} %collective-permute-done.21.a3, ...), custom_call_target="tpu_custom_call" | custom-call | flops 40000000000 | bytes 100000000 | tf_op jit(solution)/shard_map/pallas_call | solution.py:444
  160.2 2.3 %all-to-all-done.4 = bf16[16,16,1280]{2,1,0:T(8,128)(2,1)S(1)} async-done(((bf16[16,16,1280]{2,1,0:T(8,128)(2,1)}), bf16[16,16,1280]{2,1,0:T(8,128)(2,1)S(1)}, u32[]{:S(2)}, u32[]{:S(2)}) %all-to-all-start.4) | async-done | bytes 655392 | tf_op jit(solution)/shard_map/all_to_all | solution.py:618
  (70 shorter events, 11.3 us)
Async XLA Ops:
  0.6 10.1 %copy-start.15 = (f32[1280]{0:T(1024)S(1)}, f32[1280]{0:T(1024)}, u32[]{:S(2)}) copy-start(f32[1280]{0:T(1024)} %param.14) | copy-start | bytes 15364
  0.6 10.7 %copy-start.16 = (f32[1280]{0:T(1024)S(1)}, f32[1280]{0:T(1024)}, u32[]{:S(2)}) copy-start(f32[1280]{0:T(1024)} %param.15) | copy-start | bytes 15364
  0.7 24.7 %collective-permute-start = (bf16[448,5120]{1,0:T(8,128)(2,1)}, bf16[448,5120]{1,0:T(8,128)(2,1)}, u32[]{:S(2)}, u32[]{:S(2)}) collective-permute-start(bf16[448,5120]{1,0:T(8,128)(2,1)} %bitcast.21), channel_id=1, source_target_pairs={{0,1},{1,0},{2,3},{3,2},{4,5},{5,4},{6,7},{7,6},{8,9},{9,8},{10,11... | collective-permute-start | bytes 13762568 | tf_op jit(solution)/shard_map/ppermute | solution.py:522
  0.7 24.6 %collective-permute-start.1 = (bf16[448,3584]{1,0:T(8,128)(2,1)}, bf16[448,3584]{1,0:T(8,128)(2,1)}, u32[]{:S(2)}, u32[]{:S(2)}) collective-permute-start(bf16[448,3584]{1,0:T(8,128)(2,1)} %out_own.1), channel_id=1, source_target_pairs={{0,1},{1,0},{2,3},{3,2},{4,5},{5,4},{6,7},{7,6},{8,9},{9,8},{10,11... | collective-permute-start | bytes 9633800 | tf_op jit(solution)/shard_map/ppermute | solution.py:522
  3.6 21.8 %all-to-all-start = ((bf16[16,48,448]{2,1,0:T(8,128)(2,1)}), bf16[16,48,448]{2,1,0:T(8,128)(2,1)S(1)}, u32[]{:S(2)}, u32[]{:S(2)}) async-start(bf16[16,48,448]{2,1,0:T(8,128)(2,1)} %shard_map.146), calls=%async_computation | async-start | bytes 1572864 | tf_op jit(solution)/shard_map/all_to_all | solution.py:561
  16.6 22.1 %collective-permute-start.5 = (bf16[48,5120]{1,0:T(8,128)(2,1)}, bf16[48,5120]{1,0:T(8,128)(2,1)S(1)}, u32[]{:S(2)}, u32[]{:S(2)}) collective-permute-start(bf16[48,5120]{1,0:T(8,128)(2,1)} %get-tuple-element.68.b0), channel_id=1, source_target_pairs={{0,2},{1,3},{2,4},{3,5},{4,6},{5,7},{6,0},{7,1},{8,10},{9,11},{10,... | collective-permute-start | bytes 1474568 | tf_op jit(solution)/shard_map/ppermute | solution.py:527
  18.5 26.0 %collective-permute-start.4 = (bf16[48,5120]{1,0:T(8,128)(2,1)}, bf16[48,5120]{1,0:T(8,128)(2,1)S(1)}, u32[]{:S(2)}, u32[]{:S(2)}) collective-permute-start(bf16[48,5120]{1,0:T(8,128)(2,1)} %get-tuple-element.68.b0), channel_id=1, source_target_pairs={{0,4},{1,5},{2,6},{3,7},{4,0},{5,1},{6,2},{7,3},{8,12},{9,13},{10,... | collective-permute-start | bytes 1474568 | tf_op jit(solution)/shard_map/ppermute | solution.py:526
  22.1 22.5 %collective-permute-start.3 = (bf16[48,5120]{1,0:T(8,128)(2,1)}, bf16[48,5120]{1,0:T(8,128)(2,1)}, u32[]{:S(2)}, u32[]{:S(2)}) collective-permute-start(bf16[48,5120]{1,0:T(8,128)(2,1)} %get-tuple-element.68.b0), channel_id=1, source_target_pairs={{0,6},{1,7},{2,0},{3,1},{4,2},{5,3},{6,4},{7,5},{8,14},{9,15},{10,... | collective-permute-start | bytes 1474568 | tf_op jit(solution)/shard_map/ppermute | solution.py:528
  25.4 1.0 copy-start.11
  28.8 1.7 %collective-permute-start.2 = (bf16[192,448]{1,0:T(8,128)(2,1)}, bf16[192,448]{1,0:T(8,128)(2,1)S(1)}, u32[]{:S(2)}, u32[]{:S(2)}) collective-permute-start(bf16[192,448]{1,0:T(8,128)(2,1)} %get-tuple-element.63), channel_id=1, source_target_pairs={{0,1},{1,0},{2,3},{3,2},{4,5},{5,4},{6,7},{7,6},{8,9},{9,8},{10,11... | collective-permute-start | bytes 516104 | tf_op jit(solution)/shard_map/ppermute | solution.py:522
  30.4 0.7 copy-start.14
  33.4 25.2 %all-to-all-start.1 = ((bf16[4,192,896]{2,1,0:T(8,128)(2,1)}), bf16[4,192,896]{2,1,0:T(8,128)(2,1)}, u32[]{:S(2)}, u32[]{:S(2)}) async-start(bf16[4,192,896]{2,1,0:T(8,128)(2,1)} %shard_map.149), calls=%async_computation.1 | async-start | bytes 2752512 | tf_op jit(solution)/shard_map/all_to_all | solution.py:533
  38.7 14.4 %copy-start.3 = (bf16[8,24,1280]{2,1,0:T(8,128)(2,1)S(1)}, bf16[8,24,1280]{2,1,0:T(8,128)(2,1)}, u32[]{:S(2)}) copy-start(bf16[8,24,1280]{2,1,0:T(8,128)(2,1)} %param.11) | copy-start | bytes 1474564
  38.7 5.8 %copy-start.12 = (bf16[48,5120]{1,0:T(8,128)(2,1)}, bf16[48,5120]{1,0:T(8,128)(2,1)S(1)}, u32[]{:S(2)}) copy-start(bf16[48,5120]{1,0:T(8,128)(2,1)S(1)} %collective-permute-done.5.b3) | copy-start | bytes 1474564
  44.6 0.8 copy-start.13
  53.0 20.4 %collective-permute-start.6 = (bf16[192,5120]{1,0:T(8,128)(2,1)}, bf16[192,5120]{1,0:T(8,128)(2,1)}, u32[]{:S(2)}, u32[]{:S(2)}) collective-permute-start(bf16[192,5120]{1,0:T(8,128)(2,1)} %get-tuple-element.76.refs_1_), channel_id=1, source_target_pairs={{0,1},{1,0},{2,3},{3,2},{4,5},{5,4},{6,7},{7,6},{8,9},{9,8},{10,11... | collective-permute-start | bytes 5898248 | tf_op jit(solution)/shard_map/ppermute | solution.py:522
  55.6 0.7 copy-start.4
  56.3 0.7 copy-start.8
  58.6 14.8 %collective-permute-start.7 = (bf16[4,192,896]{2,1,0:T(8,128)(2,1)}, bf16[4,192,896]{2,1,0:T(8,128)(2,1)}, u32[]{:S(2)}, u32[]{:S(2)}) collective-permute-start(bf16[4,192,896]{2,1,0:T(8,128)(2,1)} %all-to-all-done.1.og.refs_3_), channel_id=1, source_target_pairs={{0,1},{1,0},{2,3},{3,2},{4,5},{5,4},{6,7},{7,6},{8,9},{9,8},{10,11... | collective-permute-start | bytes 4128776 | tf_op jit(solution)/shard_map/ppermute | solution.py:522
  69.2 4.2 %collective-permute-start.8 = (bf16[896,192]{1,0:T(8,128)(2,1)}, bf16[896,192]{1,0:T(8,128)(2,1)}, u32[]{:S(2)}, u32[]{:S(2)}) collective-permute-start(bf16[896,192]{1,0:T(8,128)(2,1)} %get-tuple-element.80), channel_id=1, source_target_pairs={{0,1},{1,0},{2,3},{3,2},{4,5},{5,4},{6,7},{7,6},{8,9},{9,8},{10,11... | collective-permute-start | bytes 1032200 | tf_op jit(solution)/shard_map/ppermute | solution.py:522
  69.8 31.2 %all-to-all-start.2 = ((bf16[4,48,5120]{2,1,0:T(8,128)(2,1)}), bf16[4,48,5120]{2,1,0:T(8,128)(2,1)S(1)}, u32[]{:S(2)}, u32[]{:S(2)}) async-start(bf16[4,48,5120]{2,1,0:T(8,128)(2,1)} %bitcast.24), calls=%async_computation.2 | async-start | bytes 3932160 | tf_op jit(solution)/shard_map/all_to_all | solution.py:533
  79.6 18.0 %collective-permute-start.9 = (bf16[112,2176]{1,0:T(8,128)(2,1)}, bf16[112,2176]{1,0:T(8,128)(2,1)}, u32[]{:S(2)}, u32[]{:S(2)}) collective-permute-start(bf16[112,2176]{1,0:T(8,128)(2,1)} %get-tuple-element.81), channel_id=1, source_target_pairs={{0,8},{8,16},{16,24},{24,0},{32,40},{40,48},{48,56},{56,32},{64,72... | collective-permute-start | bytes 1462280 | tf_op jit(solution)/shard_map/ppermute | solution.py:593
  81.0 16.5 %collective-permute-start.10 = (bf16[112,2176]{1,0:T(8,128)(2,1)}, bf16[112,2176]{1,0:T(8,128)(2,1)}, u32[]{:S(2)}, u32[]{:S(2)}) collective-permute-start(bf16[112,2176]{1,0:T(8,128)(2,1)} %get-tuple-element.87), channel_id=1, source_target_pairs={{0,24},{8,0},{16,8},{24,16},{32,56},{40,32},{48,40},{56,48},{64,88... | collective-permute-start | bytes 1462280 | tf_op jit(solution)/shard_map/ppermute | solution.py:594
  82.8 14.7 %collective-permute-start.11 = (bf16[112,2176]{1,0:T(8,128)(2,1)}, bf16[112,2176]{1,0:T(8,128)(2,1)}, u32[]{:S(2)}, u32[]{:S(2)}) collective-permute-start(bf16[112,2176]{1,0:T(8,128)(2,1)} %get-tuple-element.88), channel_id=1, source_target_pairs={{0,32},{8,40},{16,48},{24,56},{32,64},{40,72},{48,80},{56,88},{64,... | collective-permute-start | bytes 1462280 | tf_op jit(solution)/shard_map/ppermute | solution.py:595
  84.4 13.1 %collective-permute-start.12 = (bf16[112,2176]{1,0:T(8,128)(2,1)}, bf16[112,2176]{1,0:T(8,128)(2,1)}, u32[]{:S(2)}, u32[]{:S(2)}) collective-permute-start(bf16[112,2176]{1,0:T(8,128)(2,1)} %get-tuple-element.89), channel_id=1, source_target_pairs={{0,96},{8,104},{16,112},{24,120},{32,0},{40,8},{48,16},{56,24},{64... | collective-permute-start | bytes 1462280 | tf_op jit(solution)/shard_map/ppermute | solution.py:596
  97.6 6.8 %copy-start.6 = (f32[1,1280]{1,0:T(1,128)S(1)}, f32[1,1280]{1,0:T(1,128)}, u32[]{:S(2)}) copy-start(f32[1,1280]{1,0:T(1,128)} %reshape.232.gain) | copy-start | bytes 15364
  101.1 23.9 %collective-permute-start.15 = (bf16[224,2176]{1,0:T(8,128)(2,1)}, bf16[224,2176]{1,0:T(8,128)(2,1)}, u32[]{:S(2)}, u32[]{:S(2)}) collective-permute-start(bf16[224,2176]{1,0:T(8,128)(2,1)} %get-tuple-element.98), channel_id=1, source_target_pairs={{0,32},{8,40},{16,48},{24,56},{32,64},{40,72},{48,80},{56,88},{64,... | collective-permute-start | bytes 2924552 | tf_op jit(solution)/shard_map/ppermute | solution.py:612
  101.9 23.1 %collective-permute-start.16 = (bf16[224,2176]{1,0:T(8,128)(2,1)}, bf16[224,2176]{1,0:T(8,128)(2,1)}, u32[]{:S(2)}, u32[]{:S(2)}) collective-permute-start(bf16[224,2176]{1,0:T(8,128)(2,1)} %get-tuple-element.99), channel_id=1, source_target_pairs={{0,96},{8,104},{16,112},{24,120},{32,0},{40,8},{48,16},{56,24},{64... | collective-permute-start | bytes 2924552 | tf_op jit(solution)/shard_map/ppermute | solution.py:612
  104.3 1.2 copy-start.7
  105.5 0.9 copy-start.10
  106.4 1.5 copy-start.9
  106.4 5.3 %copy-start.5 = (bf16[640,192]{1,0:T(8,128)(2,1)S(1)}, bf16[640,192]{1,0:T(8,128)(2,1)}, u32[]{:S(2)}) copy-start(bf16[640,192]{1,0:T(8,128)(2,1)} %copy-done.4) | copy-start | bytes 737284
  107.9 3.8 %collective-permute-start.14 = (bf16[192,1280]{1,0:T(8,128)(2,1)}, bf16[192,1280]{1,0:T(8,128)(2,1)S(1)}, u32[]{:S(2)}, u32[]{:S(2)}) collective-permute-start(bf16[192,1280]{1,0:T(8,128)(2,1)} %shard_map.156.grad), channel_id=1, source_target_pairs={{0,1},{1,0},{2,3},{3,2},{4,5},{5,4},{6,7},{7,6},{8,9},{9,8},{10,11... | collective-permute-start | bytes 1474568 | tf_op jit(solution)/shard_map/ppermute | solution.py:522
  107.9 2.2 %collective-permute-start.13 = (bf16[640,192]{1,0:T(8,128)(2,1)S(1)}, bf16[640,192]{1,0:T(8,128)(2,1)S(1)}, u32[]{:S(2)}, u32[]{:S(2)}) collective-permute-start(bf16[640,192]{1,0:T(8,128)(2,1)S(1)} %copy-done.9), channel_id=1, source_target_pairs={{0,1},{1,0},{2,3},{3,2},{4,5},{5,4},{6,7},{7,6},{8,9},{9,8},{10,11... | collective-permute-start | bytes 737288 | tf_op jit(solution)/shard_map/ppermute | solution.py:522
  108.4 26.4 %collective-permute-start.17 = (bf16[224,2176]{1,0:T(8,128)(2,1)}, bf16[224,2176]{1,0:T(8,128)(2,1)}, u32[]{:S(2)}, u32[]{:S(2)}) collective-permute-start(bf16[224,2176]{1,0:T(8,128)(2,1)} %get-tuple-element.90), channel_id=1, source_target_pairs={{0,8},{8,16},{16,24},{24,0},{32,40},{40,48},{48,56},{56,32},{64,72... | collective-permute-start | bytes 2924552 | tf_op jit(solution)/shard_map/ppermute | solution.py:614
  110.1 24.7 %collective-permute-start.18 = (bf16[224,2176]{1,0:T(8,128)(2,1)}, bf16[224,2176]{1,0:T(8,128)(2,1)}, u32[]{:S(2)}, u32[]{:S(2)}) collective-permute-start(bf16[224,2176]{1,0:T(8,128)(2,1)} %get-tuple-element.103), channel_id=1, source_target_pairs={{0,24},{8,0},{16,8},{24,16},{32,56},{40,32},{48,40},{56,48},{64,88... | collective-permute-start | bytes 2924552 | tf_op jit(solution)/shard_map/ppermute | solution.py:614
  111.8 1.0 copy-start.1
  114.6 1.2 copy-start
  115.8 4.9 %copy-start.2 = (bf16[192,1280]{1,0:T(8,128)(2,1)S(1)}, bf16[192,1280]{1,0:T(8,128)(2,1)}, u32[]{:S(2)}) copy-start(bf16[192,1280]{1,0:T(8,128)(2,1)} %shard_map.156.grad) | copy-start | bytes 1474564
  115.8 30.7 %all-to-all-start.3 = ((bf16[4,160,1280]{2,1,0:T(8,128)(2,1)}), bf16[4,160,1280]{2,1,0:T(8,128)(2,1)S(1)}, u32[]{:S(2)}, u32[]{:S(2)}) async-start(bf16[4,160,1280]{2,1,0:T(8,128)(2,1)} %bitcast.17), calls=%async_computation.3 | async-start | bytes 3276800 | tf_op jit(solution)/shard_map/all_to_all | solution.py:533
  128.4 17.2 %collective-permute-start.22 = (bf16[224,544]{1,0:T(8,128)(2,1)}, bf16[224,544]{1,0:T(8,128)(2,1)S(1)}, u32[]{:S(2)}, u32[]{:S(2)}) collective-permute-start(bf16[224,544]{1,0:T(8,128)(2,1)} %get-tuple-element.108), channel_id=1, source_target_pairs={{0,8},{8,16},{16,24},{24,0},{32,40},{40,48},{48,56},{56,32},{64,72... | collective-permute-start | bytes 731144 | tf_op jit(solution)/shard_map/ppermute | solution.py:476
  129.0 22.7 %collective-permute-start.23 = (bf16[224,544]{1,0:T(8,128)(2,1)}, bf16[224,544]{1,0:T(8,128)(2,1)}, u32[]{:S(2)}, u32[]{:S(2)}) collective-permute-start(bf16[224,544]{1,0:T(8,128)(2,1)} %get-tuple-element.109), channel_id=1, source_target_pairs={{0,24},{8,0},{16,8},{24,16},{32,56},{40,32},{48,40},{56,48},{64,88... | collective-permute-start | bytes 731144 | tf_op jit(solution)/shard_map/ppermute | solution.py:477
  131.8 19.9 %collective-permute-start.24 = (bf16[224,544]{1,0:T(8,128)(2,1)}, bf16[224,544]{1,0:T(8,128)(2,1)}, u32[]{:S(2)}, u32[]{:S(2)}) collective-permute-start(bf16[224,544]{1,0:T(8,128)(2,1)} %get-tuple-element.110), channel_id=1, source_target_pairs={{0,16},{8,24},{16,0},{24,8},{32,48},{40,56},{48,32},{56,40},{64,80... | collective-permute-start | bytes 731144 | tf_op jit(solution)/shard_map/ppermute | solution.py:475
  138.2 13.5 %collective-permute-start.19 = (bf16[224,544]{1,0:T(8,128)(2,1)}, bf16[224,544]{1,0:T(8,128)(2,1)}, u32[]{:S(2)}, u32[]{:S(2)}) collective-permute-start(bf16[224,544]{1,0:T(8,128)(2,1)} %get-tuple-element.105), channel_id=1, source_target_pairs={{0,32},{8,40},{16,48},{24,56},{32,64},{40,72},{48,80},{56,88},{64,... | collective-permute-start | bytes 731144 | tf_op jit(solution)/shard_map/ppermute | solution.py:476
  138.2 18.2 %collective-permute-start.20 = (bf16[224,544]{1,0:T(8,128)(2,1)}, bf16[224,544]{1,0:T(8,128)(2,1)}, u32[]{:S(2)}, u32[]{:S(2)}) collective-permute-start(bf16[224,544]{1,0:T(8,128)(2,1)} %get-tuple-element.106), channel_id=1, source_target_pairs={{0,96},{8,104},{16,112},{24,120},{32,0},{40,8},{48,16},{56,24},{64... | collective-permute-start | bytes 731144 | tf_op jit(solution)/shard_map/ppermute | solution.py:477
  145.6 11.9 %copy-start.17 = (bf16[224,544]{1,0:T(8,128)(2,1)}, bf16[224,544]{1,0:T(8,128)(2,1)S(1)}, u32[]{:S(2)}) copy-start(bf16[224,544]{1,0:T(8,128)(2,1)S(1)} %collective-permute-done.22.b1) | copy-start | bytes 731140
  145.6 11.9 %collective-permute-start.21 = (bf16[224,544]{1,0:T(8,128)(2,1)}, bf16[224,544]{1,0:T(8,128)(2,1)}, u32[]{:S(2)}, u32[]{:S(2)}) collective-permute-start(bf16[224,544]{1,0:T(8,128)(2,1)} %get-tuple-element.107), channel_id=1, source_target_pairs={{0,64},{8,72},{16,80},{24,88},{32,96},{40,104},{48,112},{56,120},{... | collective-permute-start | bytes 731144 | tf_op jit(solution)/shard_map/ppermute | solution.py:475
  147.6 14.9 %all-to-all-start.4 = ((bf16[16,16,1280]{2,1,0:T(8,128)(2,1)}), bf16[16,16,1280]{2,1,0:T(8,128)(2,1)S(1)}, u32[]{:S(2)}, u32[]{:S(2)}) async-start(bf16[16,16,1280]{2,1,0:T(8,128)(2,1)} %shard_map.159), calls=%async_computation.4 | async-start | bytes 1310720 | tf_op jit(solution)/shard_map/all_to_all | solution.py:618

commit v7 on v6

--- a/solution.py
+++ b/solution.py
@@ -578,7 +578,7 @@
     rows, _ = lax.optimization_barrier((rows, grad_pair))
     stk, hid_own, hid_other, slope_own, slope_other = preact_of(ids, rows, in_own, in_other)
     stk_other = swap(stk)
-    og, _ = lax.optimization_barrier((og, context_give))
+    og, _ = lax.optimization_barrier((og, context_got))
     og_other = swap(og)
     row_part, pre_own, send = pre_grad_of(
         og, adapter_out, out_other, in_own, in_other, hid_other, slope_own, slope_other

time: 164 us -> 165 us (level)
  starting transfers between devices: 53.3 us -> 59.9 us
  waiting for transfers between devices: 26.8 us -> 21 us
    ppermute x2, starting transfers between devices: 1.6 us -> 7.5 us  [ring_of(): far = lax.ppermute(parts[2], 'seq', shift(2))]
    ppermute x2, waiting for transfers between devices: 4.21 us -> 0.01 us  [ring_of(): up = lax.ppermute(parts[1], 'seq', shift(1))]
    ppermute x1, waiting for transfers between devices: 2.27 us -> 0.45 us  [per_device(): lax.ppermute(x_down, 'seq', x_shift(-1))]
  transfers between devices with their start and end apart: 30 -> 30, of which waited for: 11 -> 10; matrix products, arithmetic and copies ran while one was open for 4% -> 4% of each run, Pallas kernels for 41% -> 41%
where the time goes in v7:
time: 165 us; the launch traced here: 164 us
  Pallas kernels  67.5 us (41%)
  starting transfers between devices  59.9 us (36%)
  waiting for transfers between devices  21 us (13%)
  local copies, waits for them, and re-layouts  10 us (6%)
  matrix products  3.93 us (2%)
    pallas_call x2, Pallas kernels, weight_grads_of(): pl.pallas_call(kernel, out_shape=tuple((struct(shape, BF16) for shape in...  17.6 us
    all_to_all x3, starting transfers between devices, z_exchange(): lax.all_to_all(parts, 'tp', split_axis=0, concat_axis=0, axis_index_group...  13.7 us
    pallas_call x1, Pallas kernels, pre_grad_of(): pl.pallas_call(pre_grad_kernel, out_shape=(struct((192, 5120), BF16), str...  10.6 us
    unnamed x36, local copies, waits for them, and re-layouts  8.21 us
    pallas_call x1, Pallas kernels, preact_of(): pl.pallas_call(preact_kernel, out_shape=(struct((192, 5120), BF16), struc...  7.65 us
    ppermute x2, starting transfers between devices, ring_of(): far = lax.ppermute(parts[2], 'seq', shift(2))  7.5 us
    all_to_all x1, starting transfers between devices, per_device(): lax.all_to_all(parcels, 'seq', split_axis=0, concat_axis=0, tiled=True)  7.12 us
    pallas_call x2, Pallas kernels, spread_of(): pl.pallas_call(spread_kernel, out_shape=(struct((224, 544), BF16),) * 4,...  6.72 us
  transfers between devices with their start and end apart: 30, of which 10 were waited for; matrix products, arithmetic and copies ran while one was open for 4% of the time, Pallas kernels for 41%

profile of v7, /device:TPU:0, one launch (start us, length us, event | category | flops | bytes accessed | tf_op | source)
XLA Modules:
  0.0 163.9 jit_solution(10824347228830206947)
XLA Ops:
  1.2 2.4 %shard_map.146 = bf16[16,48,448]{2,1,0:T(8,128)(2,1)} custom-call(s32[128]{0:T(128)} %offsets.1, s32[128]{0:T(128)} %frames.1, s32[128]{0:T(128)} %owner.1, bf16[448,384]{1,0:T(8,128)(2,1)} %bitcast.27), custom_call_target="tpu_custom_call" | custom-call | flops 1 | bytes 1 | tf_op jit(solution)/shard_map/pallas_call | solution.py:79
  3.6 7.1 %all-to-all-start = ((bf16[16,48,448]{2,1,0:T(8,128)(2,1)}), bf16[16,48,448]{2,1,0:T(8,128)(2,1)S(1)}, u32[]{:S(2)}, u32[]{:S(2)}) async-start(bf16[16,48,448]{2,1,0:T(8,128)(2,1)} %shard_map.146), calls=%async_computation | async-start | bytes 1572864 | tf_op jit(solution)/shard_map/all_to_all | solution.py:561
  11.9 4.7 %shard_map.147 = (bf16[48,5120]{1,0:T(8,128)(2,1)}, f32[192,1280]{1,0:T(8,128)}, f32[192,128]{1,0:T(8,128)}) custom-call(bf16[192,1280]{1,0:T(8,128)(2,1)} %bitcast.19, bf16[192,1280]{1,0:T(8,128)(2,1)} %bitcast.25, bf16[1280,1280]{1,0:T(8,128)(2,1)} %weight.1, f32[1,1280]{1,0:T(1,128)} %reshape.232.gain, f32[1,1280]{1,0:T(1,128)} %reshape.233.bias), custom_call_target="tpu_custom_call" | custom-call | flops 1 | bytes 1 | tf_op jit(solution)/shard_map/pallas_call | solution.py:156
  16.6 1.9 %collective-permute-start.6 = (bf16[48,5120]{1,0:T(8,128)(2,1)}, bf16[48,5120]{1,0:T(8,128)(2,1)S(1)}, u32[]{:S(2)}, u32[]{:S(2)}) collective-permute-start(bf16[48,5120]{1,0:T(8,128)(2,1)} %get-tuple-element.68.b0), channel_id=1, source_target_pairs={{0,2},{1,3},{2,4},{3,5},{4,6},{5,7},{6,0},{7,1},{8,10},{9,11},{10,... | collective-permute-start | bytes 1474568 | tf_op jit(solution)/shard_map/ppermute | solution.py:527
  18.5 3.6 %collective-permute-start.5 = (bf16[48,5120]{1,0:T(8,128)(2,1)}, bf16[48,5120]{1,0:T(8,128)(2,1)S(1)}, u32[]{:S(2)}, u32[]{:S(2)}) collective-permute-start(bf16[48,5120]{1,0:T(8,128)(2,1)} %get-tuple-element.68.b0), channel_id=1, source_target_pairs={{0,4},{1,5},{2,6},{3,7},{4,0},{5,1},{6,2},{7,3},{8,12},{9,13},{10,... | collective-permute-start | bytes 1474568 | tf_op jit(solution)/shard_map/ppermute | solution.py:526
  22.1 1.0 collective-permute-start.4
  23.7 1.6 %all-to-all-done.arrived = bf16[16,48,448]{2,1,0:T(8,128)(2,1)S(1)} async-done(((bf16[16,48,448]{2,1,0:T(8,128)(2,1)}), bf16[16,48,448]{2,1,0:T(8,128)(2,1)S(1)}, u32[]{:S(2)}, u32[]{:S(2)}) %all-to-all-start) | async-done | bytes 688160 | tf_op jit(solution)/shard_map/all_to_all | solution.py:561
  25.4 1.0 copy-done.11
  26.3 2.4 %shard_map.148 = (bf16[192,448]{1,0:T(8,128)(2,1)}, bf16[192,448]{1,0:T(8,128)(2,1)}) custom-call(s32[5]{0:T(128)} %stack.23.ids.refs_0_, s32[1,128]{1,0:T(1,128)} %bitcast.29, bf16[16,48,448]{2,1,0:T(8,128)(2,1)} %copy-done.11), custom_call_target="tpu_custom_call" | custom-call | flops 1 | bytes 1 | tf_op jit(solution)/shard_map/pallas_call | solution.py:109
  28.9 1.5 collective-permute-done.2.got
  31.1 2.3 %shard_map.149 = bf16[4,192,896]{2,1,0:T(8,128)(2,1)} custom-call(s32[5]{0:T(128)} %stack.23.ids.refs_0_, bf16[192,448]{1,0:T(8,128)(2,1)} %get-tuple-element.62.keep, bf16[192,448]{1,0:T(8,128)(2,1)} %copy-done.14), custom_call_target="tpu_custom_call" | custom-call | flops 1 | bytes 1 | tf_op jit(solution)/shard_map/pallas_call | solution.py:129
  33.4 5.3 %all-to-all-start.1 = ((bf16[4,192,896]{2,1,0:T(8,128)(2,1)}), bf16[4,192,896]{2,1,0:T(8,128)(2,1)}, u32[]{:S(2)}, u32[]{:S(2)}) async-start(bf16[4,192,896]{2,1,0:T(8,128)(2,1)} %shard_map.149), calls=%async_computation.1 | async-start | bytes 2752512 | tf_op jit(solution)/shard_map/all_to_all | solution.py:533
  38.7 5.8 %collective-permute-done.5.b2 = bf16[48,5120]{1,0:T(8,128)(2,1)S(1)} collective-permute-done((bf16[48,5120]{1,0:T(8,128)(2,1)}, bf16[48,5120]{1,0:T(8,128)(2,1)S(1)}, u32[]{:S(2)}, u32[]{:S(2)}) %collective-permute-start.5) | collective-permute-done | bytes 491552 | tf_op jit(solution)/shard_map/ppermute | solution.py:526
  45.3 7.7 %shard_map.151 = (bf16[192,5120]{1,0:T(8,128)(2,1)}, bf16[448,192]{1,0:T(8,128)(2,1)}, bf16[448,192]{1,0:T(8,128)(2,1)}, f32[448,192]{1,0:T(8,128)}, f32[448,192]{1,0:T(8,128)}) custom-call(s32[5]{0:T(128)} %stack.23.ids.refs_0_, bf16[48,5120]{1,0:T(8,128)(2,1)} %get-tuple-element.68.b0, bf16[48,5120]{1,0:T(8,128)(2,1)} %collective-permute-done.4.b1, ...), custom_call_target="tpu_custom_call" | custom-call | flops 1 | bytes 1 | tf_op jit(solution)/shard_map/pallas_call | solution.py:220
  53.1 2.5 %shard_map.150 = (bf16[640,192]{1,0:T(8,128)(2,1)S(1)}, bf16[640,192]{1,0:T(8,128)(2,1)S(1)}) custom-call(s32[1,1280]{1,0:T(1,128)S(1)} %fusion.1.target.target_other, s32[1,1280]{1,0:T(1,128)S(1)} %fusion.1.target.target_other, bf16[192,1280]{1,0:T(8,128)(2,1)S(1)} %bitcast.20), custom_call_target="tpu_custom_call" | custom-call | flops 40000000000 | bytes 100000000 | tf_op jit(solution)/shard_map/pallas_call | solution.py:489
  56.8 1.3 collective-permute-done.3.ctx_other
  59.2 10.6 %shard_map.152 = (bf16[192,5120]{1,0:T(8,128)(2,1)}, bf16[448,192]{1,0:T(8,128)(2,1)}, bf16[896,192]{1,0:T(8,128)(2,1)}) custom-call(bf16[4,192,896]{2,1,0:T(8,128)(2,1)} %all-to-all-done.1.og.refs_3_, bf16[448,3584]{1,0:T(8,128)(2,1)} %out_own.1, bf16[448,3584]{1,0:T(8,128)(2,1)} %collective-permute-done.1.out_other, bf16[448,5120]{1,0:T(8,128)(2,1)} %bitcast.23, ...), custom_call_target="tpu_custom_call" | custom-call | flops 1 | bytes 1 | tf_op jit(solution)/shard_map/pallas_call | solution.py:294
  70.0 3.6 %all-to-all-start.2 = ((bf16[4,48,5120]{2,1,0:T(8,128)(2,1)}), bf16[4,48,5120]{2,1,0:T(8,128)(2,1)S(1)}, u32[]{:S(2)}, u32[]{:S(2)}) async-start(bf16[4,48,5120]{2,1,0:T(8,128)(2,1)} %bitcast.24), calls=%async_computation.2 | async-start | bytes 3932160 | tf_op jit(solution)/shard_map/all_to_all | solution.py:533
  73.7 6.1 %shard_map.153 = (bf16[112,2176]{1,0:T(8,128)(2,1)}, bf16[112,2176]{1,0:T(8,128)(2,1)}, bf16[112,2176]{1,0:T(8,128)(2,1)}, bf16[112,2176]{1,0:T(8,128)(2,1)}) custom-call(s32[5]{0:T(128)} %stack.23.ids.refs_0_, bf16[192,5120]{1,0:T(8,128)(2,1)} %get-tuple-element.76.refs_1_, bf16[192,5120]{1,0:T(8,128)(2,1)} %collective-permute-done.7.refs_2_, ...), custom_call_target="tpu_custom_call" | custom-call | flops 1 | bytes 1 | tf_op jit(solution)/shard_map/pallas_call | solution.py:373
  79.8 2.2 %collective-permute-start.10 = (bf16[112,2176]{1,0:T(8,128)(2,1)}, bf16[112,2176]{1,0:T(8,128)(2,1)}, u32[]{:S(2)}, u32[]{:S(2)}) collective-permute-start(bf16[112,2176]{1,0:T(8,128)(2,1)} %get-tuple-element.81), channel_id=1, source_target_pairs={{0,8},{8,16},{16,24},{24,0},{32,40},{40,48},{48,56},{56,32},{64,72... | collective-permute-start | bytes 1462280 | tf_op jit(solution)/shard_map/ppermute | solution.py:593
  82.0 1.4 collective-permute-start.11
  83.3 2.0 %collective-permute-start.12 = (bf16[112,2176]{1,0:T(8,128)(2,1)}, bf16[112,2176]{1,0:T(8,128)(2,1)}, u32[]{:S(2)}, u32[]{:S(2)}) collective-permute-start(bf16[112,2176]{1,0:T(8,128)(2,1)} %get-tuple-element.88), channel_id=1, source_target_pairs={{0,32},{8,40},{16,48},{24,56},{32,64},{40,72},{48,80},{56,88},{64,... | collective-permute-start | bytes 1462280 | tf_op jit(solution)/shard_map/ppermute | solution.py:595
  85.3 1.2 collective-permute-start.13
  86.6 11.5 %shard_map.154 = (bf16[224,2176]{1,0:T(8,128)(2,1)}, bf16[224,2176]{1,0:T(8,128)(2,1)}, bf16[224,2176]{1,0:T(8,128)(2,1)}, bf16[224,2176]{1,0:T(8,128)(2,1)}, bf...) custom-call(s32[5]{0:T(128)} %stack.23.ids.refs_0_, bf16[192,5120]{1,0:T(8,128)(2,1)} %get-tuple-element.76.refs_1_, ...), custom_call_target="tpu_custom_call" | custom-call | flops 40000000000 | bytes 100000000 | tf_op jit(solution)/shard_map/pallas_call | solution.py:373
  98.2 3.5 %shard_map.155 = (bf16[224,2176]{1,0:T(8,128)(2,1)}, bf16[224,2176]{1,0:T(8,128)(2,1)}, bf16[224,2176]{1,0:T(8,128)(2,1)}, bf16[224,2176]{1,0:T(8,128)(2,1)}) custom-call(bf16[224,2176]{1,0:T(8,128)(2,1)} %get-tuple-element.83.x_up, ...), custom_call_target="tpu_custom_call", output_to_operand_aliasing={{0}: (0, {}), {1}: (1, {}), {2}: (2, {}), {3}: (3, {})} | custom-call | flops 1 | bytes 1 | tf_op jit(solution)/shard_map/pallas_call | solution.py:397
  101.7 1.5 collective-permute-start.15
  103.2 1.8 %collective-permute-start.16 = (bf16[224,2176]{1,0:T(8,128)(2,1)}, bf16[224,2176]{1,0:T(8,128)(2,1)}, u32[]{:S(2)}, u32[]{:S(2)}) collective-permute-start(bf16[224,2176]{1,0:T(8,128)(2,1)} %get-tuple-element.99), channel_id=1, source_target_pairs={{0,96},{8,104},{16,112},{24,120},{32,0},{40,8},{48,16},{56,24},{64... | collective-permute-start | bytes 2924552 | tf_op jit(solution)/shard_map/ppermute | solution.py:612
  104.9 1.2 copy-done.9
  106.2 0.9 copy-done.10
  107.0 1.5 shard_map.156.grad
  109.3 2.5 %collective-permute-start.18 = (bf16[224,2176]{1,0:T(8,128)(2,1)}, bf16[224,2176]{1,0:T(8,128)(2,1)}, u32[]{:S(2)}, u32[]{:S(2)}) collective-permute-start(bf16[224,2176]{1,0:T(8,128)(2,1)} %get-tuple-element.103), channel_id=1, source_target_pairs={{0,24},{8,0},{16,8},{24,16},{32,56},{40,32},{48,40},{56,48},{64,88... | collective-permute-start | bytes 2924552 | tf_op jit(solution)/shard_map/ppermute | solution.py:614
  111.8 1.0 copy-done.1
  112.8 1.8 %shard_map.157 = bf16[640,1280]{1,0:T(8,128)(2,1)S(1)} custom-call(bf16[640,192]{1,0:T(8,128)(2,1)S(1)} %copy-done.5, bf16[640,192]{1,0:T(8,128)(2,1)S(1)} %copy-done.7, bf16[192,1280]{1,0:T(8,128)(2,1)S(1)} %copy-done.1, bf16[192,1280]{1,0:T(8,128)(2,1)S(1)} %collective-permute-done.14.grad_other), custom_call_target="tpu_custom_call" | custom-call | flops 1 | bytes 1 | tf_op jit(solution)/shard_map/pallas_call | solution.py:510
  114.7 1.2 copy-done
  115.9 4.8 %all-to-all-start.3 = ((bf16[4,160,1280]{2,1,0:T(8,128)(2,1)}), bf16[4,160,1280]{2,1,0:T(8,128)(2,1)S(1)}, u32[]{:S(2)}, u32[]{:S(2)}) async-start(bf16[4,160,1280]{2,1,0:T(8,128)(2,1)} %bitcast.17), calls=%async_computation.3 | async-start | bytes 3276800 | tf_op jit(solution)/shard_map/all_to_all | solution.py:533
  120.6 3.9 %convolution_convert_fusion = bf16[192,1280]{1,0:T(8,128)(2,1)} fusion(bf16[192,1280]{1,0:T(8,128)(2,1)S(1)} %copy-done.2, bf16[1280,1280]{1,0:T(8,128)(2,1)} %weight.1), kind=kOutput, calls=%fused_computation | convolution fusion | flops 629391360 | bytes 4259840 | tf_op jit(solution)/shard_map/dot_general | solution.py:39
  124.6 1.6 collective-permute-done.15.b
  126.1 3.4 %shard_map.158 = (bf16[224,544]{1,0:T(8,128)(2,1)}, bf16[224,544]{1,0:T(8,128)(2,1)}, bf16[224,544]{1,0:T(8,128)(2,1)}, bf16[224,544]{1,0:T(8,128)(2,1)}) custom-call(s32[1]{0:T(128)} %bitcast.1.where, bf16[224,2176]{1,0:T(8,128)(2,1)} %get-tuple-element.97.a, bf16[224,2176]{1,0:T(8,128)(2,1)} %collective-permute-done.15.b, ...), custom_call_target="tpu_custom_call" | custom-call | flops 40000000000 | bytes 100000000 | tf_op jit(solution)/shard_map/pallas_call | solution.py:424
  130.0 2.7 %collective-permute-start.23 = (bf16[224,544]{1,0:T(8,128)(2,1)}, bf16[224,544]{1,0:T(8,128)(2,1)}, u32[]{:S(2)}, u32[]{:S(2)}) collective-permute-start(bf16[224,544]{1,0:T(8,128)(2,1)} %get-tuple-element.109), channel_id=1, source_target_pairs={{0,24},{8,0},{16,8},{24,16},{32,56},{40,32},{48,40},{56,48},{64,88... | collective-permute-start | bytes 731144 | tf_op jit(solution)/shard_map/ppermute | solution.py:477
  132.7 0.8 collective-permute-start.24
  134.5 3.4 %shard_map.160 = (bf16[224,544]{1,0:T(8,128)(2,1)}, bf16[224,544]{1,0:T(8,128)(2,1)}, bf16[224,544]{1,0:T(8,128)(2,1)}, bf16[224,544]{1,0:T(8,128)(2,1)}) custom-call(s32[1]{0:T(128)} %bitcast.where, bf16[224,2176]{1,0:T(8,128)(2,1)} %get-tuple-element.102.a, bf16[224,2176]{1,0:T(8,128)(2,1)} %collective-permute-done.17.b, ...), custom_call_target="tpu_custom_call" | custom-call | flops 40000000000 | bytes 100000000 | tf_op jit(solution)/shard_map/pallas_call | solution.py:424
  138.1 3.0 %collective-permute-start.20 = (bf16[224,544]{1,0:T(8,128)(2,1)}, bf16[224,544]{1,0:T(8,128)(2,1)}, u32[]{:S(2)}, u32[]{:S(2)}) collective-permute-start(bf16[224,544]{1,0:T(8,128)(2,1)} %get-tuple-element.106), channel_id=1, source_target_pairs={{0,96},{8,104},{16,112},{24,120},{32,0},{40,8},{48,16},{56,24},{64... | collective-permute-start | bytes 731144 | tf_op jit(solution)/shard_map/ppermute | solution.py:477
  141.1 6.7 %collective-permute-start.21 = (bf16[224,544]{1,0:T(8,128)(2,1)}, bf16[224,544]{1,0:T(8,128)(2,1)}, u32[]{:S(2)}, u32[]{:S(2)}) collective-permute-start(bf16[224,544]{1,0:T(8,128)(2,1)} %get-tuple-element.107), channel_id=1, source_target_pairs={{0,64},{8,72},{16,80},{24,88},{32,96},{40,104},{48,112},{56,120},{... | collective-permute-start | bytes 731144 | tf_op jit(solution)/shard_map/ppermute | solution.py:475
  147.7 1.1 shard_map.159
  148.8 3.6 %all-to-all-start.4 = ((bf16[16,16,1280]{2,1,0:T(8,128)(2,1)}), bf16[16,16,1280]{2,1,0:T(8,128)(2,1)S(1)}, u32[]{:S(2)}, u32[]{:S(2)}) async-start(bf16[16,16,1280]{2,1,0:T(8,128)(2,1)} %shard_map.159), calls=%async_computation.4 | async-start | bytes 1310720 | tf_op jit(solution)/shard_map/all_to_all | solution.py:618
  152.4 4.4 %collective-permute-done.20.a2 = bf16[224,544]{1,0:T(8,128)(2,1)} collective-permute-done((bf16[224,544]{1,0:T(8,128)(2,1)}, bf16[224,544]{1,0:T(8,128)(2,1)}, u32[]{:S(2)}, u32[]{:S(2)}) %collective-permute-start.20) | collective-permute-done | bytes 243744 | tf_op jit(solution)/shard_map/ppermute | solution.py:477
  156.8 2.7 %shard_map.161 = (bf16[320,448]{1,0:T(8,128)(2,1)}, bf16[448,224]{1,0:T(8,128)(2,1)}) custom-call(bf16[224,544]{1,0:T(8,128)(2,1)} %get-tuple-element.104.a0, bf16[224,544]{1,0:T(8,128)(2,1)} %collective-permute-done.19.a1, bf16[224,544]{1,0:T(8,128)(2,1)} %collective-permute-done.20.a2, bf16[224,544]{1,0:T(8,128)(2,1)} %collective-permute-done.21.a3, ...), custom_call_target="tpu_custom_call" | custom-call | flops 40000000000 | bytes 100000000 | tf_op jit(solution)/shard_map/pallas_call | solution.py:444
  159.5 3.7 %all-to-all-done.4 = bf16[16,16,1280]{2,1,0:T(8,128)(2,1)S(1)} async-done(((bf16[16,16,1280]{2,1,0:T(8,128)(2,1)}), bf16[16,16,1280]{2,1,0:T(8,128)(2,1)S(1)}, u32[]{:S(2)}, u32[]{:S(2)}) %all-to-all-start.4) | async-done | bytes 655392 | tf_op jit(solution)/shard_map/all_to_all | solution.py:618
  (70 shorter events, 9.9 us)
Async XLA Ops:
  0.6 10.1 %copy-start.15 = (f32[1280]{0:T(1024)S(1)}, f32[1280]{0:T(1024)}, u32[]{:S(2)}) copy-start(f32[1280]{0:T(1024)} %param.14) | copy-start | bytes 15364
  0.6 10.7 %copy-start.16 = (f32[1280]{0:T(1024)S(1)}, f32[1280]{0:T(1024)}, u32[]{:S(2)}) copy-start(f32[1280]{0:T(1024)} %param.15) | copy-start | bytes 15364
  0.7 24.7 %collective-permute-start = (bf16[448,5120]{1,0:T(8,128)(2,1)}, bf16[448,5120]{1,0:T(8,128)(2,1)}, u32[]{:S(2)}, u32[]{:S(2)}) collective-permute-start(bf16[448,5120]{1,0:T(8,128)(2,1)} %bitcast.21), channel_id=1, source_target_pairs={{0,1},{1,0},{2,3},{3,2},{4,5},{5,4},{6,7},{7,6},{8,9},{9,8},{10,11... | collective-permute-start | bytes 13762568 | tf_op jit(solution)/shard_map/ppermute | solution.py:522
  0.7 24.6 %collective-permute-start.1 = (bf16[448,3584]{1,0:T(8,128)(2,1)}, bf16[448,3584]{1,0:T(8,128)(2,1)}, u32[]{:S(2)}, u32[]{:S(2)}) collective-permute-start(bf16[448,3584]{1,0:T(8,128)(2,1)} %out_own.1), channel_id=1, source_target_pairs={{0,1},{1,0},{2,3},{3,2},{4,5},{5,4},{6,7},{7,6},{8,9},{9,8},{10,11... | collective-permute-start | bytes 9633800 | tf_op jit(solution)/shard_map/ppermute | solution.py:522
  3.6 21.8 %all-to-all-start = ((bf16[16,48,448]{2,1,0:T(8,128)(2,1)}), bf16[16,48,448]{2,1,0:T(8,128)(2,1)S(1)}, u32[]{:S(2)}, u32[]{:S(2)}) async-start(bf16[16,48,448]{2,1,0:T(8,128)(2,1)} %shard_map.146), calls=%async_computation | async-start | bytes 1572864 | tf_op jit(solution)/shard_map/all_to_all | solution.py:561
  16.6 22.1 %collective-permute-start.6 = (bf16[48,5120]{1,0:T(8,128)(2,1)}, bf16[48,5120]{1,0:T(8,128)(2,1)S(1)}, u32[]{:S(2)}, u32[]{:S(2)}) collective-permute-start(bf16[48,5120]{1,0:T(8,128)(2,1)} %get-tuple-element.68.b0), channel_id=1, source_target_pairs={{0,2},{1,3},{2,4},{3,5},{4,6},{5,7},{6,0},{7,1},{8,10},{9,11},{10,... | collective-permute-start | bytes 1474568 | tf_op jit(solution)/shard_map/ppermute | solution.py:527
  18.5 26.0 %collective-permute-start.5 = (bf16[48,5120]{1,0:T(8,128)(2,1)}, bf16[48,5120]{1,0:T(8,128)(2,1)S(1)}, u32[]{:S(2)}, u32[]{:S(2)}) collective-permute-start(bf16[48,5120]{1,0:T(8,128)(2,1)} %get-tuple-element.68.b0), channel_id=1, source_target_pairs={{0,4},{1,5},{2,6},{3,7},{4,0},{5,1},{6,2},{7,3},{8,12},{9,13},{10,... | collective-permute-start | bytes 1474568 | tf_op jit(solution)/shard_map/ppermute | solution.py:526
  22.1 22.5 %collective-permute-start.4 = (bf16[48,5120]{1,0:T(8,128)(2,1)}, bf16[48,5120]{1,0:T(8,128)(2,1)}, u32[]{:S(2)}, u32[]{:S(2)}) collective-permute-start(bf16[48,5120]{1,0:T(8,128)(2,1)} %get-tuple-element.68.b0), channel_id=1, source_target_pairs={{0,6},{1,7},{2,0},{3,1},{4,2},{5,3},{6,4},{7,5},{8,14},{9,15},{10,... | collective-permute-start | bytes 1474568 | tf_op jit(solution)/shard_map/ppermute | solution.py:528
  25.4 1.0 copy-start.11
  28.8 1.7 %collective-permute-start.2 = (bf16[192,448]{1,0:T(8,128)(2,1)}, bf16[192,448]{1,0:T(8,128)(2,1)S(1)}, u32[]{:S(2)}, u32[]{:S(2)}) collective-permute-start(bf16[192,448]{1,0:T(8,128)(2,1)} %get-tuple-element.63), channel_id=1, source_target_pairs={{0,1},{1,0},{2,3},{3,2},{4,5},{5,4},{6,7},{7,6},{8,9},{9,8},{10,11... | collective-permute-start | bytes 516104 | tf_op jit(solution)/shard_map/ppermute | solution.py:522
  30.4 0.7 copy-start.14
  33.4 25.4 %all-to-all-start.1 = ((bf16[4,192,896]{2,1,0:T(8,128)(2,1)}), bf16[4,192,896]{2,1,0:T(8,128)(2,1)}, u32[]{:S(2)}, u32[]{:S(2)}) async-start(bf16[4,192,896]{2,1,0:T(8,128)(2,1)} %shard_map.149), calls=%async_computation.1 | async-start | bytes 2752512 | tf_op jit(solution)/shard_map/all_to_all | solution.py:533
  38.7 14.4 %copy-start.3 = (bf16[8,24,1280]{2,1,0:T(8,128)(2,1)S(1)}, bf16[8,24,1280]{2,1,0:T(8,128)(2,1)}, u32[]{:S(2)}) copy-start(bf16[8,24,1280]{2,1,0:T(8,128)(2,1)} %param.11) | copy-start | bytes 1474564
  38.7 5.8 %copy-start.12 = (bf16[48,5120]{1,0:T(8,128)(2,1)}, bf16[48,5120]{1,0:T(8,128)(2,1)S(1)}, u32[]{:S(2)}) copy-start(bf16[48,5120]{1,0:T(8,128)(2,1)S(1)} %collective-permute-done.6.b3) | copy-start | bytes 1474564
  44.6 0.8 copy-start.13
  53.0 20.6 %collective-permute-start.7 = (bf16[192,5120]{1,0:T(8,128)(2,1)}, bf16[192,5120]{1,0:T(8,128)(2,1)}, u32[]{:S(2)}, u32[]{:S(2)}) collective-permute-start(bf16[192,5120]{1,0:T(8,128)(2,1)} %get-tuple-element.76.refs_1_), channel_id=1, source_target_pairs={{0,1},{1,0},{2,3},{3,2},{4,5},{5,4},{6,7},{7,6},{8,9},{9,8},{10,11... | collective-permute-start | bytes 5898248 | tf_op jit(solution)/shard_map/ppermute | solution.py:522
  55.6 0.7 copy-start.4
  56.3 1.7 %collective-permute-start.3 = (bf16[640,192]{1,0:T(8,128)(2,1)S(1)}, bf16[640,192]{1,0:T(8,128)(2,1)S(1)}, u32[]{:S(2)}, u32[]{:S(2)}) collective-permute-start(bf16[640,192]{1,0:T(8,128)(2,1)S(1)} %get-tuple-element.64), channel_id=1, source_target_pairs={{0,1},{1,0},{2,3},{3,2},{4,5},{5,4},{6,7},{7,6},{8,9},{9,8},{10,11... | collective-permute-start | bytes 737288 | tf_op jit(solution)/shard_map/ppermute | solution.py:522
  58.1 0.7 copy-start.6
  58.8 14.8 %collective-permute-start.8 = (bf16[4,192,896]{2,1,0:T(8,128)(2,1)}, bf16[4,192,896]{2,1,0:T(8,128)(2,1)}, u32[]{:S(2)}, u32[]{:S(2)}) collective-permute-start(bf16[4,192,896]{2,1,0:T(8,128)(2,1)} %all-to-all-done.1.og.refs_3_), channel_id=1, source_target_pairs={{0,1},{1,0},{2,3},{3,2},{4,5},{5,4},{6,7},{7,6},{8,9},{9,8},{10,11... | collective-permute-start | bytes 4128776 | tf_op jit(solution)/shard_map/ppermute | solution.py:522
  69.8 3.8 %collective-permute-start.9 = (bf16[896,192]{1,0:T(8,128)(2,1)}, bf16[896,192]{1,0:T(8,128)(2,1)}, u32[]{:S(2)}, u32[]{:S(2)}) collective-permute-start(bf16[896,192]{1,0:T(8,128)(2,1)} %get-tuple-element.80), channel_id=1, source_target_pairs={{0,1},{1,0},{2,3},{3,2},{4,5},{5,4},{6,7},{7,6},{8,9},{9,8},{10,11... | collective-permute-start | bytes 1032200 | tf_op jit(solution)/shard_map/ppermute | solution.py:522
  70.0 31.7 %all-to-all-start.2 = ((bf16[4,48,5120]{2,1,0:T(8,128)(2,1)}), bf16[4,48,5120]{2,1,0:T(8,128)(2,1)S(1)}, u32[]{:S(2)}, u32[]{:S(2)}) async-start(bf16[4,48,5120]{2,1,0:T(8,128)(2,1)} %bitcast.24), calls=%async_computation.2 | async-start | bytes 3932160 | tf_op jit(solution)/shard_map/all_to_all | solution.py:533
  79.8 18.4 %collective-permute-start.10 = (bf16[112,2176]{1,0:T(8,128)(2,1)}, bf16[112,2176]{1,0:T(8,128)(2,1)}, u32[]{:S(2)}, u32[]{:S(2)}) collective-permute-start(bf16[112,2176]{1,0:T(8,128)(2,1)} %get-tuple-element.81), channel_id=1, source_target_pairs={{0,8},{8,16},{16,24},{24,0},{32,40},{40,48},{48,56},{56,32},{64,72... | collective-permute-start | bytes 1462280 | tf_op jit(solution)/shard_map/ppermute | solution.py:593
  82.0 16.1 %collective-permute-start.11 = (bf16[112,2176]{1,0:T(8,128)(2,1)}, bf16[112,2176]{1,0:T(8,128)(2,1)}, u32[]{:S(2)}, u32[]{:S(2)}) collective-permute-start(bf16[112,2176]{1,0:T(8,128)(2,1)} %get-tuple-element.87), channel_id=1, source_target_pairs={{0,24},{8,0},{16,8},{24,16},{32,56},{40,32},{48,40},{56,48},{64,88... | collective-permute-start | bytes 1462280 | tf_op jit(solution)/shard_map/ppermute | solution.py:594
  83.3 14.7 %collective-permute-start.12 = (bf16[112,2176]{1,0:T(8,128)(2,1)}, bf16[112,2176]{1,0:T(8,128)(2,1)}, u32[]{:S(2)}, u32[]{:S(2)}) collective-permute-start(bf16[112,2176]{1,0:T(8,128)(2,1)} %get-tuple-element.88), channel_id=1, source_target_pairs={{0,32},{8,40},{16,48},{24,56},{32,64},{40,72},{48,80},{56,88},{64,... | collective-permute-start | bytes 1462280 | tf_op jit(solution)/shard_map/ppermute | solution.py:595
  85.3 12.9 %collective-permute-start.13 = (bf16[112,2176]{1,0:T(8,128)(2,1)}, bf16[112,2176]{1,0:T(8,128)(2,1)}, u32[]{:S(2)}, u32[]{:S(2)}) collective-permute-start(bf16[112,2176]{1,0:T(8,128)(2,1)} %get-tuple-element.89), channel_id=1, source_target_pairs={{0,96},{8,104},{16,112},{24,120},{32,0},{40,8},{48,16},{56,24},{64... | collective-permute-start | bytes 1462280 | tf_op jit(solution)/shard_map/ppermute | solution.py:596
  98.2 6.7 %copy-start.8 = (f32[1,1280]{1,0:T(1,128)S(1)}, f32[1,1280]{1,0:T(1,128)}, u32[]{:S(2)}) copy-start(f32[1,1280]{1,0:T(1,128)} %reshape.232.gain) | copy-start | bytes 15364
  101.7 24.4 %collective-permute-start.15 = (bf16[224,2176]{1,0:T(8,128)(2,1)}, bf16[224,2176]{1,0:T(8,128)(2,1)}, u32[]{:S(2)}, u32[]{:S(2)}) collective-permute-start(bf16[224,2176]{1,0:T(8,128)(2,1)} %get-tuple-element.98), channel_id=1, source_target_pairs={{0,32},{8,40},{16,48},{24,56},{32,64},{40,72},{48,80},{56,88},{64,... | collective-permute-start | bytes 2924552 | tf_op jit(solution)/shard_map/ppermute | solution.py:612
  103.2 23.0 %collective-permute-start.16 = (bf16[224,2176]{1,0:T(8,128)(2,1)}, bf16[224,2176]{1,0:T(8,128)(2,1)}, u32[]{:S(2)}, u32[]{:S(2)}) collective-permute-start(bf16[224,2176]{1,0:T(8,128)(2,1)} %get-tuple-element.99), channel_id=1, source_target_pairs={{0,96},{8,104},{16,112},{24,120},{32,0},{40,8},{48,16},{56,24},{64... | collective-permute-start | bytes 2924552 | tf_op jit(solution)/shard_map/ppermute | solution.py:612
  104.9 1.2 copy-start.9
  106.1 0.9 copy-start.10
  107.0 4.8 %copy-start.5 = (bf16[640,192]{1,0:T(8,128)(2,1)S(1)}, bf16[640,192]{1,0:T(8,128)(2,1)}, u32[]{:S(2)}) copy-start(bf16[640,192]{1,0:T(8,128)(2,1)} %copy-done.4) | copy-start | bytes 737284
  107.0 4.8 %copy-start.7 = (bf16[640,192]{1,0:T(8,128)(2,1)S(1)}, bf16[640,192]{1,0:T(8,128)(2,1)}, u32[]{:S(2)}) copy-start(bf16[640,192]{1,0:T(8,128)(2,1)} %copy-done.6) | copy-start | bytes 737284
  108.6 3.2 %collective-permute-start.14 = (bf16[192,1280]{1,0:T(8,128)(2,1)}, bf16[192,1280]{1,0:T(8,128)(2,1)S(1)}, u32[]{:S(2)}, u32[]{:S(2)}) collective-permute-start(bf16[192,1280]{1,0:T(8,128)(2,1)} %shard_map.156.grad), channel_id=1, source_target_pairs={{0,1},{1,0},{2,3},{3,2},{4,5},{5,4},{6,7},{7,6},{8,9},{9,8},{10,11... | collective-permute-start | bytes 1474568 | tf_op jit(solution)/shard_map/ppermute | solution.py:522
  108.6 25.9 %collective-permute-start.17 = (bf16[224,2176]{1,0:T(8,128)(2,1)}, bf16[224,2176]{1,0:T(8,128)(2,1)}, u32[]{:S(2)}, u32[]{:S(2)}) collective-permute-start(bf16[224,2176]{1,0:T(8,128)(2,1)} %get-tuple-element.90), channel_id=1, source_target_pairs={{0,8},{8,16},{16,24},{24,0},{32,40},{40,48},{48,56},{56,32},{64,72... | collective-permute-start | bytes 2924552 | tf_op jit(solution)/shard_map/ppermute | solution.py:614
  109.3 24.8 %collective-permute-start.18 = (bf16[224,2176]{1,0:T(8,128)(2,1)}, bf16[224,2176]{1,0:T(8,128)(2,1)}, u32[]{:S(2)}, u32[]{:S(2)}) collective-permute-start(bf16[224,2176]{1,0:T(8,128)(2,1)} %get-tuple-element.103), channel_id=1, source_target_pairs={{0,24},{8,0},{16,8},{24,16},{32,56},{40,32},{48,40},{56,48},{64,88... | collective-permute-start | bytes 2924552 | tf_op jit(solution)/shard_map/ppermute | solution.py:614
  111.8 1.0 copy-start.1
  114.6 1.2 copy-start
  115.9 4.8 %copy-start.2 = (bf16[192,1280]{1,0:T(8,128)(2,1)S(1)}, bf16[192,1280]{1,0:T(8,128)(2,1)}, u32[]{:S(2)}) copy-start(bf16[192,1280]{1,0:T(8,128)(2,1)} %shard_map.156.grad) | copy-start | bytes 1474564
  115.9 31.8 %all-to-all-start.3 = ((bf16[4,160,1280]{2,1,0:T(8,128)(2,1)}), bf16[4,160,1280]{2,1,0:T(8,128)(2,1)S(1)}, u32[]{:S(2)}, u32[]{:S(2)}) async-start(bf16[4,160,1280]{2,1,0:T(8,128)(2,1)} %bitcast.17), calls=%async_computation.3 | async-start | bytes 3276800 | tf_op jit(solution)/shard_map/all_to_all | solution.py:533
  129.5 11.5 %collective-permute-start.22 = (bf16[224,544]{1,0:T(8,128)(2,1)}, bf16[224,544]{1,0:T(8,128)(2,1)S(1)}, u32[]{:S(2)}, u32[]{:S(2)}) collective-permute-start(bf16[224,544]{1,0:T(8,128)(2,1)} %get-tuple-element.108), channel_id=1, source_target_pairs={{0,8},{8,16},{16,24},{24,0},{32,40},{40,48},{48,56},{56,32},{64,72... | collective-permute-start | bytes 731144 | tf_op jit(solution)/shard_map/ppermute | solution.py:476
  130.0 22.4 %collective-permute-start.23 = (bf16[224,544]{1,0:T(8,128)(2,1)}, bf16[224,544]{1,0:T(8,128)(2,1)}, u32[]{:S(2)}, u32[]{:S(2)}) collective-permute-start(bf16[224,544]{1,0:T(8,128)(2,1)} %get-tuple-element.109), channel_id=1, source_target_pairs={{0,24},{8,0},{16,8},{24,16},{32,56},{40,32},{48,40},{56,48},{64,88... | collective-permute-start | bytes 731144 | tf_op jit(solution)/shard_map/ppermute | solution.py:477
  132.7 19.7 %collective-permute-start.24 = (bf16[224,544]{1,0:T(8,128)(2,1)}, bf16[224,544]{1,0:T(8,128)(2,1)}, u32[]{:S(2)}, u32[]{:S(2)}) collective-permute-start(bf16[224,544]{1,0:T(8,128)(2,1)} %get-tuple-element.110), channel_id=1, source_target_pairs={{0,16},{8,24},{16,0},{24,8},{32,48},{40,56},{48,32},{56,40},{64,80... | collective-permute-start | bytes 731144 | tf_op jit(solution)/shard_map/ppermute | solution.py:475
  137.8 14.6 %collective-permute-start.19 = (bf16[224,544]{1,0:T(8,128)(2,1)}, bf16[224,544]{1,0:T(8,128)(2,1)}, u32[]{:S(2)}, u32[]{:S(2)}) collective-permute-start(bf16[224,544]{1,0:T(8,128)(2,1)} %get-tuple-element.105), channel_id=1, source_target_pairs={{0,32},{8,40},{16,48},{24,56},{32,64},{40,72},{48,80},{56,88},{64,... | collective-permute-start | bytes 731144 | tf_op jit(solution)/shard_map/ppermute | solution.py:476
  138.1 18.7 %collective-permute-start.20 = (bf16[224,544]{1,0:T(8,128)(2,1)}, bf16[224,544]{1,0:T(8,128)(2,1)}, u32[]{:S(2)}, u32[]{:S(2)}) collective-permute-start(bf16[224,544]{1,0:T(8,128)(2,1)} %get-tuple-element.106), channel_id=1, source_target_pairs={{0,96},{8,104},{16,112},{24,120},{32,0},{40,8},{48,16},{56,24},{64... | collective-permute-start | bytes 731144 | tf_op jit(solution)/shard_map/ppermute | solution.py:477
  141.1 15.8 %copy-start.17 = (bf16[224,544]{1,0:T(8,128)(2,1)}, bf16[224,544]{1,0:T(8,128)(2,1)S(1)}, u32[]{:S(2)}) copy-start(bf16[224,544]{1,0:T(8,128)(2,1)S(1)} %collective-permute-done.22.b1) | copy-start | bytes 731140
  141.1 15.8 %collective-permute-start.21 = (bf16[224,544]{1,0:T(8,128)(2,1)}, bf16[224,544]{1,0:T(8,128)(2,1)}, u32[]{:S(2)}, u32[]{:S(2)}) collective-permute-start(bf16[224,544]{1,0:T(8,128)(2,1)} %get-tuple-element.107), channel_id=1, source_target_pairs={{0,64},{8,72},{16,80},{24,88},{32,96},{40,104},{48,112},{56,120},{... | collective-permute-start | bytes 731144 | tf_op jit(solution)/shard_map/ppermute | solution.py:475
  148.8 14.4 %all-to-all-start.4 = ((bf16[16,16,1280]{2,1,0:T(8,128)(2,1)}), bf16[16,16,1280]{2,1,0:T(8,128)(2,1)S(1)}, u32[]{:S(2)}, u32[]{:S(2)}) async-start(bf16[16,16,1280]{2,1,0:T(8,128)(2,1)} %shard_map.159), calls=%async_computation.4 | async-start | bytes 1310720 | tf_op jit(solution)/shard_map/all_to_all | solution.py:618
